TPU v7x, 32 devices: a whole 2x2x4 slice. The times are simulated.
32 devices in a mesh: doc: 4 (over y, x), ctx: 2 (over core), head: 4 (over z).
Axes of the slice: x: 2, y: 2, z: 4, core: 2. Of those that a mesh axis runs over, the one named last changes fastest.
Arguments:
- queries: bfloat16 [128, 16384], P(('doc', 'ctx'), 'head'), as said below
- doc_of: int32 [128, 1], P(('doc', 'ctx')), may hold values from 0 to 3; in each aligned block of 16 rows (0 to 15, 16 to 31, ...) at most 6 rows name the same one
- doc_lengths: int32 [4], replicated, may hold values from 512 to 2048, as said below
- rotated_key_levels: bfloat16 [4, 2048, 1024], P('doc', 'ctx', 'head'), may hold values from -8 to 7
- rotated_value_levels: bfloat16 [4, 2048, 1024], P('doc', 'ctx', 'head'), may hold values from -8 to 7
- key_level_scale: bfloat16 [4, 8, 2048], P('doc', 'head', 'ctx'), may hold values from 0.19921875 to 0.796875
- value_level_scale: bfloat16 [4, 8, 2048], P('doc', 'head', 'ctx'), may hold values from 0.099609375 to 0.3984375
Outputs:
- attended: bfloat16 [128, 16384], P(('doc', 'ctx'))
Inputs may be any that keep to these rules, and one draw needn't show every extreme that they name: `queries`: query rows. `doc_of`: in the rows of one device no document is named by more than 6 requests, a bound that some block reaches. `doc_lengths`: some document is valid over all its positions.
All inputs are finite; a program needn't handle non-finite values.
Results may differ from a plain program's by a relative error of at most 0.02.
Values may be sent and summed in bfloat16 or wider, within the bound.
No kernel may reach another device: no remote copies, remote signals or barrier semaphores. Data moves between devices by JAX's collectives and lax.ppermute only.
A program may use at most 128 MiB of HBM per device.

v0:
```python
import math

import jax
import jax.numpy as jnp
from jax import lax
from jax.sharding import PartitionSpec as P

HEAD_WIDTH = 128


def shifted(value, axis, steps):
    count = lax.axis_size(axis)
    pairs = [(source, (source + steps) % count) for source in range(count)]
    return lax.ppermute(value, axis, pairs)


def hadamard_signs():
    idx = jnp.arange(HEAD_WIDTH, dtype=jnp.int32)
    both = jnp.bitwise_and(idx[:, None], idx[None, :])
    parity = jnp.zeros_like(both)
    for bit in range(HEAD_WIDTH.bit_length()):
        parity = parity + jnp.bitwise_and(jnp.right_shift(both, bit), 1)
    return (1 - 2 * (parity % 2)).astype(jnp.float32)


def update_state(
    softmax_state,
    query_rows,
    key_block,
    value_block,
    key_block_scale,
    value_block_scale,
    valid_mask,
):
    inverse_total = 1.0 / math.sqrt(HEAD_WIDTH)
    current_maximum, current_denominator, current_weighted_sum = softmax_state
    score_block = jnp.einsum(
        "bkgd,skd->bkgs", query_rows, key_block, preferred_element_type=jnp.float32
    )
    score_block = (
        score_block * (key_block_scale.astype(jnp.float32) * inverse_total)[None, :, None, :]
    )
    score_block = jnp.where(valid_mask[None, None, None, :], score_block, jnp.float32(-1e30))
    new_max = jnp.maximum(current_maximum, jnp.max(score_block, axis=-1))
    probs = jnp.where(
        valid_mask[None, None, None, :], jnp.exp(score_block - new_max[..., None]), jnp.float32(0.0)
    )
    factor = jnp.exp(current_maximum - new_max)
    new_total = current_denominator * factor + jnp.sum(probs, axis=-1)
    weights = (probs * value_block_scale.astype(jnp.float32)[None, :, None, :]).astype(jnp.bfloat16)
    new_sum = current_weighted_sum * factor[..., None] + jnp.einsum(
        "bkgs,skd->bkgd", weights, value_block, preferred_element_type=jnp.float32
    )
    return (new_max, new_total, new_sum)


def absorb_block(
    softmax_state,
    query_rows,
    key_block,
    value_block,
    key_block_scale,
    value_block_scale,
    valid_mask,
):
    return update_state(
        softmax_state,
        query_rows,
        key_block,
        value_block,
        key_block_scale,
        value_block_scale,
        valid_mask,
    )


def shards(
    queries,
    doc_of,
    doc_lengths,
    rotated_key_levels,
    rotated_value_levels,
    key_level_scale,
    value_level_scale,
):
    inverse_total = 1.0 / math.sqrt(HEAD_WIDTH)
    signs = hadamard_signs()
    rows_home, width = queries.shape
    heads_dev = width // HEAD_WIDTH
    kv_dev = key_level_scale.shape[1]
    head_group = heads_dev // kv_dev
    shard_len = rotated_key_levels.shape[1]
    n_doc = lax.axis_size("doc")
    n_ctx = lax.axis_size("ctx")
    cap = max(2, 3 * rows_home // (2 * n_doc))
    rotated_rows = jnp.einsum(
        "rhd,de->rhe",
        queries.reshape(rows_home, heads_dev, HEAD_WIDTH),
        signs.astype(jnp.bfloat16),
        preferred_element_type=jnp.float32,
    )
    rotated_rows = (rotated_rows * inverse_total).astype(jnp.bfloat16).reshape(rows_home, width)
    target = doc_of[:, 0]
    onehot = (target[:, None] == jnp.arange(n_doc, dtype=jnp.int32)[None, :]).astype(jnp.int32)
    earlier = jnp.cumsum(onehot, axis=0) - onehot
    rank = jnp.sum(earlier * onehot, axis=1)
    slot = target * cap + rank
    placing = (jnp.arange(n_doc * cap, dtype=jnp.int32)[:, None] == slot[None, :]).astype(
        jnp.bfloat16
    )
    outgoing = (
        jnp.dot(placing, rotated_rows, preferred_element_type=jnp.float32)
        .astype(jnp.bfloat16)
        .reshape(n_doc, cap, width)
    )
    my_doc = lax.axis_index("doc")
    my_ctx = lax.axis_index("ctx")
    length = lax.dynamic_slice_in_dim(doc_lengths, my_doc, 1)[0]
    key_block = rotated_key_levels[0].reshape(shard_len, kv_dev, HEAD_WIDTH)
    value_block = rotated_value_levels[0].reshape(shard_len, kv_dev, HEAD_WIDTH)
    key_block_scale = key_level_scale[0]
    value_block_scale = value_level_scale[0]
    positions = jnp.arange(shard_len, dtype=jnp.int32)
    block = lax.all_to_all(outgoing, "doc", split_axis=0, concat_axis=0, tiled=True)
    count = block.shape[0] * block.shape[1]
    query_rows = block.reshape(count, kv_dev, head_group, HEAD_WIDTH)
    start_max = jnp.full((count, kv_dev, head_group), -1e30, jnp.float32)
    start_total = jnp.zeros((count, kv_dev, head_group), jnp.float32)
    start_sum = jnp.zeros((count, kv_dev, head_group, HEAD_WIDTH), jnp.float32)

    def visit(step, carry):
        softmax_state, cache = carry
        anchor = (my_ctx - step) % n_ctx
        valid_mask = anchor * shard_len + positions < length
        softmax_state = absorb_block(
            softmax_state, query_rows, cache[0], cache[1], cache[2], cache[3], valid_mask
        )
        cache = shifted((cache[0], cache[1], cache[2], cache[3]), "ctx", 1)
        return (softmax_state, cache)

    softmax_state, cache = lax.fori_loop(
        0,
        n_ctx - 1,
        visit,
        (
            (start_max, start_total, start_sum),
            (key_block, value_block, key_block_scale, value_block_scale),
        ),
    )
    anchor = (my_ctx - (n_ctx - 1)) % n_ctx
    valid_mask = anchor * shard_len + positions < length
    current_maximum, current_denominator, current_weighted_sum = absorb_block(
        softmax_state, query_rows, cache[0], cache[1], cache[2], cache[3], valid_mask
    )
    mixed = current_weighted_sum / current_denominator[..., None]
    result = (
        jnp.einsum("bkgd,de->bkge", mixed, signs, precision=lax.Precision.HIGHEST) * inverse_total
    )
    finished = result.astype(jnp.bfloat16).reshape(block.shape)
    returned = lax.all_to_all(finished, "doc", split_axis=0, concat_axis=0, tiled=True).reshape(
        n_doc * cap, width
    )
    mine = jnp.einsum("sr,sc->rc", placing, returned, preferred_element_type=jnp.float32).astype(
        jnp.bfloat16
    )
    return lax.all_gather(mine, "head", axis=1, tiled=True)


def solution(mesh):
    in_specs = (
        P(("doc", "ctx"), "head"),
        P(("doc", "ctx"), None),
        P(),
        P("doc", "ctx", "head"),
        P("doc", "ctx", "head"),
        P("doc", "head", "ctx"),
        P("doc", "head", "ctx"),
    )
    out_specs = P(("doc", "ctx"), None)
    return jax.shard_map(shards, mesh=mesh, in_specs=in_specs, out_specs=out_specs, check_vma=False)
```

profile of v0, /device:TPU:0, one launch (start us, length us, event | category | flops | bytes accessed | tf_op | source)
XLA Modules:
  0.0 48.2 jit_solution(5243093201566027695)
XLA Ops:
  0.0 0.8 %fusion.48 = s32[16,4]{1,0:T(8,128)S(1)} fusion(s32[16]{0:T(128)} %bitcast.82), kind=kLoop, calls=%fused_computation.58 | loop fusion | flops 128 | bytes 320 | tf_op jit(solution)/shard_map/convert_element_type | solution.py:104
  0.8 0.8 %select_reduce_fusion = s32[16]{0:T(128)S(1)} fusion(s32[16,4]{1,0:T(8,128)S(1)} %reduce_window_sum.11, s32[16]{0:T(128)} %bitcast.83), kind=kLoop, calls=%fused_computation.56 | loop fusion | flops 304 | bytes 384 | tf_op jit(solution)/shard_map/reduce_sum | solution.py:106
  1.7 0.7 %multiply_add_fusion.1 = s32[16]{0:T(128)S(1)} fusion(s32[16]{0:T(128)S(1)} %select_reduce_fusion, s32[16,1]{0,1:T(1,128)} %param.8), kind=kLoop, calls=%fused_computation.63 | loop fusion | flops 32 | bytes 192 | tf_op jit(solution)/shard_map/add | solution.py:107
  2.3 0.9 %copy.28 = bf16[2,8,32,128]{3,2,1,0:T(8,128)(2,1)S(1)} copy(bf16[2,8,32,128]{3,1,2,0:T(8,128)(2,1)} %bitcast.78) | data formatting | bytes 262144
  3.7 0.8 %reshape.81 = bf16[4,6,4096]{2,1,0:T(8,128)(2,1)} reshape(bf16[24,4096]{1,0:T(8,128)(2,1)S(1)} %convolution_convert_fusion) | data formatting | bytes 393216 | tf_op jit(solution)/shard_map/reshape | solution.py:114
  4.5 5.2 %all-to-all-start = ((bf16[4,6,4096]{2,1,0:T(8,128)(2,1)}), bf16[4,6,4096]{2,1,0:T(8,128)(2,1)S(1)}, u32[]{:S(2)}, u32[]{:S(2)}) async-start(bf16[4,6,4096]{2,1,0:T(8,128)(2,1)} %reshape.81), calls=%async_computation | async-start | bytes 524288 | tf_op jit(solution)/shard_map/all_to_all | solution.py:124
  9.7 1.2 %copy.11 = bf16[1,1024,256]{1,2,0:T(8,128)(2,1)S(1)} copy(bf16[1,1024,256]{2,1,0:T(8,128)(2,1)} %param.10) | data formatting | bytes 1048576 | tf_op args[3]
  10.9 0.3 copy.15
  11.3 0.5 %collective-permute-start.1 = (bf16[2,1024]{1,0:T(2,128)(2,1)S(1)}, bf16[2,1024]{1,0:T(2,128)(2,1)S(1)}, u32[]{:S(2)}, u32[]{:S(2)}) collective-permute-start(bf16[2,1024]{1,0:T(2,128)(2,1)S(1)} %bitcast.81), channel_id=1, source_target_pairs={{0,4},{4,0},{1,5},{5,1},{2,6},{6,2},{3,7},{7,3},{8,12},{12,8},{9,1... | collective-permute-start | bytes 12296 | tf_op jit(solution)/shard_map/while/body/eval_jaxpr/ppermute | solution.py:14
  12.0 0.5 %collective-permute-start.3 = (bf16[1024,2,128]{2,1,0:T(2,128)(2,1)S(1)}, bf16[1024,2,128]{2,1,0:T(2,128)(2,1)}, u32[]{:S(2)}, u32[]{:S(2)}) collective-permute-start(bf16[1024,2,128]{2,1,0:T(2,128)(2,1)S(1)} %reshape_squeeze.7), channel_id=1, source_target_pairs={{0,4},{4,0},{1,5},{5,1},{2,6},{6,2},{3,7},{7,3},{8,12},{12,8},{9,1... | collective-permute-start | bytes 1572872 | tf_op jit(solution)/shard_map/while/body/eval_jaxpr/ppermute | solution.py:14
  12.5 0.7 %dynamic_slice.3 = s32[1]{0:T(128)} dynamic-slice(s32[4]{0:T(128)S(1)} %copy-done.3, s32[]{:T(128)S(6)} %select_n.46), dynamic_slice_sizes={1} | dynamic-slice | bytes 12 | tf_op jit(solution)/shard_map/dynamic_slice | solution.py:118
  13.2 0.7 %add_compare_fusion = pred[1024]{0:T(1024)(128)(4,1)S(1)} fusion(s32[]{:T(128)S(6)} %mul.135, s32[]{:T(128)} %bitcast.1), kind=kLoop, calls=%fused_computation.61 | loop fusion | flops 2048 | bytes 1032 | tf_op jit(solution)/shard_map/lt | solution.py:151
  13.9 0.7 %add_compare_fusion.1 = pred[1024]{0:T(1024)(128)(4,1)S(1)} fusion(s32[]{:T(128)} %bitcast.1, s32[]{:T(128)S(6)} %mul.124), kind=kLoop, calls=%fused_computation.62 | loop fusion | flops 2048 | bytes 1032 | tf_op jit(solution)/shard_map/while/body/eval_jaxpr/lt | solution.py:134
  14.8 0.3 all-to-all-done
  15.3 0.6 %bitcast_reduce_fusion.1 = (f32[24,2,16]{2,0,1:T(8,128)S(1)}, f32[2,24,16,1024]{3,2,1,0:T(8,128)S(1)}) fusion(f32[2,1024]{1,0:T(2,128)S(1)} %convert_multiply_fusion.1, pred[1024]{0:T(1024)(128)(4,1)S(1)} %add_compare_fusion.1, bf16[1024,2,128,1]{0,2,3,1:T(8,128)(2,1)S(1)} %bitcast.76, bf16[24,2,16,128]{3,2,1,0:T(8,128)(2,1)S(1)} %reshape.82), kind=kOutput, calls=%fused_computation.7 | convolution fusion | flops 203685120 | bytes 3878912 | tf_op jit(solution)/shard_map/while/body/eval_jaxpr/bkgd,skd->bkgs/dot_general | solution.py:37
  16.0 0.6 %bitcast_reduce_fusion = (f32[24,2,16]{2,0,1:T(8,128)S(1)}, f32[2,24,16,1024]{3,2,1,0:T(8,128)S(1)}) fusion(f32[2,1024]{1,0:T(2,128)S(1)} %convert_multiply_fusion, pred[1024]{0:T(1024)(128)(4,1)S(1)} %add_compare_fusion, bf16[1024,2,128]{2,0,1:T(8,128)(2,1)S(1)} %collective-permute-done, bf16[24,2,16,128]{3,2,1,0:T(8,128)(2,1)S(1)} %reshape.82), kind=kOutput, calls=%fused_computation.3 | convolution fusion | flops 203685120 | bytes 3878912 | tf_op jit(solution)/shard_map/bkgd,skd->bkgs/dot_general | solution.py:37
  16.6 1.0 %multiply_convert_fusion = (bf16[24,2,16,1024]{3,2,0,1:T(8,128)(2,1)S(1)}, f32[24,2,16]{2,0,1:T(8,128)S(1)}) fusion(f32[2,24,16,1024]{3,2,1,0:T(8,128)S(1)} %get-tuple-element.56, f32[2,1024]{1,0:T(2,128)S(1)} %convert_element_type.66, f32[24,2,16]{2,0,1:T(8,128)S(1)} %get-tuple-element.36, f32[2,1024]{1,0:T(2,128)S(1)} %convert_multiply_fusion, ...), kind=kLoop, calls=%fused_computation.10 | loop fusion | flops 5504256 | bytes 4742144 | tf_op jit(solution)/shard_map/convert_element_type | solution.py:50
  17.7 1.1 %fusion.4 = (f32[24,2,16]{2,0,1:T(8,128)S(1)}, bf16[24,2,16,1024]{3,2,0,1:T(8,128)(2,1)S(1)}) fusion(f32[2,24,16,1024]{3,2,1,0:T(8,128)S(1)} %get-tuple-element.52, f32[24,2,16]{2,0,1:T(8,128)S(1)} %get-tuple-element.37, f32[2,1024]{1,0:T(2,128)S(1)} %convert_multiply_fusion.1, pred[1024]{0:T(1024)(128)(4,1)S(1)} %add_compare_fusion.1, ...), kind=kLoop, calls=%fused_computation.14 | loop fusion | flops 5504256 | bytes 4742144 | tf_op jit(solution)/shard_map/while/body/eval_jaxpr/reduce_sum | solution.py:49
  18.8 0.6 %fusion.22 = f32[24,2,16,128]{3,2,1,0:T(8,128)S(1)} fusion(bf16[24,2,16,1024]{3,2,0,1:T(8,128)(2,1)S(1)} %get-tuple-element.34, bf16[1024,2,128,1]{2,1,0,3:T(2,128)(2,1)S(1)} %reshape.87, f32[24,2,16]{2,1,0:T(2,128)S(1)} %copy.17, f32[24,2,16]{2,1,0:T(2,128)S(1)} %copy.14), kind=kOutput, calls=%fused_computation.25 | convolution fusion | flops 201523200 | bytes 2496512 | tf_op jit(solution)/shard_map/while/body/eval_jaxpr/bkgs,skd->bkgd/dot_general | solution.py:51
  19.5 1.7 %fusion.25 = f32[24,2,16,128]{3,2,1,0:T(8,128)S(1)} fusion(f32[24,2,16,128]{3,2,1,0:T(8,128)S(1)} %fusion.22, bf16[24,2,16,1024]{3,2,0,1:T(8,128)(2,1)S(1)} %get-tuple-element.31, bf16[1024,2,128,1]{2,1,0,3:T(2,128)(2,1)} %bitcast.13, f32[24,2,16]{2,1,0:T(2,128)S(1)} %copy.18), kind=kOutput, calls=%fused_computation.26 | convolution fusion | flops 201523200 | bytes 2886656 | tf_op jit(solution)/shard_map/bkgs,skd->bkgd/dot_general | solution.py:51
  21.1 0.5 %fusion.28 = bf16[24,2,16,128]{3,2,1,0:T(8,128)(2,1)S(1)} fusion(f32[24,2,16,128]{3,2,1,0:T(8,128)S(1)} %fusion.25), kind=kOutput, calls=%fused_computation.27 | convolution fusion | flops 151814144 | bytes 589824 | tf_op jit(solution)/shard_map/bkgd,de->bkge/dot_general | solution.py:157
  21.9 9.7 %all_to_all.10 = bf16[4,6,4096]{2,1,0:T(8,128)(2,1)S(1)} all-to-all(bf16[4,6,4096]{2,1,0:T(8,128)(2,1)S(1)} %reshape.83), channel_id=1, replica_groups=mesh['doc'=4,'ctx'=2,'head'=4] {'doc'}, dimensions={0} | all-to-all | bytes 393216 | tf_op jit(solution)/shard_map/all_to_all | solution.py:160
  31.9 15.4 %all_gather.3 = bf16[16,16384]{1,0:T(8,128)(2,1)S(1)} all-gather(bf16[16,4096]{1,0:T(8,128)(2,1)S(1)} %convolution_convert_fusion.1), channel_id=1, replica_groups=mesh['doc'=4,'ctx'=2,'head'=4] {'head'}, dimensions={1}, use_global_device_ids=true | all-gather | bytes 655360 | tf_op jit(solution)/shard_map/all_gather | solution.py:166
  47.4 0.8 %copy.63 = bf16[16,16384]{1,0:T(8,128)(2,1)} copy(bf16[16,16384]{1,0:T(8,128)(2,1)S(1)} %all_gather.3) | data formatting | bytes 1048576
  (32 shorter events, 1.8 us)
Async XLA Ops:
  0.0 11.3 %copy-start.2 = (bf16[1,2,1024]{2,1,0:T(2,128)(2,1)S(1)}, bf16[1,2,1024]{2,1,0:T(2,128)(2,1)}, u32[]{:S(2)}) copy-start(bf16[1,2,1024]{2,1,0:T(2,128)(2,1)} %param.12) | copy-start | bytes 12292
  0.0 11.8 %copy-start.1 = (bf16[1,2,1024]{2,1,0:T(2,128)(2,1)S(1)}, bf16[1,2,1024]{2,1,0:T(2,128)(2,1)}, u32[]{:S(2)}) copy-start(bf16[1,2,1024]{2,1,0:T(2,128)(2,1)} %param.13) | copy-start | bytes 12292
  0.0 11.9 %copy-start = (bf16[1,1024,256]{2,1,0:T(8,128)(2,1)S(1)}, bf16[1,1024,256]{2,1,0:T(8,128)(2,1)}, u32[]{:S(2)}) copy-start(bf16[1,1024,256]{2,1,0:T(8,128)(2,1)} %param.11) | copy-start | bytes 1572868
  0.0 12.5 %copy-start.3 = (s32[4]{0:T(128)S(1)}, s32[4]{0:T(128)}, u32[]{:S(2)}) copy-start(s32[4]{0:T(128)} %param.9) | copy-start | bytes 52
  4.5 10.5 %all-to-all-start = ((bf16[4,6,4096]{2,1,0:T(8,128)(2,1)}), bf16[4,6,4096]{2,1,0:T(8,128)(2,1)S(1)}, u32[]{:S(2)}, u32[]{:S(2)}) async-start(bf16[4,6,4096]{2,1,0:T(8,128)(2,1)} %reshape.81), calls=%async_computation | async-start | bytes 524288 | tf_op jit(solution)/shard_map/all_to_all | solution.py:124
  11.2 4.8 %collective-permute-start = (bf16[1024,2,128]{2,0,1:T(8,128)(2,1)S(1)}, bf16[1024,2,128]{2,0,1:T(8,128)(2,1)S(1)}, u32[]{:S(2)}, u32[]{:S(2)}) collective-permute-start(bf16[1024,2,128]{2,0,1:T(8,128)(2,1)S(1)} %copy.15), channel_id=1, source_target_pairs={{0,4},{4,0},{1,5},{5,1},{2,6},{6,2},{3,7},{7,3},{8,12},{12,8},{9,1... | collective-permute-start | bytes 1572872 | tf_op jit(solution)/shard_map/while/body/eval_jaxpr/ppermute | solution.py:14
  11.3 3.5 %collective-permute-start.1 = (bf16[2,1024]{1,0:T(2,128)(2,1)S(1)}, bf16[2,1024]{1,0:T(2,128)(2,1)S(1)}, u32[]{:S(2)}, u32[]{:S(2)}) collective-permute-start(bf16[2,1024]{1,0:T(2,128)(2,1)S(1)} %bitcast.81), channel_id=1, source_target_pairs={{0,4},{4,0},{1,5},{5,1},{2,6},{6,2},{3,7},{7,3},{8,12},{12,8},{9,1... | collective-permute-start | bytes 12296 | tf_op jit(solution)/shard_map/while/body/eval_jaxpr/ppermute | solution.py:14
  11.8 3.0 %collective-permute-start.2 = (bf16[2,1024]{1,0:T(2,128)(2,1)S(1)}, bf16[2,1024]{1,0:T(2,128)(2,1)S(1)}, u32[]{:S(2)}, u32[]{:S(2)}) collective-permute-start(bf16[2,1024]{1,0:T(2,128)(2,1)S(1)} %bitcast.80), channel_id=1, source_target_pairs={{0,4},{4,0},{1,5},{5,1},{2,6},{6,2},{3,7},{7,3},{8,12},{12,8},{9,1... | collective-permute-start | bytes 12296 | tf_op jit(solution)/shard_map/while/body/eval_jaxpr/ppermute | solution.py:14
  12.0 7.5 %collective-permute-start.3 = (bf16[1024,2,128]{2,1,0:T(2,128)(2,1)S(1)}, bf16[1024,2,128]{2,1,0:T(2,128)(2,1)}, u32[]{:S(2)}, u32[]{:S(2)}) collective-permute-start(bf16[1024,2,128]{2,1,0:T(2,128)(2,1)S(1)} %reshape_squeeze.7), channel_id=1, source_target_pairs={{0,4},{4,0},{1,5},{5,1},{2,6},{6,2},{3,7},{7,3},{8,12},{12,8},{9,1... | collective-permute-start | bytes 1572872 | tf_op jit(solution)/shard_map/while/body/eval_jaxpr/ppermute | solution.py:14
where the time goes:
time: 48.6 us; the launch traced here: 48.2 us
  blocking collectives  25.1 us (52%)
  starting transfers between devices  6.31 us (13%)
  other arithmetic  5.88 us (12%)
  local copies, waits for them, and re-layouts  5.54 us (11%)
  matrix products  4.76 us (10%)
    all_gather x1, blocking collectives, shards(): return lax.all_gather(mine, 'head', axis=1, tiled=True)  15.4 us
    all_to_all x1, blocking collectives, shards(): lax.all_to_all(finished, 'doc', split_axis=0, concat_axis=0, tiled=True)  9.72 us
    all_to_all x1, starting transfers between devices, shards(): lax.all_to_all(outgoing, 'doc', split_axis=0, concat_axis=0, tiled=True)  5.18 us
    unnamed x11, local copies, waits for them, and re-layouts  2.98 us
    dot_general x2, matrix products, update_state(): jnp.einsum('bkgs,skd->bkgd', weights, value_block, preferred_element_type...  2.26 us
    dot_general x2, matrix products, update_state(): jnp.einsum('bkgd,skd->bkgs', query_rows, key_block, preferred_element_typ...  1.28 us
    ppermute x4, starting transfers between devices, shifted(): return lax.ppermute(value, axis, pairs)  1.14 us
    reduce_sum x1, other arithmetic, update_state(): new_total = current_denominator * factor + jnp.sum(probs, axis=-1)  1.05 us
  transfers between devices with their start and end apart: 5, of which 1 were waited for; matrix products, arithmetic and copies ran while one was open for 17% of the time, Pallas kernels for 0%

commit v1 on v0

v1 whole, which is shorter than its diff:
```python
import functools
import math

import jax
import jax.numpy as jnp
from jax import lax
from jax.experimental import pallas as pl
from jax.experimental.pallas import tpu as pltpu
from jax.sharding import PartitionSpec as P

HEAD_WIDTH = 128
LANES = 128
VMEM_BYTES = 40 * 1024 * 1024


def peer_of(index, step, count):
    if count & (count - 1) == 0:
        return index ^ step
    return (index + step) % count


def sent(value, axis, step):
    count = lax.axis_size(axis)
    return lax.ppermute(value, axis, [(i, peer_of(i, step, count)) for i in range(count)])


def returned(value, axis, step):
    count = lax.axis_size(axis)
    return lax.ppermute(value, axis, [(peer_of(i, step, count), i) for i in range(count)])


def sign_matrix():
    row = lax.broadcasted_iota(jnp.int32, (HEAD_WIDTH, HEAD_WIDTH), 0)
    column = lax.broadcasted_iota(jnp.int32, (HEAD_WIDTH, HEAD_WIDTH), 1)
    both = row & column
    both = both ^ (both >> 4)
    both = both ^ (both >> 2)
    both = both ^ (both >> 1)
    return (1 - 2 * (both & 1)).astype(jnp.float32).astype(jnp.bfloat16)


def placing_matrix(doc_column, n_doc, cap):
    rows = doc_column.shape[0]
    group = LANES // rows
    me = lax.axis_index("doc")
    request = lax.broadcasted_iota(jnp.int32, (rows, LANES), 0)
    lane = lax.broadcasted_iota(jnp.int32, (rows, LANES), 1)
    docs = jnp.broadcast_to(doc_column, (rows, LANES))
    lane_request = lane % rows
    lane_doc = jnp.sum(jnp.where(request == lane_request, docs, 0), axis=0, keepdims=True)
    rank = jnp.sum(
        jnp.where((docs == lane_doc) & (request < lane_request), 1, 0), axis=0, keepdims=True
    )
    if n_doc & (n_doc - 1) == 0:
        step = lane_doc ^ me
    else:
        step = (lane_doc - me + n_doc) % n_doc
    place = step * (group * cap) + (lane[:1] // rows) * cap + rank
    slots = n_doc * group * cap
    slot = lax.broadcasted_iota(jnp.int32, (slots, LANES), 0)
    return jnp.where(slot == place, 1.0, 0.0).astype(jnp.bfloat16)


def dispatch_kernel(n_doc, cap, doc_ref, query_ref, *out_refs):
    rows, width = query_ref.shape
    group = LANES // rows
    heads = width // HEAD_WIDTH
    block = group * cap
    placing = placing_matrix(doc_ref[...], n_doc, cap)
    signs = sign_matrix()
    scale = 1.0 / math.sqrt(HEAD_WIDTH)
    for g in range(heads // group):
        stacked = jnp.concatenate(
            [
                query_ref[:, (g * group + h) * HEAD_WIDTH : (g * group + h + 1) * HEAD_WIDTH]
                for h in range(group)
            ],
            axis=0,
        )
        placed = jnp.dot(placing, stacked, preferred_element_type=jnp.float32).astype(jnp.bfloat16)
        rotated = jnp.dot(placed, signs, preferred_element_type=jnp.float32) * scale
        rotated = rotated.astype(jnp.bfloat16)
        for k in range(n_doc):
            out_refs[k][g * block : (g + 1) * block, :] = rotated[k * block : (k + 1) * block]


def collect_kernel(n_doc, cap, doc_ref, *refs):
    back_refs, out_ref = refs[:n_doc], refs[n_doc]
    rows, width = out_ref.shape
    group = LANES // rows
    heads = width // HEAD_WIDTH
    block = group * cap
    placing = placing_matrix(doc_ref[...], n_doc, cap)
    for g in range(heads // group):
        slots = jnp.concatenate(
            [back_refs[k][g * block : (g + 1) * block, :] for k in range(n_doc)], axis=0
        )
        mine = lax.dot_general(
            placing, slots, (((0,), (0,)), ((), ())), preferred_element_type=jnp.float32
        ).astype(jnp.bfloat16)
        for h in range(group):
            at = (g * group + h) * HEAD_WIDTH
            out_ref[:, at : at + HEAD_WIDTH] = mine[h * rows : (h + 1) * rows]


def attend_kernel(n_doc, n_ctx, kv_dev, length_ref, *refs):
    query_refs, refs = refs[:n_doc], refs[n_doc:]
    cache_refs, out_refs = refs[: 4 * n_ctx], refs[4 * n_ctx :]
    my_ctx = lax.axis_index("ctx")
    length = length_ref[lax.axis_index("doc")]
    shard_len = cache_refs[0].shape[0]
    rows_doc = query_refs[0].shape[0] // kv_dev
    signs = sign_matrix()
    scale = 1.0 / math.sqrt(HEAD_WIDTH)
    position = lax.broadcasted_iota(jnp.int32, (1, shard_len), 1)
    for g in range(kv_dev):
        span = slice(g * rows_doc, (g + 1) * rows_doc)
        head = slice(g * HEAD_WIDTH, (g + 1) * HEAD_WIDTH)
        query_rows = jnp.concatenate([ref[span, :] for ref in query_refs], axis=0)
        state = None
        for first in range(0, n_ctx, 2):
            steps = range(first, min(first + 2, n_ctx))
            scores = []
            for step in steps:
                key_ref, key_scale_ref = cache_refs[4 * step], cache_refs[4 * step + 2]
                anchor = lax.rem(my_ctx - step + n_ctx, n_ctx) * shard_len
                key_scale = key_scale_ref[g : g + 1, :].astype(jnp.float32) * (
                    scale * math.log2(math.e)
                )
                shift = jnp.where(position + anchor < length, 0.0, -1e30)
                product = lax.dot_general(
                    query_rows,
                    key_ref[:, head],
                    (((1,), (1,)), ((), ())),
                    preferred_element_type=jnp.float32,
                )
                scores.append(product * key_scale + shift)
            top = functools.reduce(
                jnp.maximum, [jnp.max(score, axis=-1, keepdims=True) for score in scores]
            )
            if state is not None:
                top = jnp.maximum(top, state[0])
            total, summed = 0.0, 0.0
            for step, score in zip(steps, scores):
                value_ref, value_scale_ref = cache_refs[4 * step + 1], cache_refs[4 * step + 3]
                value_scale = value_scale_ref[g : g + 1, :].astype(jnp.float32)
                probs = jnp.exp2(score - top)
                total = total + jnp.sum(probs, axis=-1, keepdims=True)
                weights = (probs * value_scale).astype(jnp.bfloat16)
                summed = summed + jnp.dot(
                    weights, value_ref[:, head], preferred_element_type=jnp.float32
                )
            if state is not None:
                factor = jnp.exp2(state[0] - top)
                total = total + state[1] * factor
                summed = summed + state[2] * factor
            state = (top, total, summed)
        mixed = state[2] * (scale / state[1])
        high = mixed.astype(jnp.bfloat16)
        low = (mixed - high.astype(jnp.float32)).astype(jnp.bfloat16)
        result = jnp.dot(high, signs, preferred_element_type=jnp.float32) + jnp.dot(
            low, signs, preferred_element_type=jnp.float32
        )
        result = result.astype(jnp.bfloat16)
        for k in range(n_doc):
            out_refs[k][span, :] = result[k * rows_doc : (k + 1) * rows_doc]


def assemble_kernel(n_head, *refs):
    block_refs, out_ref, sems = refs[:n_head], refs[n_head], refs[n_head + 1]
    me = lax.axis_index("head")
    width = block_refs[0].shape[1]
    copies = []
    for step in range(n_head):
        at = pl.multiple_of(peer_of_traced(me, step, n_head) * width, width)
        copies.append(
            pltpu.make_async_copy(block_refs[step], out_ref.at[:, pl.ds(at, width)], sems.at[step])
        )
    for copy in copies:
        copy.start()
    for copy in copies:
        copy.wait()


def peer_of_traced(index, step, count):
    if count & (count - 1) == 0:
        return index ^ step
    return lax.rem(index + step, count)


def shards(
    queries,
    doc_of,
    doc_lengths,
    rotated_key_levels,
    rotated_value_levels,
    key_level_scale,
    value_level_scale,
):
    rows_home, width = queries.shape
    heads_dev = width // HEAD_WIDTH
    kv_dev = key_level_scale.shape[1]
    shard_len = rotated_key_levels.shape[1]
    n_doc = lax.axis_size("doc")
    n_ctx = lax.axis_size("ctx")
    n_head = lax.axis_size("head")
    cap = max(2, 3 * rows_home // (2 * n_doc))
    params = pltpu.CompilerParams(vmem_limit_bytes=VMEM_BYTES)
    vmem = pl.BlockSpec(memory_space=pltpu.VMEM)
    slots = heads_dev * cap
    slot_block = jax.ShapeDtypeStruct((slots, HEAD_WIDTH), jnp.bfloat16)

    own = (rotated_key_levels[0], rotated_value_levels[0], key_level_scale[0], value_level_scale[0])
    cache = list(own)
    for step in range(1, n_ctx):
        pairs = [(i, (i + step) % n_ctx) for i in range(n_ctx)]
        cache += [lax.ppermute(part, "ctx", pairs) for part in own]

    outgoing = pl.pallas_call(
        functools.partial(dispatch_kernel, n_doc, cap),
        out_shape=[slot_block] * n_doc,
        in_specs=[vmem, vmem],
        out_specs=[vmem] * n_doc,
        compiler_params=params,
    )(doc_of, queries)
    arrived = [outgoing[0]] + [sent(outgoing[k], "doc", k) for k in range(1, n_doc)]

    rows = n_doc * slots
    finished = pl.pallas_call(
        functools.partial(attend_kernel, n_doc, n_ctx, kv_dev),
        out_shape=[slot_block] * n_doc,
        in_specs=[pl.BlockSpec(memory_space=pltpu.SMEM)] + [vmem] * (n_doc + 4 * n_ctx),
        out_specs=[vmem] * n_doc,
        compiler_params=params,
        cost_estimate=pl.CostEstimate(
            flops=4 * rows * n_ctx * shard_len * HEAD_WIDTH,
            bytes_accessed=4 * n_ctx * shard_len * kv_dev * HEAD_WIDTH,
            transcendentals=rows * n_ctx * shard_len,
        ),
    )(doc_lengths, *arrived, *cache)
    back = [finished[0]] + [returned(finished[k], "doc", k) for k in range(1, n_doc)]

    mine = pl.pallas_call(
        functools.partial(collect_kernel, n_doc, cap),
        out_shape=jax.ShapeDtypeStruct((rows_home, width), jnp.bfloat16),
        in_specs=[vmem] * (1 + n_doc),
        out_specs=vmem,
        compiler_params=params,
    )(doc_of, *back)

    blocks = [mine] + [returned(mine, "head", step) for step in range(1, n_head)]
    hbm = pl.BlockSpec(memory_space=pl.ANY)
    return pl.pallas_call(
        functools.partial(assemble_kernel, n_head),
        out_shape=jax.ShapeDtypeStruct((rows_home, n_head * width), jnp.bfloat16),
        in_specs=[hbm] * n_head,
        out_specs=hbm,
        scratch_shapes=[pltpu.SemaphoreType.DMA((n_head,))],
        compiler_params=params,
    )(*blocks)


def solution(mesh):
    in_specs = (
        P(("doc", "ctx"), "head"),
        P(("doc", "ctx"), None),
        P(),
        P("doc", "ctx", "head"),
        P("doc", "ctx", "head"),
        P("doc", "head", "ctx"),
        P("doc", "head", "ctx"),
    )
    out_specs = P(("doc", "ctx"), None)
    return jax.shard_map(shards, mesh=mesh, in_specs=in_specs, out_specs=out_specs, check_vma=False)
```

time: 48.6 us -> 38.6 us (0.79)
  blocking collectives: 25.1 us -> 0 us
  waiting for transfers between devices: 0.27 us -> 14.4 us
  starting transfers between devices: 6.31 us -> 13.9 us
  Pallas kernels: 0 us -> 6.61 us
  other arithmetic: 5.88 us -> 0 us
  matrix products: 4.76 us -> 0 us
  local copies, waits for them, and re-layouts: 5.54 us -> 3.39 us
    all_gather x1 -> x0, blocking collectives: 15.4 us -> none  [shards(): return lax.all_gather(mine, 'head', axis=1, tiled=True)]
    ppermute x4 -> x13, waiting for transfers between devices: 0.01 us -> 14.4 us  [the longest x6 9.45 us: returned(): lax.ppermute(value, axis, [(peer_of(i, step, count), i) for i in range(co...]
    ppermute x4 -> x13, starting transfers between devices: 1.14 us -> 13.9 us  [the longest x6 8.29 us: returned(): lax.ppermute(value, axis, [(peer_of(i, step, count), i) for i in range(co...]
    all_to_all x1 -> x0, blocking collectives: 9.72 us -> none  [shards(): lax.all_to_all(finished, 'doc', split_axis=0, concat_axis=0, tiled=True)]
    pallas_call x0 -> x4, Pallas kernels: none -> 6.61 us  [the longest x1 5.05 us: shards(): pl.pallas_call(functools.partial(attend_kernel, n_doc, n_ctx, kv_dev), ou...]
    all_to_all x1 -> x0, starting transfers between devices: 5.18 us -> none  [shards(): lax.all_to_all(outgoing, 'doc', split_axis=0, concat_axis=0, tiled=True)]
    dot_general x8 -> x0, matrix products: 4.76 us -> none  [the longest x2 2.26 us: update_state(): jnp.einsum('bkgs,skd->bkgd', weights, value_block, preferred_element_type...]
    reduce_sum x2 -> x0, other arithmetic: 1.89 us -> none  [the longest x1 1.05 us: update_state(): new_total = current_denominator * factor + jnp.sum(probs, axis=-1)]
  transfers between devices with their start and end apart: 5 -> 13, of which waited for: 1 -> 8; matrix products, arithmetic and copies ran while one was open for 17% -> 0% of each run, Pallas kernels for 0% -> 1%
where the time goes in v1:
time: 38.6 us; the launch traced here: 38.4 us
  waiting for transfers between devices  14.4 us (37%)
  starting transfers between devices  13.9 us (36%)
  Pallas kernels  6.61 us (17%)
  local copies, waits for them, and re-layouts  3.39 us (9%)
    ppermute x6, waiting for transfers between devices, returned(): lax.ppermute(value, axis, [(peer_of(i, step, count), i) for i in range(co...  9.45 us
    ppermute x6, starting transfers between devices, returned(): lax.ppermute(value, axis, [(peer_of(i, step, count), i) for i in range(co...  8.29 us
    pallas_call x1, Pallas kernels, shards(): pl.pallas_call(functools.partial(attend_kernel, n_doc, n_ctx, kv_dev), ou...  5.05 us
    ppermute x3, waiting for transfers between devices, sent(): lax.ppermute(value, axis, [(i, peer_of(i, step, count)) for i in range(co...  4.94 us
    ppermute x3, starting transfers between devices, sent(): lax.ppermute(value, axis, [(i, peer_of(i, step, count)) for i in range(co...  4.57 us
    unnamed x15, local copies, waits for them, and re-layouts  3.39 us
    ppermute x4, starting transfers between devices, shards(): cache += [lax.ppermute(part, 'ctx', pairs) for part in own]  1.03 us
    pallas_call x1, Pallas kernels, shards(): pl.pallas_call(functools.partial(assemble_kernel, n_head), out_shape=jax....  0.82 us
  transfers between devices with their start and end apart: 13, of which 8 were waited for; matrix products, arithmetic and copies ran while one was open for 0% of the time, Pallas kernels for 1%

profile of v1, /device:TPU:0, one launch (start us, length us, event | category | flops | bytes accessed | tf_op | source)
XLA Modules:
  0.0 38.4 jit_solution(1085458714956407777)
XLA Ops:
  0.0 0.5 %collective-permute-start.3 = (bf16[1024,256]{1,0:T(8,128)(2,1)}, bf16[1024,256]{1,0:T(8,128)(2,1)S(1)}, u32[]{:S(2)}, u32[]{:S(2)}) collective-permute-start(bf16[1024,256]{1,0:T(8,128)(2,1)} %bitcast.4), channel_id=1, source_target_pairs={{0,4},{4,0},{1,5},{5,1},{2,6},{6,2},{3,7},{7,3},{8,12},{12,8},{9,1... | collective-permute-start | bytes 1572872 | tf_op jit(solution)/shard_map/ppermute | solution.py:217
  0.5 0.2 copy-done.3
  0.7 0.5 %collective-permute-start.5 = (bf16[2,1024]{1,0:T(2,128)(2,1)S(1)}, bf16[2,1024]{1,0:T(2,128)(2,1)S(1)}, u32[]{:S(2)}, u32[]{:S(2)}) collective-permute-start(bf16[2,1024]{1,0:T(2,128)(2,1)S(1)} %bitcast.8), channel_id=1, source_target_pairs={{0,4},{4,0},{1,5},{5,1},{2,6},{6,2},{3,7},{7,3},{8,12},{12,8},{9,1... | collective-permute-start | bytes 12296 | tf_op jit(solution)/shard_map/ppermute | solution.py:217
  1.4 0.9 %copy-done = bf16[16,4096]{1,0:T(8,128)(2,1)S(1)} copy-done((bf16[16,4096]{1,0:T(8,128)(2,1)S(1)}, bf16[16,4096]{1,0:T(8,128)(2,1)}, u32[]{:S(2)}) %copy-start) | copy-done | bytes 131096
  2.3 0.4 %shard_map.73 = (bf16[192,128]{1,0:T(8,128)(2,1)S(1)}, bf16[192,128]{1,0:T(8,128)(2,1)S(1)}, bf16[192,128]{1,0:T(8,128)(2,1)S(1)}, bf16[192,128]{1,0:T(8,128)(2,1)S(1)}) custom-call(s32[16,1]{1,0:T(8,128)S(1)} %copy.9.doc_ref, bf16[16,4096]{1,0:T(8,128)(2,1)S(1)} %copy-done), custom_call_target="tpu_custom_call" | custom-call | tf_op jit(solution)/shard_map/pallas_call | solution.py:219
  2.8 3.0 %collective-permute-start = (bf16[192,128]{1,0:T(8,128)(2,1)S(1)}, bf16[192,128]{1,0:T(8,128)(2,1)S(1)}, u32[]{:S(2)}, u32[]{:S(2)}) collective-permute-start(bf16[192,128]{1,0:T(8,128)(2,1)S(1)} %get-tuple-element.14), channel_id=1, source_target_pairs={{0,8},{8,0},{16,24},{24,16},{1,9},{9,1},{17,25},{25,17},{2,10},{10... | collective-permute-start | bytes 147464 | tf_op jit(solution)/shard_map/ppermute | solution.py:24
  5.8 1.5 %collective-permute-start.1 = (bf16[192,128]{1,0:T(8,128)(2,1)S(1)}, bf16[192,128]{1,0:T(8,128)(2,1)S(1)}, u32[]{:S(2)}, u32[]{:S(2)}) collective-permute-start(bf16[192,128]{1,0:T(8,128)(2,1)S(1)} %get-tuple-element.15), channel_id=1, source_target_pairs={{0,16},{8,24},{16,0},{24,8},{1,17},{9,25},{17,1},{25,9},{2,18},{10... | collective-permute-start | bytes 147464 | tf_op jit(solution)/shard_map/ppermute | solution.py:24
  7.4 0.5 %collective-permute-done.refs_1_ = bf16[192,128]{1,0:T(8,128)(2,1)S(1)} collective-permute-done((bf16[192,128]{1,0:T(8,128)(2,1)S(1)}, bf16[192,128]{1,0:T(8,128)(2,1)S(1)}, u32[]{:S(2)}, u32[]{:S(2)}) %collective-permute-start) | collective-permute-done | bytes 49184 | tf_op jit(solution)/shard_map/ppermute | solution.py:24
  7.8 2.0 %collective-permute-done.1.refs_2_ = bf16[192,128]{1,0:T(8,128)(2,1)S(1)} collective-permute-done((bf16[192,128]{1,0:T(8,128)(2,1)S(1)}, bf16[192,128]{1,0:T(8,128)(2,1)S(1)}, u32[]{:S(2)}, u32[]{:S(2)}) %collective-permute-start.1) | collective-permute-done | bytes 49184 | tf_op jit(solution)/shard_map/ppermute | solution.py:24
  9.9 2.4 %collective-permute-done.2.refs_3_ = bf16[192,128]{1,0:T(8,128)(2,1)S(1)} collective-permute-done((bf16[192,128]{1,0:T(8,128)(2,1)S(1)}, bf16[192,128]{1,0:T(8,128)(2,1)S(1)}, u32[]{:S(2)}, u32[]{:S(2)}) %collective-permute-start.2) | collective-permute-done | bytes 49184 | tf_op jit(solution)/shard_map/ppermute | solution.py:24
  12.3 1.0 %copy-done.1 = bf16[1,1024,256]{2,1,0:T(8,128)(2,1)S(1)} copy-done((bf16[1,1024,256]{2,1,0:T(8,128)(2,1)S(1)}, bf16[1,1024,256]{2,1,0:T(8,128)(2,1)}, u32[]{:S(2)}) %copy-start.1) | copy-done | bytes 524312
  13.4 1.0 %copy-done.2 = bf16[1,1024,256]{2,1,0:T(8,128)(2,1)S(1)} copy-done((bf16[1,1024,256]{2,1,0:T(8,128)(2,1)S(1)}, bf16[1,1024,256]{2,1,0:T(8,128)(2,1)}, u32[]{:S(2)}) %copy-start.2) | copy-done | bytes 524312
  14.4 5.0 %shard_map.74 = (bf16[192,128]{1,0:T(8,128)(2,1)S(1)}, bf16[192,128]{1,0:T(8,128)(2,1)S(1)}, bf16[192,128]{1,0:T(8,128)(2,1)S(1)}, bf16[192,128]{1,0:T(8,128)(2,1)S(1)}) custom-call(s32[4]{0:T(128)S(1)} %copy-done.5, bf16[192,128]{1,0:T(8,128)(2,1)S(1)} %get-tuple-element.13.refs_0_, bf16[192,128]{1,0:T(8,128)(2,1)S(1)} %collective-permute-done.refs_1_, ...), custom_call_target="tpu_custom_call" | custom-call | flops 805306368 | bytes 2097152 | tf_op jit(solution)/shard_map/pallas_call | solution.py:229
  19.5 0.6 %collective-permute-start.7 = (bf16[192,128]{1,0:T(8,128)(2,1)S(1)}, bf16[192,128]{1,0:T(8,128)(2,1)S(1)}, u32[]{:S(2)}, u32[]{:S(2)}) collective-permute-start(bf16[192,128]{1,0:T(8,128)(2,1)S(1)} %get-tuple-element.18), channel_id=1, source_target_pairs={{8,0},{0,8},{24,16},{16,24},{9,1},{1,9},{25,17},{17,25},{10,2},{2,... | collective-permute-start | bytes 147464 | tf_op jit(solution)/shard_map/ppermute | solution.py:29
  20.1 2.9 %collective-permute-start.9 = (bf16[192,128]{1,0:T(8,128)(2,1)S(1)}, bf16[192,128]{1,0:T(8,128)(2,1)S(1)}, u32[]{:S(2)}, u32[]{:S(2)}) collective-permute-start(bf16[192,128]{1,0:T(8,128)(2,1)S(1)} %get-tuple-element.20), channel_id=1, source_target_pairs={{24,0},{16,8},{8,16},{0,24},{25,1},{17,9},{9,17},{1,25},{26,2},{18... | collective-permute-start | bytes 147464 | tf_op jit(solution)/shard_map/ppermute | solution.py:29
  23.0 0.6 %collective-permute-done.7.refs_1_ = bf16[192,128]{1,0:T(8,128)(2,1)S(1)} collective-permute-done((bf16[192,128]{1,0:T(8,128)(2,1)S(1)}, bf16[192,128]{1,0:T(8,128)(2,1)S(1)}, u32[]{:S(2)}, u32[]{:S(2)}) %collective-permute-start.7) | collective-permute-done | bytes 49184 | tf_op jit(solution)/shard_map/ppermute | solution.py:29
  23.6 0.5 %collective-permute-done.8.refs_2_ = bf16[192,128]{1,0:T(8,128)(2,1)S(1)} collective-permute-done((bf16[192,128]{1,0:T(8,128)(2,1)S(1)}, bf16[192,128]{1,0:T(8,128)(2,1)S(1)}, u32[]{:S(2)}, u32[]{:S(2)}) %collective-permute-start.8) | collective-permute-done | bytes 49184 | tf_op jit(solution)/shard_map/ppermute | solution.py:29
  24.1 1.0 %collective-permute-done.9.refs_3_ = bf16[192,128]{1,0:T(8,128)(2,1)S(1)} collective-permute-done((bf16[192,128]{1,0:T(8,128)(2,1)S(1)}, bf16[192,128]{1,0:T(8,128)(2,1)S(1)}, u32[]{:S(2)}, u32[]{:S(2)}) %collective-permute-start.9) | collective-permute-done | bytes 49184 | tf_op jit(solution)/shard_map/ppermute | solution.py:29
  25.1 0.3 shard_map.75.refs_0_
  25.5 4.1 %collective-permute-start.12 = (bf16[16,4096]{1,0:T(8,128)(2,1)S(1)}, bf16[16,4096]{1,0:T(8,128)(2,1)S(1)}, u32[]{:S(2)}, u32[]{:S(2)}) collective-permute-start(bf16[16,4096]{1,0:T(8,128)(2,1)S(1)} %shard_map.75.refs_0_), channel_id=1, source_target_pairs={{3,0},{2,1},{1,2},{0,3},{7,4},{6,5},{5,6},{4,7},{11,8},{10,9},{9,1... | collective-permute-start | bytes 393224 | tf_op jit(solution)/shard_map/ppermute | solution.py:29
  29.6 0.6 %collective-permute-start.10 = (bf16[16,4096]{1,0:T(8,128)(2,1)S(1)}, bf16[16,4096]{1,0:T(8,128)(2,1)S(1)}, u32[]{:S(2)}, u32[]{:S(2)}) collective-permute-start(bf16[16,4096]{1,0:T(8,128)(2,1)S(1)} %shard_map.75.refs_0_), channel_id=1, source_target_pairs={{1,0},{0,1},{3,2},{2,3},{5,4},{4,5},{7,6},{6,7},{9,8},{8,9},{11,10... | collective-permute-start | bytes 393224 | tf_op jit(solution)/shard_map/ppermute | solution.py:29
  30.2 3.4 %collective-permute-done.12.refs_3_ = bf16[16,4096]{1,0:T(8,128)(2,1)S(1)} collective-permute-done((bf16[16,4096]{1,0:T(8,128)(2,1)S(1)}, bf16[16,4096]{1,0:T(8,128)(2,1)S(1)}, u32[]{:S(2)}, u32[]{:S(2)}) %collective-permute-start.12) | collective-permute-done | bytes 131104 | tf_op jit(solution)/shard_map/ppermute | solution.py:29
  33.6 3.9 %collective-permute-done.11.refs_2_ = bf16[16,4096]{1,0:T(8,128)(2,1)S(1)} collective-permute-done((bf16[16,4096]{1,0:T(8,128)(2,1)S(1)}, bf16[16,4096]{1,0:T(8,128)(2,1)S(1)}, u32[]{:S(2)}, u32[]{:S(2)}) %collective-permute-start.11) | collective-permute-done | bytes 131104 | tf_op jit(solution)/shard_map/ppermute | solution.py:29
  37.5 0.8 %shard_map.76 = bf16[16,16384]{1,0:T(8,128)(2,1)} custom-call(bf16[16,4096]{1,0:T(8,128)(2,1)S(1)} %shard_map.75.refs_0_, bf16[16,4096]{1,0:T(8,128)(2,1)S(1)} %collective-permute-done.10.refs_1_, bf16[16,4096]{1,0:T(8,128)(2,1)S(1)} %collective-permute-done.11.refs_2_, bf16[16,4096]{1,0:T(8,128)(2,1)S(1)} %collective-permute-done.12.refs_3_), custom_call_target="tpu_custom_call" | custom-call | tf_op jit(solution)/shard_map/pallas_call | solution.py:253
  (21 shorter events, 0.5 us)
Async XLA Ops:
  0.0 0.7 %copy-start.3 = (bf16[1,2,1024]{2,1,0:T(2,128)(2,1)S(1)}, bf16[1,2,1024]{2,1,0:T(2,128)(2,1)}, u32[]{:S(2)}) copy-start(bf16[1,2,1024]{2,1,0:T(2,128)(2,1)} %param.12) | copy-start | bytes 12292
  0.0 12.3 %collective-permute-start.3 = (bf16[1024,256]{1,0:T(8,128)(2,1)}, bf16[1024,256]{1,0:T(8,128)(2,1)S(1)}, u32[]{:S(2)}, u32[]{:S(2)}) collective-permute-start(bf16[1024,256]{1,0:T(8,128)(2,1)} %bitcast.4), channel_id=1, source_target_pairs={{0,4},{4,0},{1,5},{5,1},{2,6},{6,2},{3,7},{7,3},{8,12},{12,8},{9,1... | collective-permute-start | bytes 1572872 | tf_op jit(solution)/shard_map/ppermute | solution.py:217
  0.5 11.8 %collective-permute-start.4 = (bf16[1024,256]{1,0:T(8,128)(2,1)}, bf16[1024,256]{1,0:T(8,128)(2,1)S(1)}, u32[]{:S(2)}, u32[]{:S(2)}) collective-permute-start(bf16[1024,256]{1,0:T(8,128)(2,1)} %bitcast.6), channel_id=1, source_target_pairs={{0,4},{4,0},{1,5},{5,1},{2,6},{6,2},{3,7},{7,3},{8,12},{12,8},{9,1... | collective-permute-start | bytes 1572872 | tf_op jit(solution)/shard_map/ppermute | solution.py:217
  0.7 0.7 %copy-start.6 = (s32[16,1]{0,1:T(1,128)S(1)}, s32[16,1]{0,1:T(1,128)}, u32[]{:S(2)}) copy-start(s32[16,1]{0,1:T(1,128)} %param.8) | copy-start | bytes 196
  0.7 5.1 %collective-permute-start.5 = (bf16[2,1024]{1,0:T(2,128)(2,1)S(1)}, bf16[2,1024]{1,0:T(2,128)(2,1)S(1)}, u32[]{:S(2)}, u32[]{:S(2)}) collective-permute-start(bf16[2,1024]{1,0:T(2,128)(2,1)S(1)} %bitcast.8), channel_id=1, source_target_pairs={{0,4},{4,0},{1,5},{5,1},{2,6},{6,2},{3,7},{7,3},{8,12},{12,8},{9,1... | collective-permute-start | bytes 12296 | tf_op jit(solution)/shard_map/ppermute | solution.py:217
  1.1 6.2 %collective-permute-start.6 = (bf16[2,1024]{1,0:T(2,128)(2,1)}, bf16[2,1024]{1,0:T(2,128)(2,1)S(1)}, u32[]{:S(2)}, u32[]{:S(2)}) collective-permute-start(bf16[2,1024]{1,0:T(2,128)(2,1)} %bitcast.10), channel_id=1, source_target_pairs={{0,4},{4,0},{1,5},{5,1},{2,6},{6,2},{3,7},{7,3},{8,12},{12,8},{9,1... | collective-permute-start | bytes 12296 | tf_op jit(solution)/shard_map/ppermute | solution.py:217
  1.4 0.9 %copy-start = (bf16[16,4096]{1,0:T(8,128)(2,1)S(1)}, bf16[16,4096]{1,0:T(8,128)(2,1)}, u32[]{:S(2)}) copy-start(bf16[16,4096]{1,0:T(8,128)(2,1)} %query_ref.1) | copy-start | bytes 393220
  2.8 9.5 %copy-start.4 = (bf16[1,2,1024]{2,1,0:T(2,128)(2,1)S(1)}, bf16[1,2,1024]{2,1,0:T(2,128)(2,1)}, u32[]{:S(2)}) copy-start(bf16[1,2,1024]{2,1,0:T(2,128)(2,1)} %param.13) | copy-start | bytes 12292
  2.8 5.1 %collective-permute-start = (bf16[192,128]{1,0:T(8,128)(2,1)S(1)}, bf16[192,128]{1,0:T(8,128)(2,1)S(1)}, u32[]{:S(2)}, u32[]{:S(2)}) collective-permute-start(bf16[192,128]{1,0:T(8,128)(2,1)S(1)} %get-tuple-element.14), channel_id=1, source_target_pairs={{0,8},{8,0},{16,24},{24,16},{1,9},{9,1},{17,25},{25,17},{2,10},{10... | collective-permute-start | bytes 147464 | tf_op jit(solution)/shard_map/ppermute | solution.py:24
  5.8 4.1 %collective-permute-start.1 = (bf16[192,128]{1,0:T(8,128)(2,1)S(1)}, bf16[192,128]{1,0:T(8,128)(2,1)S(1)}, u32[]{:S(2)}, u32[]{:S(2)}) collective-permute-start(bf16[192,128]{1,0:T(8,128)(2,1)S(1)} %get-tuple-element.15), channel_id=1, source_target_pairs={{0,16},{8,24},{16,0},{24,8},{1,17},{9,25},{17,1},{25,9},{2,18},{10... | collective-permute-start | bytes 147464 | tf_op jit(solution)/shard_map/ppermute | solution.py:24
  7.3 5.0 %copy-start.5 = (s32[4]{0:T(128)S(1)}, s32[4]{0:T(128)}, u32[]{:S(2)}) copy-start(s32[4]{0:T(128)} %length_ref.1) | copy-start | bytes 52
  7.3 5.0 %collective-permute-start.2 = (bf16[192,128]{1,0:T(8,128)(2,1)S(1)}, bf16[192,128]{1,0:T(8,128)(2,1)S(1)}, u32[]{:S(2)}, u32[]{:S(2)}) collective-permute-start(bf16[192,128]{1,0:T(8,128)(2,1)S(1)} %get-tuple-element.16), channel_id=1, source_target_pairs={{0,24},{8,16},{16,8},{24,0},{1,25},{9,17},{17,9},{25,1},{2,26},{10... | collective-permute-start | bytes 147464 | tf_op jit(solution)/shard_map/ppermute | solution.py:24
  12.3 1.0 %copy-start.1 = (bf16[1,1024,256]{2,1,0:T(8,128)(2,1)S(1)}, bf16[1,1024,256]{2,1,0:T(8,128)(2,1)}, u32[]{:S(2)}) copy-start(bf16[1,1024,256]{2,1,0:T(8,128)(2,1)} %param.10) | copy-start | bytes 1572868
  13.4 1.0 %copy-start.2 = (bf16[1,1024,256]{2,1,0:T(8,128)(2,1)S(1)}, bf16[1,1024,256]{2,1,0:T(8,128)(2,1)}, u32[]{:S(2)}) copy-start(bf16[1,1024,256]{2,1,0:T(8,128)(2,1)} %param.11) | copy-start | bytes 1572868
  19.5 4.2 %collective-permute-start.7 = (bf16[192,128]{1,0:T(8,128)(2,1)S(1)}, bf16[192,128]{1,0:T(8,128)(2,1)S(1)}, u32[]{:S(2)}, u32[]{:S(2)}) collective-permute-start(bf16[192,128]{1,0:T(8,128)(2,1)S(1)} %get-tuple-element.18), channel_id=1, source_target_pairs={{8,0},{0,8},{24,16},{16,24},{9,1},{1,9},{25,17},{17,25},{10,2},{2,... | collective-permute-start | bytes 147464 | tf_op jit(solution)/shard_map/ppermute | solution.py:29
  20.1 4.1 %collective-permute-start.8 = (bf16[192,128]{1,0:T(8,128)(2,1)S(1)}, bf16[192,128]{1,0:T(8,128)(2,1)S(1)}, u32[]{:S(2)}, u32[]{:S(2)}) collective-permute-start(bf16[192,128]{1,0:T(8,128)(2,1)S(1)} %get-tuple-element.19), channel_id=1, source_target_pairs={{16,0},{24,8},{0,16},{8,24},{17,1},{25,9},{1,17},{9,25},{18,2},{26... | collective-permute-start | bytes 147464 | tf_op jit(solution)/shard_map/ppermute | solution.py:29
  20.1 5.0 %collective-permute-start.9 = (bf16[192,128]{1,0:T(8,128)(2,1)S(1)}, bf16[192,128]{1,0:T(8,128)(2,1)S(1)}, u32[]{:S(2)}, u32[]{:S(2)}) collective-permute-start(bf16[192,128]{1,0:T(8,128)(2,1)S(1)} %get-tuple-element.20), channel_id=1, source_target_pairs={{24,0},{16,8},{8,16},{0,24},{25,1},{17,9},{9,17},{1,25},{26,2},{18... | collective-permute-start | bytes 147464 | tf_op jit(solution)/shard_map/ppermute | solution.py:29
  25.5 8.1 %collective-permute-start.12 = (bf16[16,4096]{1,0:T(8,128)(2,1)S(1)}, bf16[16,4096]{1,0:T(8,128)(2,1)S(1)}, u32[]{:S(2)}, u32[]{:S(2)}) collective-permute-start(bf16[16,4096]{1,0:T(8,128)(2,1)S(1)} %shard_map.75.refs_0_), channel_id=1, source_target_pairs={{3,0},{2,1},{1,2},{0,3},{7,4},{6,5},{5,6},{4,7},{11,8},{10,9},{9,1... | collective-permute-start | bytes 393224 | tf_op jit(solution)/shard_map/ppermute | solution.py:29
  29.6 8.0 %collective-permute-start.11 = (bf16[16,4096]{1,0:T(8,128)(2,1)S(1)}, bf16[16,4096]{1,0:T(8,128)(2,1)S(1)}, u32[]{:S(2)}, u32[]{:S(2)}) collective-permute-start(bf16[16,4096]{1,0:T(8,128)(2,1)S(1)} %shard_map.75.refs_0_), channel_id=1, source_target_pairs={{2,0},{3,1},{0,2},{1,3},{6,4},{7,5},{4,6},{5,7},{10,8},{11,9},{8,1... | collective-permute-start | bytes 393224 | tf_op jit(solution)/shard_map/ppermute | solution.py:29
  29.6 8.0 %collective-permute-start.10 = (bf16[16,4096]{1,0:T(8,128)(2,1)S(1)}, bf16[16,4096]{1,0:T(8,128)(2,1)S(1)}, u32[]{:S(2)}, u32[]{:S(2)}) collective-permute-start(bf16[16,4096]{1,0:T(8,128)(2,1)S(1)} %shard_map.75.refs_0_), channel_id=1, source_target_pairs={{1,0},{0,1},{3,2},{2,3},{5,4},{4,5},{7,6},{6,7},{9,8},{8,9},{11,10... | collective-permute-start | bytes 393224 | tf_op jit(solution)/shard_map/ppermute | solution.py:29

commit v2 on v1

v2 whole, which is shorter than its diff:
```python
import functools
import math

import jax
import jax.numpy as jnp
from jax import lax
from jax.experimental import pallas as pl
from jax.experimental.pallas import tpu as pltpu
from jax.sharding import PartitionSpec as P

HEAD_WIDTH = 128
LANES = 128
VMEM_BYTES = 40 * 1024 * 1024


def peer_of(index, step, count):
    if count & (count - 1) == 0:
        return index ^ step
    return (index + step) % count


def sent(value, axis, step):
    count = lax.axis_size(axis)
    return lax.ppermute(value, axis, [(i, peer_of(i, step, count)) for i in range(count)])


def returned(value, axis, step):
    count = lax.axis_size(axis)
    return lax.ppermute(value, axis, [(peer_of(i, step, count), i) for i in range(count)])


def sign_matrix():
    row = lax.broadcasted_iota(jnp.int32, (HEAD_WIDTH, HEAD_WIDTH), 0)
    column = lax.broadcasted_iota(jnp.int32, (HEAD_WIDTH, HEAD_WIDTH), 1)
    both = row & column
    both = both ^ (both >> 4)
    both = both ^ (both >> 2)
    both = both ^ (both >> 1)
    return (1 - 2 * (both & 1)).astype(jnp.float32).astype(jnp.bfloat16)


def placing_matrix(doc_row, n_doc, cap):
    rows = doc_row.shape[1]
    group = LANES // rows
    me = lax.axis_index("doc")
    square = (rows, rows)
    diagonal = lax.broadcasted_iota(jnp.int32, square, 0) == lax.broadcasted_iota(
        jnp.int32, square, 1
    )
    doc_column = jnp.sum(
        jnp.where(diagonal, jnp.broadcast_to(doc_row, square), 0), axis=1, keepdims=True
    )
    request = lax.broadcasted_iota(jnp.int32, (rows, LANES), 0)
    lane = lax.broadcasted_iota(jnp.int32, (rows, LANES), 1)
    docs = jnp.broadcast_to(doc_column, (rows, LANES))
    lane_request = lane % rows
    lane_doc = jnp.sum(jnp.where(request == lane_request, docs, 0), axis=0, keepdims=True)
    rank = jnp.sum(
        jnp.where((docs == lane_doc) & (request < lane_request), 1, 0), axis=0, keepdims=True
    )
    if n_doc & (n_doc - 1) == 0:
        step = lane_doc ^ me
    else:
        step = (lane_doc - me + n_doc) % n_doc
    place = step * (group * cap) + (lane[:1] // rows) * cap + rank
    slots = n_doc * group * cap
    slot = lax.broadcasted_iota(jnp.int32, (slots, LANES), 0)
    return jnp.where(slot == place, 1.0, 0.0).astype(jnp.bfloat16)


def dispatch_kernel(
    n_doc,
    n_ctx,
    cap,
    doc_hbm,
    length_hbm,
    query_hbm,
    key_hbm,
    value_hbm,
    key_scale_hbm,
    value_scale_hbm,
    placing_ref,
    shift_ref,
    scales_ref,
    key_ref,
    value_ref,
    *refs,
):
    out_refs, (doc_ref, length_ref, query_ref, key_scale_ref, value_scale_ref, sems) = (
        refs[:n_doc],
        refs[n_doc:],
    )
    pairs = (
        (doc_hbm, doc_ref),
        (query_hbm, query_ref),
        (length_hbm, length_ref),
        (key_scale_hbm, key_scale_ref),
        (value_scale_hbm, value_scale_ref),
        (key_hbm, key_ref),
        (value_hbm, value_ref),
    )
    copies = [
        pltpu.make_async_copy(source, target, sems.at[at])
        for at, (source, target) in enumerate(pairs)
    ]
    for copy in copies:
        copy.start()
    rows, width = query_ref.shape
    group = LANES // rows
    heads = width // HEAD_WIDTH
    block = group * cap
    signs = sign_matrix()
    scale = 1.0 / math.sqrt(HEAD_WIDTH)
    copies[0].wait()
    placing = placing_matrix(doc_ref[...], n_doc, cap)
    placing_ref[...] = placing
    copies[1].wait()
    rotated = []
    for g in range(heads // group):
        stacked = jnp.concatenate(
            [
                query_ref[:, (g * group + h) * HEAD_WIDTH : (g * group + h + 1) * HEAD_WIDTH]
                for h in range(group)
            ],
            axis=0,
        )
        product = jnp.dot(stacked, signs, preferred_element_type=jnp.float32) * scale
        rotated.append(product.astype(jnp.bfloat16))
    for g in range(heads // group):
        placed = jnp.dot(placing, rotated[g], preferred_element_type=jnp.float32).astype(
            jnp.bfloat16
        )
        for k in range(n_doc):
            out_refs[k][g * block : (g + 1) * block, :] = placed[k * block : (k + 1) * block]
    for copy in copies[2:5]:
        copy.wait()
    scales_ref[...] = jnp.concatenate(
        [key_scale_ref[...].astype(jnp.float32), value_scale_ref[...].astype(jnp.float32)], axis=0
    ).astype(jnp.bfloat16)
    lengths = length_ref[...]
    lane = lax.broadcasted_iota(jnp.int32, lengths.shape, 1)
    length = jnp.sum(
        jnp.where(lane == lax.axis_index("doc"), lengths, 0), axis=1, keepdims=True
    )
    shard_len = key_ref.shape[0]
    step = lax.broadcasted_iota(jnp.int32, shift_ref.shape, 0)
    anchor = (lax.axis_index("ctx") - step + n_ctx) % n_ctx
    position = lax.broadcasted_iota(jnp.int32, shift_ref.shape, 1) + anchor * shard_len
    shift_ref[...] = jnp.where(position < length, 0.0, -1e30)
    for copy in copies[5:]:
        copy.wait()


def collect_kernel(n_doc, cap, placing_ref, *refs):
    back_refs, out_ref = refs[:n_doc], refs[n_doc]
    rows, width = out_ref.shape
    group = LANES // rows
    heads = width // HEAD_WIDTH
    block = group * cap
    placing = placing_ref[...]
    for g in range(heads // group):
        slots = jnp.concatenate(
            [back_refs[k][g * block : (g + 1) * block, :] for k in range(n_doc)], axis=0
        )
        mine = lax.dot_general(
            placing, slots, (((0,), (0,)), ((), ())), preferred_element_type=jnp.float32
        ).astype(jnp.bfloat16)
        for h in range(group):
            at = (g * group + h) * HEAD_WIDTH
            out_ref[:, at : at + HEAD_WIDTH] = mine[h * rows : (h + 1) * rows]


def attend_kernel(sources, n_ctx, kv_dev, shift_ref, *refs):
    query_refs, refs = refs[:sources], refs[sources:]
    cache_refs, out_refs = refs[: 3 * n_ctx], refs[3 * n_ctx :]
    rows_doc = query_refs[0].shape[0] // kv_dev
    signs = sign_matrix()
    scale = 1.0 / math.sqrt(HEAD_WIDTH)
    groups = range(kv_dev)
    spans = [slice(g * rows_doc, (g + 1) * rows_doc) for g in groups]
    heads = [slice(g * HEAD_WIDTH, (g + 1) * HEAD_WIDTH) for g in groups]
    rows = [jnp.concatenate([ref[span, :] for ref in query_refs], axis=0) for span in spans]
    states = [None] * kv_dev
    for first in range(0, n_ctx, 2):
        steps = range(first, min(first + 2, n_ctx))
        scores = {}
        for g in groups:
            for step in steps:
                key_ref, scales_ref = cache_refs[3 * step], cache_refs[3 * step + 2]
                key_scale = scales_ref[g : g + 1, :].astype(jnp.float32) * (
                    scale * math.log2(math.e)
                )
                product = lax.dot_general(
                    rows[g],
                    key_ref[:, heads[g]],
                    (((1,), (1,)), ((), ())),
                    preferred_element_type=jnp.float32,
                )
                scores[g, step] = product * key_scale + shift_ref[step : step + 1, :]
        tops = []
        for g in groups:
            top = functools.reduce(
                jnp.maximum, [jnp.max(scores[g, step], axis=-1, keepdims=True) for step in steps]
            )
            tops.append(top if states[g] is None else jnp.maximum(top, states[g][0]))
        for g in groups:
            all_probs, summed = 0.0, 0.0
            for step in steps:
                value_ref, scales_ref = cache_refs[3 * step + 1], cache_refs[3 * step + 2]
                value_scale = scales_ref[kv_dev + g : kv_dev + g + 1, :].astype(jnp.float32)
                probs = jnp.exp2(scores[g, step] - tops[g])
                all_probs = all_probs + probs
                weights = (probs * value_scale).astype(jnp.bfloat16)
                summed = summed + jnp.dot(
                    weights, value_ref[:, heads[g]], preferred_element_type=jnp.float32
                )
            total = jnp.sum(all_probs, axis=-1, keepdims=True)
            if states[g] is not None:
                factor = jnp.exp2(states[g][0] - tops[g])
                total = total + states[g][1] * factor
                summed = summed + states[g][2] * factor
            states[g] = (tops[g], total, summed)
    for g in groups:
        _, total, summed = states[g]
        mixed = summed * (scale / total)
        high = mixed.astype(jnp.bfloat16)
        low = (mixed - high.astype(jnp.float32)).astype(jnp.bfloat16)
        result = jnp.dot(high, signs, preferred_element_type=jnp.float32) + jnp.dot(
            low, signs, preferred_element_type=jnp.float32
        )
        result = result.astype(jnp.bfloat16)
        for k in range(sources):
            out_refs[k][spans[g], :] = result[k * rows_doc : (k + 1) * rows_doc]


def assemble_kernel(n_head, places, *refs):
    block_refs, out_ref, sems = refs[: len(places)], refs[-2], refs[-1]
    me, parity = lax.axis_index("head"), lax.rem(lax.axis_index("ctx"), 2)
    width = block_refs[0].shape[1]
    copies = []
    for at, (step, wanted) in enumerate(places):
        column = pl.multiple_of(peer_of_traced(me, step, n_head) * width, width)
        copy = pltpu.make_async_copy(
            block_refs[at], out_ref.at[:, pl.ds(column, width)], sems.at[at]
        )
        copies.append((copy, wanted))
    for copy, wanted in copies:
        if wanted is None:
            copy.start()
        else:
            pl.when(parity == wanted)(copy.start)
    for copy, wanted in copies:
        if wanted is None:
            copy.wait()
        else:
            pl.when(parity == wanted)(copy.wait)


def peer_of_traced(index, step, count):
    if count & (count - 1) == 0:
        return index ^ step
    return lax.rem(index + step, count)


def shards(
    queries,
    doc_of,
    doc_lengths,
    rotated_key_levels,
    rotated_value_levels,
    key_level_scale,
    value_level_scale,
):
    rows_home, width = queries.shape
    heads_dev = width // HEAD_WIDTH
    kv_dev = key_level_scale.shape[1]
    shard_len = rotated_key_levels.shape[1]
    n_doc = lax.axis_size("doc")
    n_ctx = lax.axis_size("ctx")
    n_head = lax.axis_size("head")
    cap = max(2, 3 * rows_home // (2 * n_doc))
    params = pltpu.CompilerParams(vmem_limit_bytes=VMEM_BYTES)
    vmem = pl.BlockSpec(memory_space=pltpu.VMEM)
    slots = heads_dev * cap
    slot_block = jax.ShapeDtypeStruct((slots, HEAD_WIDTH), jnp.bfloat16)

    key_block, value_block = rotated_key_levels[0], rotated_value_levels[0]
    args = (
        doc_of.reshape(1, rows_home),
        doc_lengths.reshape(1, doc_lengths.shape[0]),
        queries,
        key_block,
        value_block,
        key_level_scale[0],
        value_level_scale[0],
    )
    placing_block = jax.ShapeDtypeStruct((n_doc * (LANES // rows_home) * cap, LANES), jnp.bfloat16)
    hbm = pl.BlockSpec(memory_space=pltpu.HBM)
    anywhere = pl.BlockSpec(memory_space=pl.ANY)
    placing, shift, scales, own_key, own_value, *outgoing = pl.pallas_call(
        functools.partial(dispatch_kernel, n_doc, n_ctx, cap),
        out_shape=[
            placing_block,
            jax.ShapeDtypeStruct((n_ctx, shard_len), jnp.float32),
            jax.ShapeDtypeStruct((2 * kv_dev, shard_len), jnp.bfloat16),
            jax.ShapeDtypeStruct(key_block.shape, key_block.dtype),
            jax.ShapeDtypeStruct(value_block.shape, value_block.dtype),
        ]
        + [slot_block] * n_doc,
        in_specs=[hbm] * len(args),
        out_specs=[vmem] * (n_doc + 5),
        scratch_shapes=[
            pltpu.VMEM(args[at].shape, args[at].dtype) for at in (0, 1, 2, 5, 6)
        ]
        + [pltpu.SemaphoreType.DMA((len(args),))],
        compiler_params=params,
    )(*[pltpu.with_memory_space_constraint(arg, pltpu.HBM) for arg in args])
    cache = [own_key, own_value, scales]
    for step in range(1, n_ctx):
        pairs = [(i, (i + step) % n_ctx) for i in range(n_ctx)]
        cache += [lax.ppermute(part, "ctx", pairs) for part in (key_block, value_block, scales)]
    arrived = [outgoing[0]] + [sent(outgoing[k], "doc", k) for k in range(1, n_doc)]

    def attended_for(steps):
        sources = [arrived[k] for k in steps]
        rows = len(sources) * slots
        return pl.pallas_call(
            functools.partial(attend_kernel, len(sources), n_ctx, kv_dev),
            out_shape=[slot_block] * len(sources),
            in_specs=[vmem] * (1 + len(sources) + 3 * n_ctx),
            out_specs=[vmem] * len(sources),
            compiler_params=params,
            cost_estimate=pl.CostEstimate(
                flops=4 * rows * n_ctx * shard_len * HEAD_WIDTH,
                bytes_accessed=4 * n_ctx * shard_len * kv_dev * HEAD_WIDTH,
                transcendentals=rows * n_ctx * shard_len,
            ),
        )(shift, *sources, *cache)

    half = max(1, n_doc // 2)
    finished = []
    for first in range(0, n_doc, half):
        finished += attended_for(range(first, min(first + half, n_doc)))
    back = [finished[0]] + [returned(finished[k], "doc", k) for k in range(1, n_doc)]

    def assembled(pieces, before):
        return pl.pallas_call(
            functools.partial(assemble_kernel, n_head, [place for place, _ in pieces]),
            out_shape=jax.ShapeDtypeStruct((rows_home, n_head * width), jnp.bfloat16),
            in_specs=[anywhere] * len(pieces) + [hbm] * len(before),
            out_specs=hbm,
            scratch_shapes=[pltpu.SemaphoreType.DMA((len(pieces),))],
            input_output_aliases={len(pieces): 0} if before else {},
            compiler_params=params,
        )(*[block for _, block in pieces], *before)

    mine = pl.pallas_call(
        functools.partial(collect_kernel, n_doc, cap),
        out_shape=jax.ShapeDtypeStruct((rows_home, width), jnp.bfloat16),
        in_specs=[vmem] * (1 + n_doc),
        out_specs=vmem,
        compiler_params=params,
    )(placing, *back)

    if n_head != 4:
        return assembled(
            [((0, None), mine)]
            + [((step, None), returned(mine, "head", step)) for step in range(1, n_head)],
            (),
        )
    devices = [(c, h) for c in range(n_ctx) for h in range(n_head)]

    def swapped(value, step, parity):
        pairs = [
            (c * n_head + h, c * n_head + (h ^ step)) for c, h in devices if c % 2 == parity
        ]
        return lax.ppermute(value, ("ctx", "head"), pairs)

    mirror = returned(mine, "head", 3)
    near = returned(mine, "head", 1)
    second = swapped(mine, 2, 0)
    passed = swapped(mirror, 1, 1)
    attended = assembled([((0, None), mine), ((3, None), mirror)], ())
    return assembled([((1, None), near), ((2, 0), second), ((2, 1), passed)], (attended,))


def solution(mesh):
    in_specs = (
        P(("doc", "ctx"), "head"),
        P(("doc", "ctx"), None),
        P(),
        P("doc", "ctx", "head"),
        P("doc", "ctx", "head"),
        P("doc", "head", "ctx"),
        P("doc", "head", "ctx"),
    )
    out_specs = P(("doc", "ctx"), None)
    return jax.shard_map(shards, mesh=mesh, in_specs=in_specs, out_specs=out_specs, check_vma=False)
```

time: 38.6 us -> 32.6 us (0.84)
  waiting for transfers between devices: 14.4 us -> 9.2 us
  local copies, waits for them, and re-layouts: 3.39 us -> 0 us
  starting transfers between devices: 13.9 us -> 16.9 us
    ppermute x6 -> x5, waiting for transfers between devices: 9.45 us -> 4.82 us  [returned(): lax.ppermute(value, axis, [(peer_of(i, step, count), i) for i in range(co...]
    ppermute x3, waiting for transfers between devices: 4.94 us -> 0.69 us  [sent(): lax.ppermute(value, axis, [(i, peer_of(i, step, count)) for i in range(co...]
    ppermute x4 -> x5, waiting for transfers between devices: 0.01 us -> 3.69 us  [the longest x2 3.68 us: swapped(): return lax.ppermute(value, ('ctx', 'head'), pairs)]
    unnamed x15 -> x0, local copies, waits for them, and re-layouts: 3.39 us -> none
    ppermute x4 -> x5, starting transfers between devices: 1.03 us -> 3.08 us  [the longest x2 2.57 us: swapped(): return lax.ppermute(value, ('ctx', 'head'), pairs)]
    ppermute x3, starting transfers between devices: 4.57 us -> 5.66 us  [sent(): lax.ppermute(value, axis, [(i, peer_of(i, step, count)) for i in range(co...]
    pallas_call x3 -> x5, Pallas kernels: 6.28 us -> 6.04 us  [the longest x2 3.17 us: attended_for(): pl.pallas_call(functools.partial(attend_kernel, len(sources), n_ctx, kv_d...]
    ppermute x6 -> x5, starting transfers between devices: 8.29 us -> 8.12 us  [returned(): lax.ppermute(value, axis, [(peer_of(i, step, count), i) for i in range(co...]
  transfers between devices with their start and end apart: 13 -> 13, of which waited for: 8 -> 6; matrix products, arithmetic and copies ran while one was open for 0% -> 0% of each run, Pallas kernels for 1% -> 16%
where the time goes in v2:
time: 32.6 us; the launch traced here: 32.4 us
  starting transfers between devices  16.9 us (52%)
  waiting for transfers between devices  9.2 us (28%)
  Pallas kernels  6.28 us (19%)
    ppermute x5, starting transfers between devices, returned(): lax.ppermute(value, axis, [(peer_of(i, step, count), i) for i in range(co...  8.12 us
    ppermute x3, starting transfers between devices, sent(): lax.ppermute(value, axis, [(i, peer_of(i, step, count)) for i in range(co...  5.66 us
    ppermute x5, waiting for transfers between devices, returned(): lax.ppermute(value, axis, [(peer_of(i, step, count), i) for i in range(co...  4.82 us
    ppermute x2, waiting for transfers between devices, swapped(): return lax.ppermute(value, ('ctx', 'head'), pairs)  3.68 us
    pallas_call x2, Pallas kernels, attended_for(): pl.pallas_call(functools.partial(attend_kernel, len(sources), n_ctx, kv_d...  3.17 us
    ppermute x2, starting transfers between devices, swapped(): return lax.ppermute(value, ('ctx', 'head'), pairs)  2.57 us
    pallas_call x2, Pallas kernels, assembled(): pl.pallas_call(functools.partial(assemble_kernel, n_head, [place for plac...  1.45 us
    pallas_call x1, Pallas kernels, shards(): pl.pallas_call(functools.partial(dispatch_kernel, n_doc, n_ctx, cap), out...  1.42 us
  transfers between devices with their start and end apart: 13, of which 6 were waited for; matrix products, arithmetic and copies ran while one was open for 0% of the time, Pallas kernels for 16%

profile of v2, /device:TPU:0, one launch (start us, length us, event | category | flops | bytes accessed | tf_op | source)
XLA Modules:
  0.0 32.4 jit_solution(17972251251653274631)
XLA Ops:
  0.0 0.5 %collective-permute-start.1 = (bf16[1024,256]{1,0:T(8,128)(2,1)}, bf16[1024,256]{1,0:T(8,128)(2,1)S(1)}, u32[]{:S(2)}, u32[]{:S(2)}) collective-permute-start(bf16[1024,256]{1,0:T(8,128)(2,1)} %bitcast.6), channel_id=1, source_target_pairs={{0,4},{4,0},{1,5},{5,1},{2,6},{6,2},{3,7},{7,3},{8,12},{12,8},{9,1... | collective-permute-start | bytes 1572872 | tf_op jit(solution)/shard_map/ppermute | solution.py:321
  0.5 0.1 collective-permute-start.2
  0.5 1.4 %shard_map.73 = (bf16[192,128]{1,0:T(8,128)(2,1)S(1)}, f32[2,1024]{1,0:T(2,128)S(1)}, bf16[4,1024]{1,0:T(4,128)(2,1)S(1)}, bf16[1024,256]{1,0:T(8,128)(2,1)S(1)}...) custom-call(s32[1,16]{1,0:T(1,128)} %bitcast.12, ...), custom_call_target="tpu_custom_call" | custom-call | tf_op jit(solution)/shard_map/pallas_call | solution.py:300
  1.9 3.0 %collective-permute-start = (bf16[192,128]{1,0:T(8,128)(2,1)S(1)}, bf16[192,128]{1,0:T(8,128)(2,1)S(1)}, u32[]{:S(2)}, u32[]{:S(2)}) collective-permute-start(bf16[192,128]{1,0:T(8,128)(2,1)S(1)} %get-tuple-element.21), channel_id=1, source_target_pairs={{0,8},{8,0},{16,24},{24,16},{1,9},{9,1},{17,25},{25,17},{2,10},{10... | collective-permute-start | bytes 147464 | tf_op jit(solution)/shard_map/ppermute | solution.py:24
  5.0 1.5 %collective-permute-start.5 = (bf16[192,128]{1,0:T(8,128)(2,1)S(1)}, bf16[192,128]{1,0:T(8,128)(2,1)S(1)}, u32[]{:S(2)}, u32[]{:S(2)}) collective-permute-start(bf16[192,128]{1,0:T(8,128)(2,1)S(1)} %get-tuple-element.27), channel_id=1, source_target_pairs={{0,16},{8,24},{16,0},{24,8},{1,17},{9,25},{17,1},{25,9},{2,18},{10... | collective-permute-start | bytes 147464 | tf_op jit(solution)/shard_map/ppermute | solution.py:24
  6.5 1.1 %collective-permute-start.6 = (bf16[192,128]{1,0:T(8,128)(2,1)S(1)}, bf16[192,128]{1,0:T(8,128)(2,1)S(1)}, u32[]{:S(2)}, u32[]{:S(2)}) collective-permute-start(bf16[192,128]{1,0:T(8,128)(2,1)S(1)} %get-tuple-element.28), channel_id=1, source_target_pairs={{0,24},{8,16},{16,8},{24,0},{1,25},{9,17},{17,9},{25,1},{2,26},{10... | collective-permute-start | bytes 147464 | tf_op jit(solution)/shard_map/ppermute | solution.py:24
  7.6 1.6 %shard_map.74 = (bf16[192,128]{1,0:T(8,128)(2,1)S(1)}, bf16[192,128]{1,0:T(8,128)(2,1)S(1)}) custom-call(f32[2,1024]{1,0:T(2,128)S(1)} %get-tuple-element.19.shift_ref, bf16[192,128]{1,0:T(8,128)(2,1)S(1)} %get-tuple-element.20.refs_0_, bf16[192,128]{1,0:T(8,128)(2,1)S(1)} %collective-permute-done.refs_1_, bf16[1024,256]{1,0:T(8,128)(2,1)S(1)} %get-tuple-element.22.refs_2_, ...), custom_call_target="tpu_custom_call" | custom-call | flops 402653184 | bytes 2097152 | tf_op jit(solution)/shard_map/pallas_call | solution.py:327
  9.2 1.6 %collective-permute-start.4 = (bf16[192,128]{1,0:T(8,128)(2,1)S(1)}, bf16[192,128]{1,0:T(8,128)(2,1)S(1)}, u32[]{:S(2)}, u32[]{:S(2)}) collective-permute-start(bf16[192,128]{1,0:T(8,128)(2,1)S(1)} %get-tuple-element.26), channel_id=1, source_target_pairs={{8,0},{0,8},{24,16},{16,24},{9,1},{1,9},{25,17},{17,25},{10,2},{2,... | collective-permute-start | bytes 147464 | tf_op jit(solution)/shard_map/ppermute | solution.py:29
  10.8 0.7 %collective-permute-done.6.refs_1_ = bf16[192,128]{1,0:T(8,128)(2,1)S(1)} collective-permute-done((bf16[192,128]{1,0:T(8,128)(2,1)S(1)}, bf16[192,128]{1,0:T(8,128)(2,1)S(1)}, u32[]{:S(2)}, u32[]{:S(2)}) %collective-permute-start.6) | collective-permute-done | bytes 49184 | tf_op jit(solution)/shard_map/ppermute | solution.py:24
  11.5 1.6 %shard_map.75 = (bf16[192,128]{1,0:T(8,128)(2,1)S(1)}, bf16[192,128]{1,0:T(8,128)(2,1)S(1)}) custom-call(f32[2,1024]{1,0:T(2,128)S(1)} %get-tuple-element.19.shift_ref, bf16[192,128]{1,0:T(8,128)(2,1)S(1)} %collective-permute-done.5.refs_0_, bf16[192,128]{1,0:T(8,128)(2,1)S(1)} %collective-permute-done.6.refs_1_, ...), custom_call_target="tpu_custom_call" | custom-call | flops 402653184 | bytes 2097152 | tf_op jit(solution)/shard_map/pallas_call | solution.py:327
  13.1 1.2 %collective-permute-start.7 = (bf16[192,128]{1,0:T(8,128)(2,1)S(1)}, bf16[192,128]{1,0:T(8,128)(2,1)S(1)}, u32[]{:S(2)}, u32[]{:S(2)}) collective-permute-start(bf16[192,128]{1,0:T(8,128)(2,1)S(1)} %get-tuple-element.29), channel_id=1, source_target_pairs={{16,0},{24,8},{0,16},{8,24},{17,1},{25,9},{1,17},{9,25},{18,2},{26... | collective-permute-start | bytes 147464 | tf_op jit(solution)/shard_map/ppermute | solution.py:29
  14.3 0.8 %collective-permute-start.8 = (bf16[192,128]{1,0:T(8,128)(2,1)S(1)}, bf16[192,128]{1,0:T(8,128)(2,1)S(1)}, u32[]{:S(2)}, u32[]{:S(2)}) collective-permute-start(bf16[192,128]{1,0:T(8,128)(2,1)S(1)} %get-tuple-element.30), channel_id=1, source_target_pairs={{24,0},{16,8},{8,16},{0,24},{25,1},{17,9},{9,17},{1,25},{26,2},{18... | collective-permute-start | bytes 147464 | tf_op jit(solution)/shard_map/ppermute | solution.py:29
  15.1 2.4 %collective-permute-done.7.refs_2_ = bf16[192,128]{1,0:T(8,128)(2,1)S(1)} collective-permute-done((bf16[192,128]{1,0:T(8,128)(2,1)S(1)}, bf16[192,128]{1,0:T(8,128)(2,1)S(1)}, u32[]{:S(2)}, u32[]{:S(2)}) %collective-permute-start.7) | collective-permute-done | bytes 49184 | tf_op jit(solution)/shard_map/ppermute | solution.py:29
  17.6 1.7 %collective-permute-done.8.refs_3_ = bf16[192,128]{1,0:T(8,128)(2,1)S(1)} collective-permute-done((bf16[192,128]{1,0:T(8,128)(2,1)S(1)}, bf16[192,128]{1,0:T(8,128)(2,1)S(1)}, u32[]{:S(2)}, u32[]{:S(2)}) %collective-permute-start.8) | collective-permute-done | bytes 49184 | tf_op jit(solution)/shard_map/ppermute | solution.py:29
  19.3 0.2 shard_map.76.refs_0_
  19.5 3.7 %collective-permute-start.11 = (bf16[16,4096]{1,0:T(8,128)(2,1)S(1)}, bf16[16,4096]{1,0:T(8,128)(2,1)S(1)}, u32[]{:S(2)}, u32[]{:S(2)}) collective-permute-start(bf16[16,4096]{1,0:T(8,128)(2,1)S(1)} %shard_map.76.refs_0_), channel_id=1, source_target_pairs={{3,0},{2,1},{1,2},{0,3},{7,4},{6,5},{5,6},{4,7},{11,8},{10,9},{9,1... | collective-permute-start | bytes 393224 | tf_op jit(solution)/shard_map/ppermute | solution.py:29
  23.2 1.9 %collective-permute-start.10 = (bf16[16,4096]{1,0:T(8,128)(2,1)S(1)}, bf16[16,4096]{1,0:T(8,128)(2,1)S(1)}, u32[]{:S(2)}, u32[]{:S(2)}) collective-permute-start(bf16[16,4096]{1,0:T(8,128)(2,1)S(1)} %shard_map.76.refs_0_), channel_id=1, source_target_pairs={{0,2},{1,3},{2,0},{3,1},{8,10},{9,11},{10,8},{11,9},{16,18},{17,19... | collective-permute-start | bytes 393224 | tf_op jit(solution)/shard_map/ppermute | solution.py:377
  25.1 0.8 %collective-permute-start.9 = (bf16[16,4096]{1,0:T(8,128)(2,1)S(1)}, bf16[16,4096]{1,0:T(8,128)(2,1)S(1)}, u32[]{:S(2)}, u32[]{:S(2)}) collective-permute-start(bf16[16,4096]{1,0:T(8,128)(2,1)S(1)} %shard_map.76.refs_0_), channel_id=1, source_target_pairs={{1,0},{0,1},{3,2},{2,3},{5,4},{4,5},{7,6},{6,7},{9,8},{8,9},{11,10... | collective-permute-start | bytes 393224 | tf_op jit(solution)/shard_map/ppermute | solution.py:29
  25.9 0.6 %collective-permute-done.11.refs_1_ = bf16[16,4096]{1,0:T(8,128)(2,1)S(1)} collective-permute-done((bf16[16,4096]{1,0:T(8,128)(2,1)S(1)}, bf16[16,4096]{1,0:T(8,128)(2,1)S(1)}, u32[]{:S(2)}, u32[]{:S(2)}) %collective-permute-start.11) | collective-permute-done | bytes 131104 | tf_op jit(solution)/shard_map/ppermute | solution.py:29
  26.5 0.7 %collective-permute-start.12 = (bf16[16,4096]{1,0:T(8,128)(2,1)S(1)}, bf16[16,4096]{1,0:T(8,128)(2,1)S(1)}, u32[]{:S(2)}, u32[]{:S(2)}) collective-permute-start(bf16[16,4096]{1,0:T(8,128)(2,1)S(1)} %collective-permute-done.11.refs_1_), channel_id=1, source_target_pairs={{4,5},{5,4},{6,7},{7,6},{12,13},{13,12},{14,15},{15,14},{20,21},{2... | collective-permute-start | bytes 393224 | tf_op jit(solution)/shard_map/ppermute | solution.py:377
  27.2 0.7 %shard_map.77.refs_3_ = bf16[16,16384]{1,0:T(8,128)(2,1)} custom-call(bf16[16,4096]{1,0:T(8,128)(2,1)S(1)} %shard_map.76.refs_0_, bf16[16,4096]{1,0:T(8,128)(2,1)S(1)} %collective-permute-done.11.refs_1_), custom_call_target="tpu_custom_call" | custom-call | tf_op jit(solution)/shard_map/pallas_call | solution.py:347
  27.9 3.7 %collective-permute-done.10.refs_1_ = bf16[16,4096]{1,0:T(8,128)(2,1)S(1)} collective-permute-done((bf16[16,4096]{1,0:T(8,128)(2,1)S(1)}, bf16[16,4096]{1,0:T(8,128)(2,1)S(1)}, u32[]{:S(2)}, u32[]{:S(2)}) %collective-permute-start.10) | collective-permute-done | bytes 131104 | tf_op jit(solution)/shard_map/ppermute | solution.py:377
  31.6 0.1 collective-permute-done.9.refs_0_
  31.7 0.7 %shard_map.78 = bf16[16,16384]{1,0:T(8,128)(2,1)} custom-call(bf16[16,4096]{1,0:T(8,128)(2,1)S(1)} %collective-permute-done.9.refs_0_, bf16[16,4096]{1,0:T(8,128)(2,1)S(1)} %collective-permute-done.10.refs_1_, bf16[16,4096]{1,0:T(8,128)(2,1)S(1)} %collective-permute-done.12.refs_2_, bf16[16,16384]{1,0:T(8,128)(2,1)} %shard_map.77.refs_3_), custom_call_target="tpu_custom_call", output_to_operand_aliasing={{}: (3, {})} | custom-call | tf_op jit(solution)/shard_map/pallas_call | solution.py:347
  (8 shorter events, 0.0 us)
Async XLA Ops:
  0.0 7.6 %collective-permute-start.1 = (bf16[1024,256]{1,0:T(8,128)(2,1)}, bf16[1024,256]{1,0:T(8,128)(2,1)S(1)}, u32[]{:S(2)}, u32[]{:S(2)}) collective-permute-start(bf16[1024,256]{1,0:T(8,128)(2,1)} %bitcast.6), channel_id=1, source_target_pairs={{0,4},{4,0},{1,5},{5,1},{2,6},{6,2},{3,7},{7,3},{8,12},{12,8},{9,1... | collective-permute-start | bytes 1572872 | tf_op jit(solution)/shard_map/ppermute | solution.py:321
  0.5 7.2 %collective-permute-start.2 = (bf16[1024,256]{1,0:T(8,128)(2,1)}, bf16[1024,256]{1,0:T(8,128)(2,1)S(1)}, u32[]{:S(2)}, u32[]{:S(2)}) collective-permute-start(bf16[1024,256]{1,0:T(8,128)(2,1)} %bitcast.8), channel_id=1, source_target_pairs={{0,4},{4,0},{1,5},{5,1},{2,6},{6,2},{3,7},{7,3},{8,12},{12,8},{9,1... | collective-permute-start | bytes 1572872 | tf_op jit(solution)/shard_map/ppermute | solution.py:321
  1.9 5.7 %collective-permute-start = (bf16[192,128]{1,0:T(8,128)(2,1)S(1)}, bf16[192,128]{1,0:T(8,128)(2,1)S(1)}, u32[]{:S(2)}, u32[]{:S(2)}) collective-permute-start(bf16[192,128]{1,0:T(8,128)(2,1)S(1)} %get-tuple-element.21), channel_id=1, source_target_pairs={{0,8},{8,0},{16,24},{24,16},{1,9},{9,1},{17,25},{25,17},{2,10},{10... | collective-permute-start | bytes 147464 | tf_op jit(solution)/shard_map/ppermute | solution.py:24
  4.9 1.5 %collective-permute-start.3 = (bf16[4,1024]{1,0:T(4,128)(2,1)S(1)}, bf16[4,1024]{1,0:T(4,128)(2,1)S(1)}, u32[]{:S(2)}, u32[]{:S(2)}) collective-permute-start(bf16[4,1024]{1,0:T(4,128)(2,1)S(1)} %get-tuple-element.24.refs_4_), channel_id=1, source_target_pairs={{0,4},{4,0},{1,5},{5,1},{2,6},{6,2},{3,7},{7,3},{8,12},{12,8},{9,1... | collective-permute-start | bytes 24584 | tf_op jit(solution)/shard_map/ppermute | solution.py:321
  5.0 5.8 %collective-permute-start.5 = (bf16[192,128]{1,0:T(8,128)(2,1)S(1)}, bf16[192,128]{1,0:T(8,128)(2,1)S(1)}, u32[]{:S(2)}, u32[]{:S(2)}) collective-permute-start(bf16[192,128]{1,0:T(8,128)(2,1)S(1)} %get-tuple-element.27), channel_id=1, source_target_pairs={{0,16},{8,24},{16,0},{24,8},{1,17},{9,25},{17,1},{25,9},{2,18},{10... | collective-permute-start | bytes 147464 | tf_op jit(solution)/shard_map/ppermute | solution.py:24
  6.5 5.0 %collective-permute-start.6 = (bf16[192,128]{1,0:T(8,128)(2,1)S(1)}, bf16[192,128]{1,0:T(8,128)(2,1)S(1)}, u32[]{:S(2)}, u32[]{:S(2)}) collective-permute-start(bf16[192,128]{1,0:T(8,128)(2,1)S(1)} %get-tuple-element.28), channel_id=1, source_target_pairs={{0,24},{8,16},{16,8},{24,0},{1,25},{9,17},{17,9},{25,1},{2,26},{10... | collective-permute-start | bytes 147464 | tf_op jit(solution)/shard_map/ppermute | solution.py:24
  9.2 5.9 %collective-permute-start.4 = (bf16[192,128]{1,0:T(8,128)(2,1)S(1)}, bf16[192,128]{1,0:T(8,128)(2,1)S(1)}, u32[]{:S(2)}, u32[]{:S(2)}) collective-permute-start(bf16[192,128]{1,0:T(8,128)(2,1)S(1)} %get-tuple-element.26), channel_id=1, source_target_pairs={{8,0},{0,8},{24,16},{16,24},{9,1},{1,9},{25,17},{17,25},{10,2},{2,... | collective-permute-start | bytes 147464 | tf_op jit(solution)/shard_map/ppermute | solution.py:29
  13.1 4.5 %collective-permute-start.7 = (bf16[192,128]{1,0:T(8,128)(2,1)S(1)}, bf16[192,128]{1,0:T(8,128)(2,1)S(1)}, u32[]{:S(2)}, u32[]{:S(2)}) collective-permute-start(bf16[192,128]{1,0:T(8,128)(2,1)S(1)} %get-tuple-element.29), channel_id=1, source_target_pairs={{16,0},{24,8},{0,16},{8,24},{17,1},{25,9},{1,17},{9,25},{18,2},{26... | collective-permute-start | bytes 147464 | tf_op jit(solution)/shard_map/ppermute | solution.py:29
  14.3 5.0 %collective-permute-start.8 = (bf16[192,128]{1,0:T(8,128)(2,1)S(1)}, bf16[192,128]{1,0:T(8,128)(2,1)S(1)}, u32[]{:S(2)}, u32[]{:S(2)}) collective-permute-start(bf16[192,128]{1,0:T(8,128)(2,1)S(1)} %get-tuple-element.30), channel_id=1, source_target_pairs={{24,0},{16,8},{8,16},{0,24},{25,1},{17,9},{9,17},{1,25},{26,2},{18... | collective-permute-start | bytes 147464 | tf_op jit(solution)/shard_map/ppermute | solution.py:29
  19.5 7.0 %collective-permute-start.11 = (bf16[16,4096]{1,0:T(8,128)(2,1)S(1)}, bf16[16,4096]{1,0:T(8,128)(2,1)S(1)}, u32[]{:S(2)}, u32[]{:S(2)}) collective-permute-start(bf16[16,4096]{1,0:T(8,128)(2,1)S(1)} %shard_map.76.refs_0_), channel_id=1, source_target_pairs={{3,0},{2,1},{1,2},{0,3},{7,4},{6,5},{5,6},{4,7},{11,8},{10,9},{9,1... | collective-permute-start | bytes 393224 | tf_op jit(solution)/shard_map/ppermute | solution.py:29
  23.2 8.4 %collective-permute-start.10 = (bf16[16,4096]{1,0:T(8,128)(2,1)S(1)}, bf16[16,4096]{1,0:T(8,128)(2,1)S(1)}, u32[]{:S(2)}, u32[]{:S(2)}) collective-permute-start(bf16[16,4096]{1,0:T(8,128)(2,1)S(1)} %shard_map.76.refs_0_), channel_id=1, source_target_pairs={{0,2},{1,3},{2,0},{3,1},{8,10},{9,11},{10,8},{11,9},{16,18},{17,19... | collective-permute-start | bytes 393224 | tf_op jit(solution)/shard_map/ppermute | solution.py:377
  25.1 6.6 %collective-permute-start.9 = (bf16[16,4096]{1,0:T(8,128)(2,1)S(1)}, bf16[16,4096]{1,0:T(8,128)(2,1)S(1)}, u32[]{:S(2)}, u32[]{:S(2)}) collective-permute-start(bf16[16,4096]{1,0:T(8,128)(2,1)S(1)} %shard_map.76.refs_0_), channel_id=1, source_target_pairs={{1,0},{0,1},{3,2},{2,3},{5,4},{4,5},{7,6},{6,7},{9,8},{8,9},{11,10... | collective-permute-start | bytes 393224 | tf_op jit(solution)/shard_map/ppermute | solution.py:29
  26.5 5.2 %collective-permute-start.12 = (bf16[16,4096]{1,0:T(8,128)(2,1)S(1)}, bf16[16,4096]{1,0:T(8,128)(2,1)S(1)}, u32[]{:S(2)}, u32[]{:S(2)}) collective-permute-start(bf16[16,4096]{1,0:T(8,128)(2,1)S(1)} %collective-permute-done.11.refs_1_), channel_id=1, source_target_pairs={{4,5},{5,4},{6,7},{7,6},{12,13},{13,12},{14,15},{15,14},{20,21},{2... | collective-permute-start | bytes 393224 | tf_op jit(solution)/shard_map/ppermute | solution.py:377

commit v3 on v2

--- a/solution.py
+++ b/solution.py
@@ -81,23 +81,22 @@
     value_scale_hbm,
     placing_ref,
     shift_ref,
-    scales_ref,
-    key_ref,
-    value_ref,
+    cache_ref,
     *refs,
 ):
     out_refs, (doc_ref, length_ref, query_ref, key_scale_ref, value_scale_ref, sems) = (
         refs[:n_doc],
         refs[n_doc:],
     )
+    shard_len, span = key_hbm.shape
     pairs = (
         (doc_hbm, doc_ref),
         (query_hbm, query_ref),
         (length_hbm, length_ref),
         (key_scale_hbm, key_scale_ref),
         (value_scale_hbm, value_scale_ref),
-        (key_hbm, key_ref),
-        (value_hbm, value_ref),
+        (key_hbm, cache_ref.at[pl.ds(0, shard_len)]),
+        (value_hbm, cache_ref.at[pl.ds(shard_len, shard_len)]),
     )
     copies = [
         pltpu.make_async_copy(source, target, sems.at[at])
@@ -134,15 +133,20 @@
             out_refs[k][g * block : (g + 1) * block, :] = placed[k * block : (k + 1) * block]
     for copy in copies[2:5]:
         copy.wait()
-    scales_ref[...] = jnp.concatenate(
-        [key_scale_ref[...].astype(jnp.float32), value_scale_ref[...].astype(jnp.float32)], axis=0
-    ).astype(jnp.bfloat16)
+    scale_rows = []
+    for scale_ref in (key_scale_ref, value_scale_ref):
+        scales = scale_ref[...].astype(jnp.float32)
+        scale_rows += [
+            scales[row : row + 1, at : at + span]
+            for row in range(scales.shape[0])
+            for at in range(0, shard_len, span)
+        ]
+    cache_ref[2 * shard_len :, :] = jnp.concatenate(scale_rows, axis=0).astype(jnp.bfloat16)
     lengths = length_ref[...]
     lane = lax.broadcasted_iota(jnp.int32, lengths.shape, 1)
     length = jnp.sum(
         jnp.where(lane == lax.axis_index("doc"), lengths, 0), axis=1, keepdims=True
     )
-    shard_len = key_ref.shape[0]
     step = lax.broadcasted_iota(jnp.int32, shift_ref.shape, 0)
     anchor = (lax.axis_index("ctx") - step + n_ctx) % n_ctx
     position = lax.broadcasted_iota(jnp.int32, shift_ref.shape, 1) + anchor * shard_len
@@ -172,7 +176,16 @@
 
 def attend_kernel(sources, n_ctx, kv_dev, shift_ref, *refs):
     query_refs, refs = refs[:sources], refs[sources:]
-    cache_refs, out_refs = refs[: 3 * n_ctx], refs[3 * n_ctx :]
+    cache_refs, out_refs = refs[:n_ctx], refs[n_ctx:]
+    shard_len = shift_ref.shape[1]
+    span = kv_dev * HEAD_WIDTH
+    pieces = shard_len // span
+
+    def scale_row(scales, row):
+        return jnp.concatenate(
+            [scales[row * pieces + at : row * pieces + at + 1, :] for at in range(pieces)], axis=1
+        )
+
     rows_doc = query_refs[0].shape[0] // kv_dev
     signs = sign_matrix()
     scale = 1.0 / math.sqrt(HEAD_WIDTH)
@@ -183,16 +196,14 @@
     states = [None] * kv_dev
     for first in range(0, n_ctx, 2):
         steps = range(first, min(first + 2, n_ctx))
+        scales = {step: cache_refs[step][2 * shard_len :, :].astype(jnp.float32) for step in steps}
         scores = {}
         for g in groups:
             for step in steps:
-                key_ref, scales_ref = cache_refs[3 * step], cache_refs[3 * step + 2]
-                key_scale = scales_ref[g : g + 1, :].astype(jnp.float32) * (
-                    scale * math.log2(math.e)
-                )
+                key_scale = scale_row(scales[step], g) * (scale * math.log2(math.e))
                 product = lax.dot_general(
                     rows[g],
-                    key_ref[:, heads[g]],
+                    cache_refs[step][:shard_len, heads[g]],
                     (((1,), (1,)), ((), ())),
                     preferred_element_type=jnp.float32,
                 )
@@ -206,13 +217,14 @@
         for g in groups:
             all_probs, summed = 0.0, 0.0
             for step in steps:
-                value_ref, scales_ref = cache_refs[3 * step + 1], cache_refs[3 * step + 2]
-                value_scale = scales_ref[kv_dev + g : kv_dev + g + 1, :].astype(jnp.float32)
+                value_scale = scale_row(scales[step], kv_dev + g)
                 probs = jnp.exp2(scores[g, step] - tops[g])
                 all_probs = all_probs + probs
                 weights = (probs * value_scale).astype(jnp.bfloat16)
                 summed = summed + jnp.dot(
-                    weights, value_ref[:, heads[g]], preferred_element_type=jnp.float32
+                    weights,
+                    cache_refs[step][shard_len : 2 * shard_len, heads[g]],
+                    preferred_element_type=jnp.float32,
                 )
             total = jnp.sum(all_probs, axis=-1, keepdims=True)
             if states[g] is not None:
@@ -238,12 +250,13 @@
     me, parity = lax.axis_index("head"), lax.rem(lax.axis_index("ctx"), 2)
     width = block_refs[0].shape[1]
     copies = []
-    for at, (step, wanted) in enumerate(places):
+    for at, (even, odd) in enumerate(places):
+        step = jnp.where(parity == 0, even or 0, odd or 0)
         column = pl.multiple_of(peer_of_traced(me, step, n_head) * width, width)
         copy = pltpu.make_async_copy(
             block_refs[at], out_ref.at[:, pl.ds(column, width)], sems.at[at]
         )
-        copies.append((copy, wanted))
+        copies.append((copy, 1 if even is None else 0 if odd is None else None))
     for copy, wanted in copies:
         if wanted is None:
             copy.start()
@@ -297,37 +310,37 @@
     placing_block = jax.ShapeDtypeStruct((n_doc * (LANES // rows_home) * cap, LANES), jnp.bfloat16)
     hbm = pl.BlockSpec(memory_space=pltpu.HBM)
     anywhere = pl.BlockSpec(memory_space=pl.ANY)
-    placing, shift, scales, own_key, own_value, *outgoing = pl.pallas_call(
+    cache_rows = 2 * shard_len + 2 * shard_len // HEAD_WIDTH
+    placing, shift, own_cache, *outgoing = pl.pallas_call(
         functools.partial(dispatch_kernel, n_doc, n_ctx, cap),
         out_shape=[
             placing_block,
             jax.ShapeDtypeStruct((n_ctx, shard_len), jnp.float32),
-            jax.ShapeDtypeStruct((2 * kv_dev, shard_len), jnp.bfloat16),
-            jax.ShapeDtypeStruct(key_block.shape, key_block.dtype),
-            jax.ShapeDtypeStruct(value_block.shape, value_block.dtype),
+            jax.ShapeDtypeStruct((cache_rows, kv_dev * HEAD_WIDTH), key_block.dtype),
         ]
         + [slot_block] * n_doc,
         in_specs=[hbm] * len(args),
-        out_specs=[vmem] * (n_doc + 5),
+        out_specs=[vmem] * (n_doc + 3),
         scratch_shapes=[
             pltpu.VMEM(args[at].shape, args[at].dtype) for at in (0, 1, 2, 5, 6)
         ]
         + [pltpu.SemaphoreType.DMA((len(args),))],
         compiler_params=params,
     )(*[pltpu.with_memory_space_constraint(arg, pltpu.HBM) for arg in args])
-    cache = [own_key, own_value, scales]
+    cache = [own_cache]
     for step in range(1, n_ctx):
-        pairs = [(i, (i + step) % n_ctx) for i in range(n_ctx)]
-        cache += [lax.ppermute(part, "ctx", pairs) for part in (key_block, value_block, scales)]
+        cache.append(
+            lax.ppermute(own_cache, "ctx", [(i, (i + step) % n_ctx) for i in range(n_ctx)])
+        )
     arrived = [outgoing[0]] + [sent(outgoing[k], "doc", k) for k in range(1, n_doc)]
 
-    def attended_for(steps):
+    def attended_for(steps, shift):
         sources = [arrived[k] for k in steps]
         rows = len(sources) * slots
         return pl.pallas_call(
             functools.partial(attend_kernel, len(sources), n_ctx, kv_dev),
             out_shape=[slot_block] * len(sources),
-            in_specs=[vmem] * (1 + len(sources) + 3 * n_ctx),
+            in_specs=[vmem] * (1 + len(sources) + n_ctx),
             out_specs=[vmem] * len(sources),
             compiler_params=params,
             cost_estimate=pl.CostEstimate(
@@ -340,7 +353,8 @@
     half = max(1, n_doc // 2)
     finished = []
     for first in range(0, n_doc, half):
-        finished += attended_for(range(first, min(first + half, n_doc)))
+        finished += attended_for(range(first, min(first + half, n_doc)), shift)
+        finished[0], shift = lax.optimization_barrier((finished[0], shift))
     back = [finished[0]] + [returned(finished[k], "doc", k) for k in range(1, n_doc)]
 
     def assembled(pieces, before):
@@ -364,24 +378,27 @@
 
     if n_head != 4:
         return assembled(
-            [((0, None), mine)]
-            + [((step, None), returned(mine, "head", step)) for step in range(1, n_head)],
+            [((0, 0), mine)]
+            + [((step, step), returned(mine, "head", step)) for step in range(1, n_head)],
             (),
         )
-    devices = [(c, h) for c in range(n_ctx) for h in range(n_head)]
-
-    def swapped(value, step, parity):
-        pairs = [
-            (c * n_head + h, c * n_head + (h ^ step)) for c, h in devices if c % 2 == parity
-        ]
+
+    def swapped(value, even, odd):
+        pairs = []
+        for c in range(n_ctx):
+            step = odd if c % 2 else even
+            if step is not None:
+                pairs += [(c * n_head + h, c * n_head + (h ^ step)) for h in range(n_head)]
         return lax.ppermute(value, ("ctx", "head"), pairs)
 
-    mirror = returned(mine, "head", 3)
-    near = returned(mine, "head", 1)
-    second = swapped(mine, 2, 0)
-    passed = swapped(mirror, 1, 1)
-    attended = assembled([((0, None), mine), ((3, None), mirror)], ())
-    return assembled([((1, None), near), ((2, 0), second), ((2, 1), passed)], (attended,))
+    first = swapped(mine, 3, 3)
+    second = swapped(mine, 1, 1)
+    third = swapped(mine, 2, None)
+    passed = swapped(first, None, 1)
+    attended = assembled([((0, 0), mine), ((3, 3), first)], ())
+    return assembled(
+        [((2, None), third), ((1, 1), second), ((None, 2), passed)], (attended,)
+    )
 
 
 def solution(mesh):

time: 32.6 us -> 31.4 us (0.963)
  starting transfers between devices: 16.9 us -> 15.2 us
  waiting for transfers between devices: 9.2 us -> 9.66 us
    ppermute x5 -> x3, starting transfers between devices: 8.12 us -> 3.55 us  [returned(): lax.ppermute(value, axis, [(peer_of(i, step, count), i) for i in range(co...]
    ppermute x2 -> x4, starting transfers between devices: 2.57 us -> 7.01 us  [swapped(): return lax.ppermute(value, ('ctx', 'head'), pairs)]
    ppermute x3, waiting for transfers between devices: 0.69 us -> 3.36 us  [sent(): lax.ppermute(value, axis, [(i, peer_of(i, step, count)) for i in range(co...]
    ppermute x5 -> x3, waiting for transfers between devices: 4.82 us -> 2.6 us  [returned(): lax.ppermute(value, axis, [(peer_of(i, step, count), i) for i in range(co...]
    ppermute x3, starting transfers between devices: 5.66 us -> 4.11 us  [sent(): lax.ppermute(value, axis, [(i, peer_of(i, step, count)) for i in range(co...]
    ppermute x2 -> x4, waiting for transfers between devices: 3.68 us -> 3.69 us  [swapped(): return lax.ppermute(value, ('ctx', 'head'), pairs)]
  transfers between devices with their start and end apart: 13 -> 11, of which waited for: 6 -> 9; matrix products, arithmetic and copies ran while one was open for 0% -> 0% of each run, Pallas kernels for 16% -> 7%
where the time goes in v3:
time: 31.4 us; the launch traced here: 31.2 us
  starting transfers between devices  15.2 us (48%)
  waiting for transfers between devices  9.66 us (31%)
  Pallas kernels  6.3 us (20%)
    ppermute x4, starting transfers between devices, swapped(): return lax.ppermute(value, ('ctx', 'head'), pairs)  7.01 us
    ppermute x3, starting transfers between devices, sent(): lax.ppermute(value, axis, [(i, peer_of(i, step, count)) for i in range(co...  4.11 us
    ppermute x4, waiting for transfers between devices, swapped(): return lax.ppermute(value, ('ctx', 'head'), pairs)  3.69 us
    ppermute x3, starting transfers between devices, returned(): lax.ppermute(value, axis, [(peer_of(i, step, count), i) for i in range(co...  3.55 us
    ppermute x3, waiting for transfers between devices, sent(): lax.ppermute(value, axis, [(i, peer_of(i, step, count)) for i in range(co...  3.36 us
    pallas_call x2, Pallas kernels, attended_for(): pl.pallas_call(functools.partial(attend_kernel, len(sources), n_ctx, kv_d...  3.18 us
    ppermute x3, waiting for transfers between devices, returned(): lax.ppermute(value, axis, [(peer_of(i, step, count), i) for i in range(co...  2.6 us
    pallas_call x2, Pallas kernels, assembled(): pl.pallas_call(functools.partial(assemble_kernel, n_head, [place for plac...  1.45 us
  transfers between devices with their start and end apart: 11, of which 9 were waited for; matrix products, arithmetic and copies ran while one was open for 0% of the time, Pallas kernels for 7%

profile of v3, /device:TPU:0, one launch (start us, length us, event | category | flops | bytes accessed | tf_op | source)
XLA Modules:
  0.0 31.2 jit_solution(4981286772306565043)
XLA Ops:
  0.0 1.4 %shard_map.73 = (bf16[192,128]{1,0:T(8,128)(2,1)S(1)}, f32[2,1024]{1,0:T(2,128)S(1)}, bf16[2064,256]{1,0:T(8,128)(2,1)S(1)}, bf16[192,128]{1,0:T(8,128)(2,1)S(1)...) custom-call(s32[1,16]{1,0:T(1,128)} %bitcast.10, s32[1,4]{1,0:T(1,128)} %bitcast.11, ...), custom_call_target="tpu_custom_call" | custom-call | tf_op jit(solution)/shard_map/pallas_call | solution.py:314
  1.4 0.5 %collective-permute-start.1 = (bf16[2064,256]{1,0:T(8,128)(2,1)S(1)}, bf16[2064,256]{1,0:T(8,128)(2,1)S(1)}, u32[]{:S(2)}, u32[]{:S(2)}) collective-permute-start(bf16[2064,256]{1,0:T(8,128)(2,1)S(1)} %get-tuple-element.23.refs_2_), channel_id=1, source_target_pairs={{0,4},{4,0},{1,5},{5,1},{2,6},{6,2},{3,7},{7,3},{8,12},{12,8},{9,1... | collective-permute-start | bytes 3170312 | tf_op jit(solution)/shard_map/ppermute | solution.py:333
  2.0 2.6 %collective-permute-start = (bf16[192,128]{1,0:T(8,128)(2,1)S(1)}, bf16[192,128]{1,0:T(8,128)(2,1)S(1)}, u32[]{:S(2)}, u32[]{:S(2)}) collective-permute-start(bf16[192,128]{1,0:T(8,128)(2,1)S(1)} %get-tuple-element.22), channel_id=1, source_target_pairs={{0,8},{8,0},{16,24},{24,16},{1,9},{9,1},{17,25},{25,17},{2,10},{10... | collective-permute-start | bytes 147464 | tf_op jit(solution)/shard_map/ppermute | solution.py:24
  4.5 1.5 %collective-permute-start.3 = (bf16[192,128]{1,0:T(8,128)(2,1)S(1)}, bf16[192,128]{1,0:T(8,128)(2,1)S(1)}, u32[]{:S(2)}, u32[]{:S(2)}) collective-permute-start(bf16[192,128]{1,0:T(8,128)(2,1)S(1)} %get-tuple-element.28), channel_id=1, source_target_pairs={{0,16},{8,24},{16,0},{24,8},{1,17},{9,25},{17,1},{25,9},{2,18},{10... | collective-permute-start | bytes 147464 | tf_op jit(solution)/shard_map/ppermute | solution.py:24
  6.1 0.8 %collective-permute-done.refs_1_ = bf16[192,128]{1,0:T(8,128)(2,1)S(1)} collective-permute-done((bf16[192,128]{1,0:T(8,128)(2,1)S(1)}, bf16[192,128]{1,0:T(8,128)(2,1)S(1)}, u32[]{:S(2)}, u32[]{:S(2)}) %collective-permute-start) | collective-permute-done | bytes 49184 | tf_op jit(solution)/shard_map/ppermute | solution.py:24
  6.9 1.6 %shard_map.74 = (bf16[192,128]{1,0:T(8,128)(2,1)S(1)}, bf16[192,128]{1,0:T(8,128)(2,1)S(1)}) custom-call(f32[2,1024]{1,0:T(2,128)S(1)} %get-tuple-element.27.shift_ref, bf16[192,128]{1,0:T(8,128)(2,1)S(1)} %get-tuple-element.21.refs_0_, bf16[192,128]{1,0:T(8,128)(2,1)S(1)} %collective-permute-done.refs_1_, bf16[2064,256]{1,0:T(8,128)(2,1)S(1)} %get-tuple-element.23.refs_2_, ...), custom_call_target="tpu_custom_call" | custom-call | flops 402653184 | bytes 2097152 | tf_op jit(solution)/shard_map/pallas_call | solution.py:340
  8.5 0.2 collective-permute-done.3.refs_0_
  8.6 2.4 %collective-permute-done.4.refs_1_ = bf16[192,128]{1,0:T(8,128)(2,1)S(1)} collective-permute-done((bf16[192,128]{1,0:T(8,128)(2,1)S(1)}, bf16[192,128]{1,0:T(8,128)(2,1)S(1)}, u32[]{:S(2)}, u32[]{:S(2)}) %collective-permute-start.4) | collective-permute-done | bytes 49184 | tf_op jit(solution)/shard_map/ppermute | solution.py:24
  11.0 1.6 %shard_map.75 = (bf16[192,128]{1,0:T(8,128)(2,1)S(1)}, bf16[192,128]{1,0:T(8,128)(2,1)S(1)}) custom-call(f32[2,1024]{1,0:T(2,128)S(1)} %get-tuple-element.27.shift_ref, bf16[192,128]{1,0:T(8,128)(2,1)S(1)} %collective-permute-done.3.refs_0_, bf16[192,128]{1,0:T(8,128)(2,1)S(1)} %collective-permute-done.4.refs_1_, ...), custom_call_target="tpu_custom_call" | custom-call | flops 402653184 | bytes 2097152 | tf_op jit(solution)/shard_map/pallas_call | solution.py:340
  12.6 0.6 %collective-permute-start.5 = (bf16[192,128]{1,0:T(8,128)(2,1)S(1)}, bf16[192,128]{1,0:T(8,128)(2,1)S(1)}, u32[]{:S(2)}, u32[]{:S(2)}) collective-permute-start(bf16[192,128]{1,0:T(8,128)(2,1)S(1)} %get-tuple-element.30), channel_id=1, source_target_pairs={{16,0},{24,8},{0,16},{8,24},{17,1},{25,9},{1,17},{9,25},{18,2},{26... | collective-permute-start | bytes 147464 | tf_op jit(solution)/shard_map/ppermute | solution.py:29
  13.2 1.5 %collective-permute-start.6 = (bf16[192,128]{1,0:T(8,128)(2,1)S(1)}, bf16[192,128]{1,0:T(8,128)(2,1)S(1)}, u32[]{:S(2)}, u32[]{:S(2)}) collective-permute-start(bf16[192,128]{1,0:T(8,128)(2,1)S(1)} %get-tuple-element.31), channel_id=1, source_target_pairs={{24,0},{16,8},{8,16},{0,24},{25,1},{17,9},{9,17},{1,25},{26,2},{18... | collective-permute-start | bytes 147464 | tf_op jit(solution)/shard_map/ppermute | solution.py:29
  14.7 1.5 %collective-permute-start.2 = (bf16[192,128]{1,0:T(8,128)(2,1)S(1)}, bf16[192,128]{1,0:T(8,128)(2,1)S(1)}, u32[]{:S(2)}, u32[]{:S(2)}) collective-permute-start(bf16[192,128]{1,0:T(8,128)(2,1)S(1)} %get-tuple-element.26), channel_id=1, source_target_pairs={{8,0},{0,8},{24,16},{16,24},{9,1},{1,9},{25,17},{17,25},{10,2},{2,... | collective-permute-start | bytes 147464 | tf_op jit(solution)/shard_map/ppermute | solution.py:29
  16.2 0.6 %collective-permute-done.5.refs_2_ = bf16[192,128]{1,0:T(8,128)(2,1)S(1)} collective-permute-done((bf16[192,128]{1,0:T(8,128)(2,1)S(1)}, bf16[192,128]{1,0:T(8,128)(2,1)S(1)}, u32[]{:S(2)}, u32[]{:S(2)}) %collective-permute-start.5) | collective-permute-done | bytes 49184 | tf_op jit(solution)/shard_map/ppermute | solution.py:29
  16.8 1.4 %collective-permute-done.6.refs_3_ = bf16[192,128]{1,0:T(8,128)(2,1)S(1)} collective-permute-done((bf16[192,128]{1,0:T(8,128)(2,1)S(1)}, bf16[192,128]{1,0:T(8,128)(2,1)S(1)}, u32[]{:S(2)}, u32[]{:S(2)}) %collective-permute-start.6) | collective-permute-done | bytes 49184 | tf_op jit(solution)/shard_map/ppermute | solution.py:29
  18.2 0.6 %collective-permute-done.2.refs_1_ = bf16[192,128]{1,0:T(8,128)(2,1)S(1)} collective-permute-done((bf16[192,128]{1,0:T(8,128)(2,1)S(1)}, bf16[192,128]{1,0:T(8,128)(2,1)S(1)}, u32[]{:S(2)}, u32[]{:S(2)}) %collective-permute-start.2) | collective-permute-done | bytes 49184 | tf_op jit(solution)/shard_map/ppermute | solution.py:29
  18.8 0.2 shard_map.76.refs_0_
  19.0 3.7 %collective-permute-start.9 = (bf16[16,4096]{1,0:T(8,128)(2,1)S(1)}, bf16[16,4096]{1,0:T(8,128)(2,1)S(1)}, u32[]{:S(2)}, u32[]{:S(2)}) collective-permute-start(bf16[16,4096]{1,0:T(8,128)(2,1)S(1)} %shard_map.76.refs_0_), channel_id=1, source_target_pairs={{0,3},{1,2},{2,1},{3,0},{4,7},{5,6},{6,5},{7,4},{8,11},{9,10},{10,... | collective-permute-start | bytes 393224 | tf_op jit(solution)/shard_map/ppermute | solution.py:392
  22.7 2.7 %collective-permute-start.7 = (bf16[16,4096]{1,0:T(8,128)(2,1)S(1)}, bf16[16,4096]{1,0:T(8,128)(2,1)S(1)}, u32[]{:S(2)}, u32[]{:S(2)}) collective-permute-start(bf16[16,4096]{1,0:T(8,128)(2,1)S(1)} %shard_map.76.refs_0_), channel_id=1, source_target_pairs={{0,2},{1,3},{2,0},{3,1},{8,10},{9,11},{10,8},{11,9},{16,18},{17,19... | collective-permute-start | bytes 393224 | tf_op jit(solution)/shard_map/ppermute | solution.py:392
  25.4 0.6 %collective-permute-done.9.refs_1_ = bf16[16,4096]{1,0:T(8,128)(2,1)S(1)} collective-permute-done((bf16[16,4096]{1,0:T(8,128)(2,1)S(1)}, bf16[16,4096]{1,0:T(8,128)(2,1)S(1)}, u32[]{:S(2)}, u32[]{:S(2)}) %collective-permute-start.9) | collective-permute-done | bytes 131104 | tf_op jit(solution)/shard_map/ppermute | solution.py:392
  26.0 0.7 %collective-permute-start.10 = (bf16[16,4096]{1,0:T(8,128)(2,1)S(1)}, bf16[16,4096]{1,0:T(8,128)(2,1)S(1)}, u32[]{:S(2)}, u32[]{:S(2)}) collective-permute-start(bf16[16,4096]{1,0:T(8,128)(2,1)S(1)} %collective-permute-done.9.refs_1_), channel_id=1, source_target_pairs={{4,5},{5,4},{6,7},{7,6},{12,13},{13,12},{14,15},{15,14},{20,21},{2... | collective-permute-start | bytes 393224 | tf_op jit(solution)/shard_map/ppermute | solution.py:392
  26.6 0.7 %shard_map.77.refs_3_ = bf16[16,16384]{1,0:T(8,128)(2,1)} custom-call(bf16[16,4096]{1,0:T(8,128)(2,1)S(1)} %shard_map.76.refs_0_, bf16[16,4096]{1,0:T(8,128)(2,1)S(1)} %collective-permute-done.9.refs_1_), custom_call_target="tpu_custom_call" | custom-call | tf_op jit(solution)/shard_map/pallas_call | solution.py:361
  27.4 1.1 %collective-permute-done.8.refs_1_ = bf16[16,4096]{1,0:T(8,128)(2,1)S(1)} collective-permute-done((bf16[16,4096]{1,0:T(8,128)(2,1)S(1)}, bf16[16,4096]{1,0:T(8,128)(2,1)S(1)}, u32[]{:S(2)}, u32[]{:S(2)}) %collective-permute-start.8) | collective-permute-done | bytes 131104 | tf_op jit(solution)/shard_map/ppermute | solution.py:392
  28.4 2.1 %collective-permute-done.7.refs_0_ = bf16[16,4096]{1,0:T(8,128)(2,1)S(1)} collective-permute-done((bf16[16,4096]{1,0:T(8,128)(2,1)S(1)}, bf16[16,4096]{1,0:T(8,128)(2,1)S(1)}, u32[]{:S(2)}, u32[]{:S(2)}) %collective-permute-start.7) | collective-permute-done | bytes 131104 | tf_op jit(solution)/shard_map/ppermute | solution.py:392
  30.5 0.7 %shard_map.78 = bf16[16,16384]{1,0:T(8,128)(2,1)} custom-call(bf16[16,4096]{1,0:T(8,128)(2,1)S(1)} %collective-permute-done.7.refs_0_, bf16[16,4096]{1,0:T(8,128)(2,1)S(1)} %collective-permute-done.8.refs_1_, bf16[16,4096]{1,0:T(8,128)(2,1)S(1)} %collective-permute-done.10.refs_2_, bf16[16,16384]{1,0:T(8,128)(2,1)} %shard_map.77.refs_3_), custom_call_target="tpu_custom_call", output_to_operand_aliasing={{}: (3, {})} | custom-call | tf_op jit(solution)/shard_map/pallas_call | solution.py:361
  (4 shorter events, 0.0 us)
Async XLA Ops:
  1.4 5.4 %collective-permute-start.1 = (bf16[2064,256]{1,0:T(8,128)(2,1)S(1)}, bf16[2064,256]{1,0:T(8,128)(2,1)S(1)}, u32[]{:S(2)}, u32[]{:S(2)}) collective-permute-start(bf16[2064,256]{1,0:T(8,128)(2,1)S(1)} %get-tuple-element.23.refs_2_), channel_id=1, source_target_pairs={{0,4},{4,0},{1,5},{5,1},{2,6},{6,2},{3,7},{7,3},{8,12},{12,8},{9,1... | collective-permute-start | bytes 3170312 | tf_op jit(solution)/shard_map/ppermute | solution.py:333
  2.0 4.9 %collective-permute-start = (bf16[192,128]{1,0:T(8,128)(2,1)S(1)}, bf16[192,128]{1,0:T(8,128)(2,1)S(1)}, u32[]{:S(2)}, u32[]{:S(2)}) collective-permute-start(bf16[192,128]{1,0:T(8,128)(2,1)S(1)} %get-tuple-element.22), channel_id=1, source_target_pairs={{0,8},{8,0},{16,24},{24,16},{1,9},{9,1},{17,25},{25,17},{2,10},{10... | collective-permute-start | bytes 147464 | tf_op jit(solution)/shard_map/ppermute | solution.py:24
  4.5 4.1 %collective-permute-start.3 = (bf16[192,128]{1,0:T(8,128)(2,1)S(1)}, bf16[192,128]{1,0:T(8,128)(2,1)S(1)}, u32[]{:S(2)}, u32[]{:S(2)}) collective-permute-start(bf16[192,128]{1,0:T(8,128)(2,1)S(1)} %get-tuple-element.28), channel_id=1, source_target_pairs={{0,16},{8,24},{16,0},{24,8},{1,17},{9,25},{17,1},{25,9},{2,18},{10... | collective-permute-start | bytes 147464 | tf_op jit(solution)/shard_map/ppermute | solution.py:24
  6.0 5.0 %collective-permute-start.4 = (bf16[192,128]{1,0:T(8,128)(2,1)S(1)}, bf16[192,128]{1,0:T(8,128)(2,1)S(1)}, u32[]{:S(2)}, u32[]{:S(2)}) collective-permute-start(bf16[192,128]{1,0:T(8,128)(2,1)S(1)} %get-tuple-element.29), channel_id=1, source_target_pairs={{0,24},{8,16},{16,8},{24,0},{1,25},{9,17},{17,9},{25,1},{2,26},{10... | collective-permute-start | bytes 147464 | tf_op jit(solution)/shard_map/ppermute | solution.py:24
  12.6 4.2 %collective-permute-start.5 = (bf16[192,128]{1,0:T(8,128)(2,1)S(1)}, bf16[192,128]{1,0:T(8,128)(2,1)S(1)}, u32[]{:S(2)}, u32[]{:S(2)}) collective-permute-start(bf16[192,128]{1,0:T(8,128)(2,1)S(1)} %get-tuple-element.30), channel_id=1, source_target_pairs={{16,0},{24,8},{0,16},{8,24},{17,1},{25,9},{1,17},{9,25},{18,2},{26... | collective-permute-start | bytes 147464 | tf_op jit(solution)/shard_map/ppermute | solution.py:29
  13.2 5.0 %collective-permute-start.6 = (bf16[192,128]{1,0:T(8,128)(2,1)S(1)}, bf16[192,128]{1,0:T(8,128)(2,1)S(1)}, u32[]{:S(2)}, u32[]{:S(2)}) collective-permute-start(bf16[192,128]{1,0:T(8,128)(2,1)S(1)} %get-tuple-element.31), channel_id=1, source_target_pairs={{24,0},{16,8},{8,16},{0,24},{25,1},{17,9},{9,17},{1,25},{26,2},{18... | collective-permute-start | bytes 147464 | tf_op jit(solution)/shard_map/ppermute | solution.py:29
  14.7 4.1 %collective-permute-start.2 = (bf16[192,128]{1,0:T(8,128)(2,1)S(1)}, bf16[192,128]{1,0:T(8,128)(2,1)S(1)}, u32[]{:S(2)}, u32[]{:S(2)}) collective-permute-start(bf16[192,128]{1,0:T(8,128)(2,1)S(1)} %get-tuple-element.26), channel_id=1, source_target_pairs={{8,0},{0,8},{24,16},{16,24},{9,1},{1,9},{25,17},{17,25},{10,2},{2,... | collective-permute-start | bytes 147464 | tf_op jit(solution)/shard_map/ppermute | solution.py:29
  19.0 6.9 %collective-permute-start.9 = (bf16[16,4096]{1,0:T(8,128)(2,1)S(1)}, bf16[16,4096]{1,0:T(8,128)(2,1)S(1)}, u32[]{:S(2)}, u32[]{:S(2)}) collective-permute-start(bf16[16,4096]{1,0:T(8,128)(2,1)S(1)} %shard_map.76.refs_0_), channel_id=1, source_target_pairs={{0,3},{1,2},{2,1},{3,0},{4,7},{5,6},{6,5},{7,4},{8,11},{9,10},{10,... | collective-permute-start | bytes 393224 | tf_op jit(solution)/shard_map/ppermute | solution.py:392
  22.7 5.7 %collective-permute-start.8 = (bf16[16,4096]{1,0:T(8,128)(2,1)S(1)}, bf16[16,4096]{1,0:T(8,128)(2,1)S(1)}, u32[]{:S(2)}, u32[]{:S(2)}) collective-permute-start(bf16[16,4096]{1,0:T(8,128)(2,1)S(1)} %shard_map.76.refs_0_), channel_id=1, source_target_pairs={{0,1},{1,0},{2,3},{3,2},{4,5},{5,4},{6,7},{7,6},{8,9},{9,8},{10,11... | collective-permute-start | bytes 393224 | tf_op jit(solution)/shard_map/ppermute | solution.py:392
  22.7 7.8 %collective-permute-start.7 = (bf16[16,4096]{1,0:T(8,128)(2,1)S(1)}, bf16[16,4096]{1,0:T(8,128)(2,1)S(1)}, u32[]{:S(2)}, u32[]{:S(2)}) collective-permute-start(bf16[16,4096]{1,0:T(8,128)(2,1)S(1)} %shard_map.76.refs_0_), channel_id=1, source_target_pairs={{0,2},{1,3},{2,0},{3,1},{8,10},{9,11},{10,8},{11,9},{16,18},{17,19... | collective-permute-start | bytes 393224 | tf_op jit(solution)/shard_map/ppermute | solution.py:392
  26.0 4.5 %collective-permute-start.10 = (bf16[16,4096]{1,0:T(8,128)(2,1)S(1)}, bf16[16,4096]{1,0:T(8,128)(2,1)S(1)}, u32[]{:S(2)}, u32[]{:S(2)}) collective-permute-start(bf16[16,4096]{1,0:T(8,128)(2,1)S(1)} %collective-permute-done.9.refs_1_), channel_id=1, source_target_pairs={{4,5},{5,4},{6,7},{7,6},{12,13},{13,12},{14,15},{15,14},{20,21},{2... | collective-permute-start | bytes 393224 | tf_op jit(solution)/shard_map/ppermute | solution.py:392

commit v4 on v3

--- a/solution.py
+++ b/solution.py
@@ -80,7 +80,7 @@
     key_scale_hbm,
     value_scale_hbm,
     placing_ref,
-    shift_ref,
+    valid_ref,
     cache_ref,
     *refs,
 ):
@@ -147,10 +147,10 @@
     length = jnp.sum(
         jnp.where(lane == lax.axis_index("doc"), lengths, 0), axis=1, keepdims=True
     )
-    step = lax.broadcasted_iota(jnp.int32, shift_ref.shape, 0)
+    step = lax.broadcasted_iota(jnp.int32, valid_ref.shape, 0)
     anchor = (lax.axis_index("ctx") - step + n_ctx) % n_ctx
-    position = lax.broadcasted_iota(jnp.int32, shift_ref.shape, 1) + anchor * shard_len
-    shift_ref[...] = jnp.where(position < length, 0.0, -1e30)
+    position = lax.broadcasted_iota(jnp.int32, valid_ref.shape, 1) + anchor * shard_len
+    valid_ref[...] = jnp.where(position < length, 1.0, 0.0)
     for copy in copies[5:]:
         copy.wait()
 
@@ -174,10 +174,10 @@
             out_ref[:, at : at + HEAD_WIDTH] = mine[h * rows : (h + 1) * rows]
 
 
-def attend_kernel(sources, n_ctx, kv_dev, shift_ref, *refs):
+def attend_kernel(sources, n_ctx, kv_dev, valid_ref, *refs):
     query_refs, refs = refs[:sources], refs[sources:]
     cache_refs, out_refs = refs[:n_ctx], refs[n_ctx:]
-    shard_len = shift_ref.shape[1]
+    shard_len = valid_ref.shape[1]
     span = kv_dev * HEAD_WIDTH
     pieces = shard_len // span
 
@@ -197,6 +197,7 @@
     for first in range(0, n_ctx, 2):
         steps = range(first, min(first + 2, n_ctx))
         scales = {step: cache_refs[step][2 * shard_len :, :].astype(jnp.float32) for step in steps}
+        valid = {step: valid_ref[step : step + 1, :] > 0.0 for step in steps}
         scores = {}
         for g in groups:
             for step in steps:
@@ -207,7 +208,7 @@
                     (((1,), (1,)), ((), ())),
                     preferred_element_type=jnp.float32,
                 )
-                scores[g, step] = product * key_scale + shift_ref[step : step + 1, :]
+                scores[g, step] = jnp.where(valid[step], product * key_scale, -1e30)
         tops = []
         for g in groups:
             top = functools.reduce(
@@ -311,7 +312,7 @@
     hbm = pl.BlockSpec(memory_space=pltpu.HBM)
     anywhere = pl.BlockSpec(memory_space=pl.ANY)
     cache_rows = 2 * shard_len + 2 * shard_len // HEAD_WIDTH
-    placing, shift, own_cache, *outgoing = pl.pallas_call(
+    placing, valid, own_cache, *outgoing = pl.pallas_call(
         functools.partial(dispatch_kernel, n_doc, n_ctx, cap),
         out_shape=[
             placing_block,
@@ -334,7 +335,7 @@
         )
     arrived = [outgoing[0]] + [sent(outgoing[k], "doc", k) for k in range(1, n_doc)]
 
-    def attended_for(steps, shift):
+    def attended_for(steps, valid):
         sources = [arrived[k] for k in steps]
         rows = len(sources) * slots
         return pl.pallas_call(
@@ -348,13 +349,15 @@
                 bytes_accessed=4 * n_ctx * shard_len * kv_dev * HEAD_WIDTH,
                 transcendentals=rows * n_ctx * shard_len,
             ),
-        )(shift, *sources, *cache)
-
-    half = max(1, n_doc // 2)
-    finished = []
-    for first in range(0, n_doc, half):
-        finished += attended_for(range(first, min(first + half, n_doc)), shift)
-        finished[0], shift = lax.optimization_barrier((finished[0], shift))
+        )(valid, *sources, *cache)
+
+    finished = {}
+    for steps in (range(1, n_doc - 1), range(max(1, n_doc - 1), n_doc)):
+        if len(steps) > 0:
+            finished.update(zip(steps, attended_for(steps, valid)))
+    if n_doc > 1:
+        finished[n_doc - 1], valid = lax.optimization_barrier((finished[n_doc - 1], valid))
+    finished[0] = attended_for((0,), valid)[0]
     back = [finished[0]] + [returned(finished[k], "doc", k) for k in range(1, n_doc)]
 
     def assembled(pieces, before):

time: 31.4 us -> 30.6 us (0.975)
  waiting for transfers between devices: 9.66 us -> 7.92 us
  Pallas kernels: 6.3 us -> 6.93 us
    ppermute x3, waiting for transfers between devices: 3.36 us -> 1.7 us  [sent(): lax.ppermute(value, axis, [(i, peer_of(i, step, count)) for i in range(co...]
    pallas_call x2 -> x3, Pallas kernels: 3.18 us -> 3.81 us  [attended_for(): pl.pallas_call(functools.partial(attend_kernel, len(sources), n_ctx, kv_d...]
  transfers between devices with their start and end apart: 11 -> 11, of which waited for: 9 -> 6; matrix products, arithmetic and copies ran while one was open for 0% -> 0% of each run, Pallas kernels for 7% -> 15%
where the time goes in v4:
time: 30.6 us; the launch traced here: 30.4 us
  starting transfers between devices  15.5 us (51%)
  waiting for transfers between devices  7.92 us (26%)
  Pallas kernels  6.93 us (23%)
    ppermute x4, starting transfers between devices, swapped(): return lax.ppermute(value, ('ctx', 'head'), pairs)  7.01 us
    ppermute x3, starting transfers between devices, sent(): lax.ppermute(value, axis, [(i, peer_of(i, step, count)) for i in range(co...  4.16 us
    ppermute x3, starting transfers between devices, returned(): lax.ppermute(value, axis, [(peer_of(i, step, count), i) for i in range(co...  3.83 us
    pallas_call x3, Pallas kernels, attended_for(): pl.pallas_call(functools.partial(attend_kernel, len(sources), n_ctx, kv_d...  3.81 us
    ppermute x4, waiting for transfers between devices, swapped(): return lax.ppermute(value, ('ctx', 'head'), pairs)  3.67 us
    ppermute x3, waiting for transfers between devices, returned(): lax.ppermute(value, axis, [(peer_of(i, step, count), i) for i in range(co...  2.55 us
    ppermute x3, waiting for transfers between devices, sent(): lax.ppermute(value, axis, [(i, peer_of(i, step, count)) for i in range(co...  1.7 us
    pallas_call x2, Pallas kernels, assembled(): pl.pallas_call(functools.partial(assemble_kernel, n_head, [place for plac...  1.45 us
  transfers between devices with their start and end apart: 11, of which 6 were waited for; matrix products, arithmetic and copies ran while one was open for 0% of the time, Pallas kernels for 15%

profile of v4, /device:TPU:0, one launch (start us, length us, event | category | flops | bytes accessed | tf_op | source)
XLA Modules:
  0.0 30.4 jit_solution(4722690287785675297)
XLA Ops:
  0.0 1.4 %shard_map.73 = (bf16[192,128]{1,0:T(8,128)(2,1)S(1)}, f32[2,1024]{1,0:T(2,128)S(1)}, bf16[2064,256]{1,0:T(8,128)(2,1)S(1)}, bf16[192,128]{1,0:T(8,128)(2,1)S(1)...) custom-call(s32[1,16]{1,0:T(1,128)} %bitcast.10, s32[1,4]{1,0:T(1,128)} %bitcast.11, ...), custom_call_target="tpu_custom_call" | custom-call | tf_op jit(solution)/shard_map/pallas_call | solution.py:315
  1.4 0.5 %collective-permute-start.1 = (bf16[2064,256]{1,0:T(8,128)(2,1)S(1)}, bf16[2064,256]{1,0:T(8,128)(2,1)S(1)}, u32[]{:S(2)}, u32[]{:S(2)}) collective-permute-start(bf16[2064,256]{1,0:T(8,128)(2,1)S(1)} %get-tuple-element.19.refs_1_.refs_2_), channel_id=1, source_target_pairs={{0,4},{4,0},{1,5},{5,1},{2,6},{6,2},{3,7},{7,3},{8,12},{12,8},{9,1... | collective-permute-start | bytes 3170312 | tf_op jit(solution)/shard_map/ppermute | solution.py:334
  2.0 3.5 %collective-permute-start = (bf16[192,128]{1,0:T(8,128)(2,1)S(1)}, bf16[192,128]{1,0:T(8,128)(2,1)S(1)}, u32[]{:S(2)}, u32[]{:S(2)}) collective-permute-start(bf16[192,128]{1,0:T(8,128)(2,1)S(1)} %get-tuple-element.18), channel_id=1, source_target_pairs={{0,24},{8,16},{16,8},{24,0},{1,25},{9,17},{17,9},{25,1},{2,26},{10... | collective-permute-start | bytes 147464 | tf_op jit(solution)/shard_map/ppermute | solution.py:24
  5.5 0.5 %collective-permute-start.2 = (bf16[192,128]{1,0:T(8,128)(2,1)S(1)}, bf16[192,128]{1,0:T(8,128)(2,1)S(1)}, u32[]{:S(2)}, u32[]{:S(2)}) collective-permute-start(bf16[192,128]{1,0:T(8,128)(2,1)S(1)} %get-tuple-element.22), channel_id=1, source_target_pairs={{0,8},{8,0},{16,24},{24,16},{1,9},{9,1},{17,25},{25,17},{2,10},{10... | collective-permute-start | bytes 147464 | tf_op jit(solution)/shard_map/ppermute | solution.py:24
  6.0 0.1 collective-permute-start.3
  6.1 1.7 %collective-permute-done.refs_0_ = bf16[192,128]{1,0:T(8,128)(2,1)S(1)} collective-permute-done((bf16[192,128]{1,0:T(8,128)(2,1)S(1)}, bf16[192,128]{1,0:T(8,128)(2,1)S(1)}, u32[]{:S(2)}, u32[]{:S(2)}) %collective-permute-start) | collective-permute-done | bytes 49184 | tf_op jit(solution)/shard_map/ppermute | solution.py:24
  7.8 1.1 %shard_map.74 = bf16[192,128]{1,0:T(8,128)(2,1)S(1)} custom-call(f32[2,1024]{1,0:T(2,128)S(1)} %get-tuple-element.20.valid_ref, bf16[192,128]{1,0:T(8,128)(2,1)S(1)} %collective-permute-done.refs_0_, bf16[2064,256]{1,0:T(8,128)(2,1)S(1)} %get-tuple-element.19.refs_1_.refs_2_, bf16[2064,256]{1,0:T(8,128)(2,1)S(1)} %collective-permute-done.1.refs_2_.refs_3_), custom_call_target="tpu_custom_call" | custom-call | flops 201326592 | bytes 2097152 | tf_op jit(solution)/shard_map/pallas_call | solution.py:341
  8.9 3.2 %collective-permute-start.6 = (bf16[192,128]{1,0:T(8,128)(2,1)S(1)}, bf16[192,128]{1,0:T(8,128)(2,1)S(1)}, u32[]{:S(2)}, u32[]{:S(2)}) collective-permute-start(bf16[192,128]{1,0:T(8,128)(2,1)S(1)} %shard_map.74), channel_id=1, source_target_pairs={{24,0},{16,8},{8,16},{0,24},{25,1},{17,9},{9,17},{1,25},{26,2},{18... | collective-permute-start | bytes 147464 | tf_op jit(solution)/shard_map/ppermute | solution.py:29
  12.1 0.0 collective-permute-done.2.refs_0_
  12.1 1.6 %shard_map.76 = (bf16[192,128]{1,0:T(8,128)(2,1)S(1)}, bf16[192,128]{1,0:T(8,128)(2,1)S(1)}) custom-call(f32[2,1024]{1,0:T(2,128)S(1)} %get-tuple-element.20.valid_ref, bf16[192,128]{1,0:T(8,128)(2,1)S(1)} %collective-permute-done.2.refs_0_, bf16[192,128]{1,0:T(8,128)(2,1)S(1)} %collective-permute-done.3.refs_1_, ...), custom_call_target="tpu_custom_call" | custom-call | flops 402653184 | bytes 2097152 | tf_op jit(solution)/shard_map/pallas_call | solution.py:341
  13.7 0.2 collective-permute-start.4
  13.9 0.4 %collective-permute-start.5 = (bf16[192,128]{1,0:T(8,128)(2,1)S(1)}, bf16[192,128]{1,0:T(8,128)(2,1)S(1)}, u32[]{:S(2)}, u32[]{:S(2)}) collective-permute-start(bf16[192,128]{1,0:T(8,128)(2,1)S(1)} %get-tuple-element.25), channel_id=1, source_target_pairs={{16,0},{24,8},{0,16},{8,24},{17,1},{25,9},{1,17},{9,25},{18,2},{26... | collective-permute-start | bytes 147464 | tf_op jit(solution)/shard_map/ppermute | solution.py:29
  14.4 1.1 %shard_map.75.refs_0_ = bf16[192,128]{1,0:T(8,128)(2,1)S(1)} custom-call(f32[2,1024]{1,0:T(2,128)S(1)} %get-tuple-element.20.valid_ref, bf16[192,128]{1,0:T(8,128)(2,1)S(1)} %get-tuple-element.21.refs_0_, bf16[2064,256]{1,0:T(8,128)(2,1)S(1)} %get-tuple-element.19.refs_1_.refs_2_, bf16[2064,256]{1,0:T(8,128)(2,1)S(1)} %collective-permute-done.1.refs_2_.refs_3_), custom_call_target="tpu_custom_call" | custom-call | flops 201326592 | bytes 2097152 | tf_op jit(solution)/shard_map/pallas_call | solution.py:341
  15.5 2.4 %collective-permute-done.4.refs_1_ = bf16[192,128]{1,0:T(8,128)(2,1)S(1)} collective-permute-done((bf16[192,128]{1,0:T(8,128)(2,1)S(1)}, bf16[192,128]{1,0:T(8,128)(2,1)S(1)}, u32[]{:S(2)}, u32[]{:S(2)}) %collective-permute-start.4) | collective-permute-done | bytes 49184 | tf_op jit(solution)/shard_map/ppermute | solution.py:29
  17.9 0.2 collective-permute-done.5.refs_2_
  18.0 0.2 shard_map.77.refs_0_
  18.3 3.6 %collective-permute-start.9 = (bf16[16,4096]{1,0:T(8,128)(2,1)S(1)}, bf16[16,4096]{1,0:T(8,128)(2,1)S(1)}, u32[]{:S(2)}, u32[]{:S(2)}) collective-permute-start(bf16[16,4096]{1,0:T(8,128)(2,1)S(1)} %shard_map.77.refs_0_), channel_id=1, source_target_pairs={{0,3},{1,2},{2,1},{3,0},{4,7},{5,6},{6,5},{7,4},{8,11},{9,10},{10,... | collective-permute-start | bytes 393224 | tf_op jit(solution)/shard_map/ppermute | solution.py:395
  21.9 2.7 %collective-permute-start.7 = (bf16[16,4096]{1,0:T(8,128)(2,1)S(1)}, bf16[16,4096]{1,0:T(8,128)(2,1)S(1)}, u32[]{:S(2)}, u32[]{:S(2)}) collective-permute-start(bf16[16,4096]{1,0:T(8,128)(2,1)S(1)} %shard_map.77.refs_0_), channel_id=1, source_target_pairs={{0,2},{1,3},{2,0},{3,1},{8,10},{9,11},{10,8},{11,9},{16,18},{17,19... | collective-permute-start | bytes 393224 | tf_op jit(solution)/shard_map/ppermute | solution.py:395
  24.6 0.6 %collective-permute-done.9.refs_1_ = bf16[16,4096]{1,0:T(8,128)(2,1)S(1)} collective-permute-done((bf16[16,4096]{1,0:T(8,128)(2,1)S(1)}, bf16[16,4096]{1,0:T(8,128)(2,1)S(1)}, u32[]{:S(2)}, u32[]{:S(2)}) %collective-permute-start.9) | collective-permute-done | bytes 131104 | tf_op jit(solution)/shard_map/ppermute | solution.py:395
  25.2 0.7 %collective-permute-start.10 = (bf16[16,4096]{1,0:T(8,128)(2,1)S(1)}, bf16[16,4096]{1,0:T(8,128)(2,1)S(1)}, u32[]{:S(2)}, u32[]{:S(2)}) collective-permute-start(bf16[16,4096]{1,0:T(8,128)(2,1)S(1)} %collective-permute-done.9.refs_1_), channel_id=1, source_target_pairs={{4,5},{5,4},{6,7},{7,6},{12,13},{13,12},{14,15},{15,14},{20,21},{2... | collective-permute-start | bytes 393224 | tf_op jit(solution)/shard_map/ppermute | solution.py:395
  25.9 0.7 %shard_map.78.refs_3_ = bf16[16,16384]{1,0:T(8,128)(2,1)} custom-call(bf16[16,4096]{1,0:T(8,128)(2,1)S(1)} %shard_map.77.refs_0_, bf16[16,4096]{1,0:T(8,128)(2,1)S(1)} %collective-permute-done.9.refs_1_), custom_call_target="tpu_custom_call" | custom-call | tf_op jit(solution)/shard_map/pallas_call | solution.py:364
  26.6 1.1 %collective-permute-done.8.refs_1_ = bf16[16,4096]{1,0:T(8,128)(2,1)S(1)} collective-permute-done((bf16[16,4096]{1,0:T(8,128)(2,1)S(1)}, bf16[16,4096]{1,0:T(8,128)(2,1)S(1)}, u32[]{:S(2)}, u32[]{:S(2)}) %collective-permute-start.8) | collective-permute-done | bytes 131104 | tf_op jit(solution)/shard_map/ppermute | solution.py:395
  27.7 2.0 %collective-permute-done.7.refs_0_ = bf16[16,4096]{1,0:T(8,128)(2,1)S(1)} collective-permute-done((bf16[16,4096]{1,0:T(8,128)(2,1)S(1)}, bf16[16,4096]{1,0:T(8,128)(2,1)S(1)}, u32[]{:S(2)}, u32[]{:S(2)}) %collective-permute-start.7) | collective-permute-done | bytes 131104 | tf_op jit(solution)/shard_map/ppermute | solution.py:395
  29.7 0.7 %shard_map.79 = bf16[16,16384]{1,0:T(8,128)(2,1)} custom-call(bf16[16,4096]{1,0:T(8,128)(2,1)S(1)} %collective-permute-done.7.refs_0_, bf16[16,4096]{1,0:T(8,128)(2,1)S(1)} %collective-permute-done.8.refs_1_, bf16[16,4096]{1,0:T(8,128)(2,1)S(1)} %collective-permute-done.10.refs_2_, bf16[16,16384]{1,0:T(8,128)(2,1)} %shard_map.78.refs_3_), custom_call_target="tpu_custom_call", output_to_operand_aliasing={{}: (3, {})} | custom-call | tf_op jit(solution)/shard_map/pallas_call | solution.py:364
  (5 shorter events, 0.0 us)
Async XLA Ops:
  1.4 6.4 %collective-permute-start.1 = (bf16[2064,256]{1,0:T(8,128)(2,1)S(1)}, bf16[2064,256]{1,0:T(8,128)(2,1)S(1)}, u32[]{:S(2)}, u32[]{:S(2)}) collective-permute-start(bf16[2064,256]{1,0:T(8,128)(2,1)S(1)} %get-tuple-element.19.refs_1_.refs_2_), channel_id=1, source_target_pairs={{0,4},{4,0},{1,5},{5,1},{2,6},{6,2},{3,7},{7,3},{8,12},{12,8},{9,1... | collective-permute-start | bytes 3170312 | tf_op jit(solution)/shard_map/ppermute | solution.py:334
  2.0 5.9 %collective-permute-start = (bf16[192,128]{1,0:T(8,128)(2,1)S(1)}, bf16[192,128]{1,0:T(8,128)(2,1)S(1)}, u32[]{:S(2)}, u32[]{:S(2)}) collective-permute-start(bf16[192,128]{1,0:T(8,128)(2,1)S(1)} %get-tuple-element.18), channel_id=1, source_target_pairs={{0,24},{8,16},{16,8},{24,0},{1,25},{9,17},{17,9},{25,1},{2,26},{10... | collective-permute-start | bytes 147464 | tf_op jit(solution)/shard_map/ppermute | solution.py:24
  5.5 6.6 %collective-permute-start.2 = (bf16[192,128]{1,0:T(8,128)(2,1)S(1)}, bf16[192,128]{1,0:T(8,128)(2,1)S(1)}, u32[]{:S(2)}, u32[]{:S(2)}) collective-permute-start(bf16[192,128]{1,0:T(8,128)(2,1)S(1)} %get-tuple-element.22), channel_id=1, source_target_pairs={{0,8},{8,0},{16,24},{24,16},{1,9},{9,1},{17,25},{25,17},{2,10},{10... | collective-permute-start | bytes 147464 | tf_op jit(solution)/shard_map/ppermute | solution.py:24
  6.0 6.1 %collective-permute-start.3 = (bf16[192,128]{1,0:T(8,128)(2,1)S(1)}, bf16[192,128]{1,0:T(8,128)(2,1)S(1)}, u32[]{:S(2)}, u32[]{:S(2)}) collective-permute-start(bf16[192,128]{1,0:T(8,128)(2,1)S(1)} %get-tuple-element.23), channel_id=1, source_target_pairs={{0,16},{8,24},{16,0},{24,8},{1,17},{9,25},{17,1},{25,9},{2,18},{10... | collective-permute-start | bytes 147464 | tf_op jit(solution)/shard_map/ppermute | solution.py:24
  8.9 6.6 %collective-permute-start.6 = (bf16[192,128]{1,0:T(8,128)(2,1)S(1)}, bf16[192,128]{1,0:T(8,128)(2,1)S(1)}, u32[]{:S(2)}, u32[]{:S(2)}) collective-permute-start(bf16[192,128]{1,0:T(8,128)(2,1)S(1)} %shard_map.74), channel_id=1, source_target_pairs={{24,0},{16,8},{8,16},{0,24},{25,1},{17,9},{9,17},{1,25},{26,2},{18... | collective-permute-start | bytes 147464 | tf_op jit(solution)/shard_map/ppermute | solution.py:29
  13.7 4.2 %collective-permute-start.4 = (bf16[192,128]{1,0:T(8,128)(2,1)S(1)}, bf16[192,128]{1,0:T(8,128)(2,1)S(1)}, u32[]{:S(2)}, u32[]{:S(2)}) collective-permute-start(bf16[192,128]{1,0:T(8,128)(2,1)S(1)} %get-tuple-element.24), channel_id=1, source_target_pairs={{8,0},{0,8},{24,16},{16,24},{9,1},{1,9},{25,17},{17,25},{10,2},{2,... | collective-permute-start | bytes 147464 | tf_op jit(solution)/shard_map/ppermute | solution.py:29
  13.9 4.1 %collective-permute-start.5 = (bf16[192,128]{1,0:T(8,128)(2,1)S(1)}, bf16[192,128]{1,0:T(8,128)(2,1)S(1)}, u32[]{:S(2)}, u32[]{:S(2)}) collective-permute-start(bf16[192,128]{1,0:T(8,128)(2,1)S(1)} %get-tuple-element.25), channel_id=1, source_target_pairs={{16,0},{24,8},{0,16},{8,24},{17,1},{25,9},{1,17},{9,25},{18,2},{26... | collective-permute-start | bytes 147464 | tf_op jit(solution)/shard_map/ppermute | solution.py:29
  18.3 6.9 %collective-permute-start.9 = (bf16[16,4096]{1,0:T(8,128)(2,1)S(1)}, bf16[16,4096]{1,0:T(8,128)(2,1)S(1)}, u32[]{:S(2)}, u32[]{:S(2)}) collective-permute-start(bf16[16,4096]{1,0:T(8,128)(2,1)S(1)} %shard_map.77.refs_0_), channel_id=1, source_target_pairs={{0,3},{1,2},{2,1},{3,0},{4,7},{5,6},{6,5},{7,4},{8,11},{9,10},{10,... | collective-permute-start | bytes 393224 | tf_op jit(solution)/shard_map/ppermute | solution.py:395
  21.9 5.8 %collective-permute-start.8 = (bf16[16,4096]{1,0:T(8,128)(2,1)S(1)}, bf16[16,4096]{1,0:T(8,128)(2,1)S(1)}, u32[]{:S(2)}, u32[]{:S(2)}) collective-permute-start(bf16[16,4096]{1,0:T(8,128)(2,1)S(1)} %shard_map.77.refs_0_), channel_id=1, source_target_pairs={{0,1},{1,0},{2,3},{3,2},{4,5},{5,4},{6,7},{7,6},{8,9},{9,8},{10,11... | collective-permute-start | bytes 393224 | tf_op jit(solution)/shard_map/ppermute | solution.py:395
  21.9 7.8 %collective-permute-start.7 = (bf16[16,4096]{1,0:T(8,128)(2,1)S(1)}, bf16[16,4096]{1,0:T(8,128)(2,1)S(1)}, u32[]{:S(2)}, u32[]{:S(2)}) collective-permute-start(bf16[16,4096]{1,0:T(8,128)(2,1)S(1)} %shard_map.77.refs_0_), channel_id=1, source_target_pairs={{0,2},{1,3},{2,0},{3,1},{8,10},{9,11},{10,8},{11,9},{16,18},{17,19... | collective-permute-start | bytes 393224 | tf_op jit(solution)/shard_map/ppermute | solution.py:395
  25.2 4.5 %collective-permute-start.10 = (bf16[16,4096]{1,0:T(8,128)(2,1)S(1)}, bf16[16,4096]{1,0:T(8,128)(2,1)S(1)}, u32[]{:S(2)}, u32[]{:S(2)}) collective-permute-start(bf16[16,4096]{1,0:T(8,128)(2,1)S(1)} %collective-permute-done.9.refs_1_), channel_id=1, source_target_pairs={{4,5},{5,4},{6,7},{7,6},{12,13},{13,12},{14,15},{15,14},{20,21},{2... | collective-permute-start | bytes 393224 | tf_op jit(solution)/shard_map/ppermute | solution.py:395

commit v5 on v4

--- a/solution.py
+++ b/solution.py
@@ -246,28 +246,20 @@
             out_refs[k][spans[g], :] = result[k * rows_doc : (k + 1) * rows_doc]
 
 
-def assemble_kernel(n_head, places, *refs):
-    block_refs, out_ref, sems = refs[: len(places)], refs[-2], refs[-1]
-    me, parity = lax.axis_index("head"), lax.rem(lax.axis_index("ctx"), 2)
+def assemble_kernel(n_head, steps, *refs):
+    block_refs, out_ref, sems = refs[: len(steps)], refs[-2], refs[-1]
+    me = lax.axis_index("head")
     width = block_refs[0].shape[1]
     copies = []
-    for at, (even, odd) in enumerate(places):
-        step = jnp.where(parity == 0, even or 0, odd or 0)
+    for at, step in enumerate(steps):
         column = pl.multiple_of(peer_of_traced(me, step, n_head) * width, width)
-        copy = pltpu.make_async_copy(
-            block_refs[at], out_ref.at[:, pl.ds(column, width)], sems.at[at]
-        )
-        copies.append((copy, 1 if even is None else 0 if odd is None else None))
-    for copy, wanted in copies:
-        if wanted is None:
-            copy.start()
-        else:
-            pl.when(parity == wanted)(copy.start)
-    for copy, wanted in copies:
-        if wanted is None:
-            copy.wait()
-        else:
-            pl.when(parity == wanted)(copy.wait)
+        copies.append(
+            pltpu.make_async_copy(block_refs[at], out_ref.at[:, pl.ds(column, width)], sems.at[at])
+        )
+    for copy in copies:
+        copy.start()
+    for copy in copies:
+        copy.wait()
 
 
 def peer_of_traced(index, step, count):
@@ -360,17 +352,6 @@
     finished[0] = attended_for((0,), valid)[0]
     back = [finished[0]] + [returned(finished[k], "doc", k) for k in range(1, n_doc)]
 
-    def assembled(pieces, before):
-        return pl.pallas_call(
-            functools.partial(assemble_kernel, n_head, [place for place, _ in pieces]),
-            out_shape=jax.ShapeDtypeStruct((rows_home, n_head * width), jnp.bfloat16),
-            in_specs=[anywhere] * len(pieces) + [hbm] * len(before),
-            out_specs=hbm,
-            scratch_shapes=[pltpu.SemaphoreType.DMA((len(pieces),))],
-            input_output_aliases={len(pieces): 0} if before else {},
-            compiler_params=params,
-        )(*[block for _, block in pieces], *before)
-
     mine = pl.pallas_call(
         functools.partial(collect_kernel, n_doc, cap),
         out_shape=jax.ShapeDtypeStruct((rows_home, width), jnp.bfloat16),
@@ -379,29 +360,25 @@
         compiler_params=params,
     )(placing, *back)
 
-    if n_head != 4:
-        return assembled(
-            [((0, 0), mine)]
-            + [((step, step), returned(mine, "head", step)) for step in range(1, n_head)],
-            (),
-        )
-
-    def swapped(value, even, odd):
-        pairs = []
-        for c in range(n_ctx):
-            step = odd if c % 2 else even
-            if step is not None:
-                pairs += [(c * n_head + h, c * n_head + (h ^ step)) for h in range(n_head)]
-        return lax.ppermute(value, ("ctx", "head"), pairs)
-
-    first = swapped(mine, 3, 3)
-    second = swapped(mine, 1, 1)
-    third = swapped(mine, 2, None)
-    passed = swapped(first, None, 1)
-    attended = assembled([((0, 0), mine), ((3, 3), first)], ())
-    return assembled(
-        [((2, None), third), ((1, 1), second), ((None, 2), passed)], (attended,)
-    )
+    def assembled(steps, before):
+        return pl.pallas_call(
+            functools.partial(assemble_kernel, n_head, steps),
+            out_shape=jax.ShapeDtypeStruct((rows_home, n_head * width), jnp.bfloat16),
+            in_specs=[anywhere] * len(steps) + [hbm] * len(before),
+            out_specs=hbm,
+            scratch_shapes=[pltpu.SemaphoreType.DMA((len(steps),))],
+            input_output_aliases={len(steps): 0} if before else {},
+            compiler_params=params,
+        )(*[blocks[step] for step in steps], *before)
+
+    order = sorted(range(1, n_head), key=lambda step: (step % 2, step))
+    blocks = {0: mine}
+    for step in order:
+        blocks[step] = returned(mine, "head", step)
+    if len(order) < 2:
+        return assembled([0] + order, ())
+    attended = assembled([0, order[0]], ())
+    return assembled(order[:0:-1], (attended,))
 
 
 def solution(mesh):

time: 30.6 us -> 30.4 us (level)
  starting transfers between devices: 15.5 us -> 13 us
  waiting for transfers between devices: 7.92 us -> 10.4 us
    ppermute x4 -> x0, starting transfers between devices: 7.01 us -> none  [swapped(): return lax.ppermute(value, ('ctx', 'head'), pairs)]
    ppermute x3 -> x6, waiting for transfers between devices: 2.55 us -> 8.65 us  [returned(): lax.ppermute(value, axis, [(peer_of(i, step, count), i) for i in range(co...]
    ppermute x3 -> x6, starting transfers between devices: 3.83 us -> 8.28 us  [returned(): lax.ppermute(value, axis, [(peer_of(i, step, count), i) for i in range(co...]
    ppermute x4 -> x0, waiting for transfers between devices: 3.67 us -> none  [swapped(): return lax.ppermute(value, ('ctx', 'head'), pairs)]
  transfers between devices with their start and end apart: 11 -> 10, of which waited for: 6 -> 5; matrix products, arithmetic and copies ran while one was open for 0% -> 0% of each run, Pallas kernels for 15% -> 15%
where the time goes in v5:
time: 30.4 us; the launch traced here: 30.3 us
  starting transfers between devices  13 us (43%)
  waiting for transfers between devices  10.4 us (34%)
  Pallas kernels  6.91 us (23%)
    ppermute x6, waiting for transfers between devices, returned(): lax.ppermute(value, axis, [(peer_of(i, step, count), i) for i in range(co...  8.65 us
    ppermute x6, starting transfers between devices, returned(): lax.ppermute(value, axis, [(peer_of(i, step, count), i) for i in range(co...  8.28 us
    ppermute x3, starting transfers between devices, sent(): lax.ppermute(value, axis, [(i, peer_of(i, step, count)) for i in range(co...  4.16 us
    pallas_call x3, Pallas kernels, attended_for(): pl.pallas_call(functools.partial(attend_kernel, len(sources), n_ctx, kv_d...  3.81 us
    ppermute x3, waiting for transfers between devices, sent(): lax.ppermute(value, axis, [(i, peer_of(i, step, count)) for i in range(co...  1.7 us
    pallas_call x2, Pallas kernels, assembled(): pl.pallas_call(functools.partial(assemble_kernel, n_head, steps), out_sha...  1.43 us
    pallas_call x1, Pallas kernels, shards(): pl.pallas_call(functools.partial(dispatch_kernel, n_doc, n_ctx, cap), out...  1.43 us
  transfers between devices with their start and end apart: 10, of which 5 were waited for; matrix products, arithmetic and copies ran while one was open for 0% of the time, Pallas kernels for 15%

profile of v5, /device:TPU:0, one launch (start us, length us, event | category | flops | bytes accessed | tf_op | source)
XLA Modules:
  0.0 30.3 jit_solution(4800837708312373394)
XLA Ops:
  0.0 1.4 %shard_map.73 = (bf16[192,128]{1,0:T(8,128)(2,1)S(1)}, f32[2,1024]{1,0:T(2,128)S(1)}, bf16[2064,256]{1,0:T(8,128)(2,1)S(1)}, bf16[192,128]{1,0:T(8,128)(2,1)S(1)...) custom-call(s32[1,16]{1,0:T(1,128)} %bitcast.10, s32[1,4]{1,0:T(1,128)} %bitcast.11, ...), custom_call_target="tpu_custom_call" | custom-call | tf_op jit(solution)/shard_map/pallas_call | solution.py:307
  1.4 0.5 %collective-permute-start.1 = (bf16[2064,256]{1,0:T(8,128)(2,1)S(1)}, bf16[2064,256]{1,0:T(8,128)(2,1)S(1)}, u32[]{:S(2)}, u32[]{:S(2)}) collective-permute-start(bf16[2064,256]{1,0:T(8,128)(2,1)S(1)} %get-tuple-element.19.refs_1_.refs_2_), channel_id=1, source_target_pairs={{0,4},{4,0},{1,5},{5,1},{2,6},{6,2},{3,7},{7,3},{8,12},{12,8},{9,1... | collective-permute-start | bytes 3170312 | tf_op jit(solution)/shard_map/ppermute | solution.py:326
  2.0 3.5 %collective-permute-start = (bf16[192,128]{1,0:T(8,128)(2,1)S(1)}, bf16[192,128]{1,0:T(8,128)(2,1)S(1)}, u32[]{:S(2)}, u32[]{:S(2)}) collective-permute-start(bf16[192,128]{1,0:T(8,128)(2,1)S(1)} %get-tuple-element.18), channel_id=1, source_target_pairs={{0,24},{8,16},{16,8},{24,0},{1,25},{9,17},{17,9},{25,1},{2,26},{10... | collective-permute-start | bytes 147464 | tf_op jit(solution)/shard_map/ppermute | solution.py:24
  5.5 0.5 %collective-permute-start.2 = (bf16[192,128]{1,0:T(8,128)(2,1)S(1)}, bf16[192,128]{1,0:T(8,128)(2,1)S(1)}, u32[]{:S(2)}, u32[]{:S(2)}) collective-permute-start(bf16[192,128]{1,0:T(8,128)(2,1)S(1)} %get-tuple-element.22), channel_id=1, source_target_pairs={{0,8},{8,0},{16,24},{24,16},{1,9},{9,1},{17,25},{25,17},{2,10},{10... | collective-permute-start | bytes 147464 | tf_op jit(solution)/shard_map/ppermute | solution.py:24
  6.0 0.1 collective-permute-start.3
  6.1 1.7 %collective-permute-done.refs_0_ = bf16[192,128]{1,0:T(8,128)(2,1)S(1)} collective-permute-done((bf16[192,128]{1,0:T(8,128)(2,1)S(1)}, bf16[192,128]{1,0:T(8,128)(2,1)S(1)}, u32[]{:S(2)}, u32[]{:S(2)}) %collective-permute-start) | collective-permute-done | bytes 49184 | tf_op jit(solution)/shard_map/ppermute | solution.py:24
  7.8 1.1 %shard_map.74 = bf16[192,128]{1,0:T(8,128)(2,1)S(1)} custom-call(f32[2,1024]{1,0:T(2,128)S(1)} %get-tuple-element.20.valid_ref, bf16[192,128]{1,0:T(8,128)(2,1)S(1)} %collective-permute-done.refs_0_, bf16[2064,256]{1,0:T(8,128)(2,1)S(1)} %get-tuple-element.19.refs_1_.refs_2_, bf16[2064,256]{1,0:T(8,128)(2,1)S(1)} %collective-permute-done.1.refs_2_.refs_3_), custom_call_target="tpu_custom_call" | custom-call | flops 201326592 | bytes 2097152 | tf_op jit(solution)/shard_map/pallas_call | solution.py:333
  8.9 3.2 %collective-permute-start.6 = (bf16[192,128]{1,0:T(8,128)(2,1)S(1)}, bf16[192,128]{1,0:T(8,128)(2,1)S(1)}, u32[]{:S(2)}, u32[]{:S(2)}) collective-permute-start(bf16[192,128]{1,0:T(8,128)(2,1)S(1)} %shard_map.74), channel_id=1, source_target_pairs={{24,0},{16,8},{8,16},{0,24},{25,1},{17,9},{9,17},{1,25},{26,2},{18... | collective-permute-start | bytes 147464 | tf_op jit(solution)/shard_map/ppermute | solution.py:29
  12.1 0.0 collective-permute-done.2.refs_0_
  12.1 0.0 collective-permute-done.3.refs_1_
  12.1 1.6 %shard_map.76 = (bf16[192,128]{1,0:T(8,128)(2,1)S(1)}, bf16[192,128]{1,0:T(8,128)(2,1)S(1)}) custom-call(f32[2,1024]{1,0:T(2,128)S(1)} %get-tuple-element.20.valid_ref, bf16[192,128]{1,0:T(8,128)(2,1)S(1)} %collective-permute-done.2.refs_0_, bf16[192,128]{1,0:T(8,128)(2,1)S(1)} %collective-permute-done.3.refs_1_, ...), custom_call_target="tpu_custom_call" | custom-call | flops 402653184 | bytes 2097152 | tf_op jit(solution)/shard_map/pallas_call | solution.py:333
  13.7 0.2 collective-permute-start.4
  13.9 0.4 %collective-permute-start.5 = (bf16[192,128]{1,0:T(8,128)(2,1)S(1)}, bf16[192,128]{1,0:T(8,128)(2,1)S(1)}, u32[]{:S(2)}, u32[]{:S(2)}) collective-permute-start(bf16[192,128]{1,0:T(8,128)(2,1)S(1)} %get-tuple-element.25), channel_id=1, source_target_pairs={{16,0},{24,8},{0,16},{8,24},{17,1},{25,9},{1,17},{9,25},{18,2},{26... | collective-permute-start | bytes 147464 | tf_op jit(solution)/shard_map/ppermute | solution.py:29
  14.4 1.1 %shard_map.75.refs_0_ = bf16[192,128]{1,0:T(8,128)(2,1)S(1)} custom-call(f32[2,1024]{1,0:T(2,128)S(1)} %get-tuple-element.20.valid_ref, bf16[192,128]{1,0:T(8,128)(2,1)S(1)} %get-tuple-element.21.refs_0_, bf16[2064,256]{1,0:T(8,128)(2,1)S(1)} %get-tuple-element.19.refs_1_.refs_2_, bf16[2064,256]{1,0:T(8,128)(2,1)S(1)} %collective-permute-done.1.refs_2_.refs_3_), custom_call_target="tpu_custom_call" | custom-call | flops 201326592 | bytes 2097152 | tf_op jit(solution)/shard_map/pallas_call | solution.py:333
  15.5 2.4 %collective-permute-done.4.refs_1_ = bf16[192,128]{1,0:T(8,128)(2,1)S(1)} collective-permute-done((bf16[192,128]{1,0:T(8,128)(2,1)S(1)}, bf16[192,128]{1,0:T(8,128)(2,1)S(1)}, u32[]{:S(2)}, u32[]{:S(2)}) %collective-permute-start.4) | collective-permute-done | bytes 49184 | tf_op jit(solution)/shard_map/ppermute | solution.py:29
  17.9 0.2 collective-permute-done.5.refs_2_
  18.0 0.2 shard_map.77.refs_0_
  18.3 2.6 %collective-permute-start.9 = (bf16[16,4096]{1,0:T(8,128)(2,1)S(1)}, bf16[16,4096]{1,0:T(8,128)(2,1)S(1)}, u32[]{:S(2)}, u32[]{:S(2)}) collective-permute-start(bf16[16,4096]{1,0:T(8,128)(2,1)S(1)} %shard_map.77.refs_0_), channel_id=1, source_target_pairs={{2,0},{3,1},{0,2},{1,3},{6,4},{7,5},{4,6},{5,7},{10,8},{11,9},{8,1... | collective-permute-start | bytes 393224 | tf_op jit(solution)/shard_map/ppermute | solution.py:29
  20.9 1.6 %collective-permute-start.8 = (bf16[16,4096]{1,0:T(8,128)(2,1)S(1)}, bf16[16,4096]{1,0:T(8,128)(2,1)S(1)}, u32[]{:S(2)}, u32[]{:S(2)}) collective-permute-start(bf16[16,4096]{1,0:T(8,128)(2,1)S(1)} %shard_map.77.refs_0_), channel_id=1, source_target_pairs={{1,0},{0,1},{3,2},{2,3},{5,4},{4,5},{7,6},{6,7},{9,8},{8,9},{11,10... | collective-permute-start | bytes 393224 | tf_op jit(solution)/shard_map/ppermute | solution.py:29
  22.5 0.2 collective-permute-start.7
  22.7 5.1 %collective-permute-done.9.refs_1_ = bf16[16,4096]{1,0:T(8,128)(2,1)S(1)} collective-permute-done((bf16[16,4096]{1,0:T(8,128)(2,1)S(1)}, bf16[16,4096]{1,0:T(8,128)(2,1)S(1)}, u32[]{:S(2)}, u32[]{:S(2)}) %collective-permute-start.9) | collective-permute-done | bytes 131104 | tf_op jit(solution)/shard_map/ppermute | solution.py:29
  27.9 0.7 %shard_map.78.refs_2_ = bf16[16,16384]{1,0:T(8,128)(2,1)} custom-call(bf16[16,4096]{1,0:T(8,128)(2,1)S(1)} %shard_map.77.refs_0_, bf16[16,4096]{1,0:T(8,128)(2,1)S(1)} %collective-permute-done.9.refs_1_), custom_call_target="tpu_custom_call" | custom-call | tf_op jit(solution)/shard_map/pallas_call | solution.py:364
  28.6 1.0 %collective-permute-done.7.refs_0_ = bf16[16,4096]{1,0:T(8,128)(2,1)S(1)} collective-permute-done((bf16[16,4096]{1,0:T(8,128)(2,1)S(1)}, bf16[16,4096]{1,0:T(8,128)(2,1)S(1)}, u32[]{:S(2)}, u32[]{:S(2)}) %collective-permute-start.7) | collective-permute-done | bytes 131104 | tf_op jit(solution)/shard_map/ppermute | solution.py:29
  29.6 0.7 %shard_map.79 = bf16[16,16384]{1,0:T(8,128)(2,1)} custom-call(bf16[16,4096]{1,0:T(8,128)(2,1)S(1)} %collective-permute-done.7.refs_0_, bf16[16,4096]{1,0:T(8,128)(2,1)S(1)} %collective-permute-done.8.refs_1_, bf16[16,16384]{1,0:T(8,128)(2,1)} %shard_map.78.refs_2_), custom_call_target="tpu_custom_call", output_to_operand_aliasing={{}: (2, {})} | custom-call | tf_op jit(solution)/shard_map/pallas_call | solution.py:364
  (3 shorter events, 0.0 us)
Async XLA Ops:
  1.4 6.4 %collective-permute-start.1 = (bf16[2064,256]{1,0:T(8,128)(2,1)S(1)}, bf16[2064,256]{1,0:T(8,128)(2,1)S(1)}, u32[]{:S(2)}, u32[]{:S(2)}) collective-permute-start(bf16[2064,256]{1,0:T(8,128)(2,1)S(1)} %get-tuple-element.19.refs_1_.refs_2_), channel_id=1, source_target_pairs={{0,4},{4,0},{1,5},{5,1},{2,6},{6,2},{3,7},{7,3},{8,12},{12,8},{9,1... | collective-permute-start | bytes 3170312 | tf_op jit(solution)/shard_map/ppermute | solution.py:326
  2.0 5.9 %collective-permute-start = (bf16[192,128]{1,0:T(8,128)(2,1)S(1)}, bf16[192,128]{1,0:T(8,128)(2,1)S(1)}, u32[]{:S(2)}, u32[]{:S(2)}) collective-permute-start(bf16[192,128]{1,0:T(8,128)(2,1)S(1)} %get-tuple-element.18), channel_id=1, source_target_pairs={{0,24},{8,16},{16,8},{24,0},{1,25},{9,17},{17,9},{25,1},{2,26},{10... | collective-permute-start | bytes 147464 | tf_op jit(solution)/shard_map/ppermute | solution.py:24
  5.5 6.6 %collective-permute-start.2 = (bf16[192,128]{1,0:T(8,128)(2,1)S(1)}, bf16[192,128]{1,0:T(8,128)(2,1)S(1)}, u32[]{:S(2)}, u32[]{:S(2)}) collective-permute-start(bf16[192,128]{1,0:T(8,128)(2,1)S(1)} %get-tuple-element.22), channel_id=1, source_target_pairs={{0,8},{8,0},{16,24},{24,16},{1,9},{9,1},{17,25},{25,17},{2,10},{10... | collective-permute-start | bytes 147464 | tf_op jit(solution)/shard_map/ppermute | solution.py:24
  6.0 6.1 %collective-permute-start.3 = (bf16[192,128]{1,0:T(8,128)(2,1)S(1)}, bf16[192,128]{1,0:T(8,128)(2,1)S(1)}, u32[]{:S(2)}, u32[]{:S(2)}) collective-permute-start(bf16[192,128]{1,0:T(8,128)(2,1)S(1)} %get-tuple-element.23), channel_id=1, source_target_pairs={{0,16},{8,24},{16,0},{24,8},{1,17},{9,25},{17,1},{25,9},{2,18},{10... | collective-permute-start | bytes 147464 | tf_op jit(solution)/shard_map/ppermute | solution.py:24
  8.9 6.6 %collective-permute-start.6 = (bf16[192,128]{1,0:T(8,128)(2,1)S(1)}, bf16[192,128]{1,0:T(8,128)(2,1)S(1)}, u32[]{:S(2)}, u32[]{:S(2)}) collective-permute-start(bf16[192,128]{1,0:T(8,128)(2,1)S(1)} %shard_map.74), channel_id=1, source_target_pairs={{24,0},{16,8},{8,16},{0,24},{25,1},{17,9},{9,17},{1,25},{26,2},{18... | collective-permute-start | bytes 147464 | tf_op jit(solution)/shard_map/ppermute | solution.py:29
  13.7 4.2 %collective-permute-start.4 = (bf16[192,128]{1,0:T(8,128)(2,1)S(1)}, bf16[192,128]{1,0:T(8,128)(2,1)S(1)}, u32[]{:S(2)}, u32[]{:S(2)}) collective-permute-start(bf16[192,128]{1,0:T(8,128)(2,1)S(1)} %get-tuple-element.24), channel_id=1, source_target_pairs={{8,0},{0,8},{24,16},{16,24},{9,1},{1,9},{25,17},{17,25},{10,2},{2,... | collective-permute-start | bytes 147464 | tf_op jit(solution)/shard_map/ppermute | solution.py:29
  13.9 4.1 %collective-permute-start.5 = (bf16[192,128]{1,0:T(8,128)(2,1)S(1)}, bf16[192,128]{1,0:T(8,128)(2,1)S(1)}, u32[]{:S(2)}, u32[]{:S(2)}) collective-permute-start(bf16[192,128]{1,0:T(8,128)(2,1)S(1)} %get-tuple-element.25), channel_id=1, source_target_pairs={{16,0},{24,8},{0,16},{8,24},{17,1},{25,9},{1,17},{9,25},{18,2},{26... | collective-permute-start | bytes 147464 | tf_op jit(solution)/shard_map/ppermute | solution.py:29
  18.3 9.6 %collective-permute-start.9 = (bf16[16,4096]{1,0:T(8,128)(2,1)S(1)}, bf16[16,4096]{1,0:T(8,128)(2,1)S(1)}, u32[]{:S(2)}, u32[]{:S(2)}) collective-permute-start(bf16[16,4096]{1,0:T(8,128)(2,1)S(1)} %shard_map.77.refs_0_), channel_id=1, source_target_pairs={{2,0},{3,1},{0,2},{1,3},{6,4},{7,5},{4,6},{5,7},{10,8},{11,9},{8,1... | collective-permute-start | bytes 393224 | tf_op jit(solution)/shard_map/ppermute | solution.py:29
  20.9 7.7 %collective-permute-start.8 = (bf16[16,4096]{1,0:T(8,128)(2,1)S(1)}, bf16[16,4096]{1,0:T(8,128)(2,1)S(1)}, u32[]{:S(2)}, u32[]{:S(2)}) collective-permute-start(bf16[16,4096]{1,0:T(8,128)(2,1)S(1)} %shard_map.77.refs_0_), channel_id=1, source_target_pairs={{1,0},{0,1},{3,2},{2,3},{5,4},{4,5},{7,6},{6,7},{9,8},{8,9},{11,10... | collective-permute-start | bytes 393224 | tf_op jit(solution)/shard_map/ppermute | solution.py:29
  22.5 7.1 %collective-permute-start.7 = (bf16[16,4096]{1,0:T(8,128)(2,1)S(1)}, bf16[16,4096]{1,0:T(8,128)(2,1)S(1)}, u32[]{:S(2)}, u32[]{:S(2)}) collective-permute-start(bf16[16,4096]{1,0:T(8,128)(2,1)S(1)} %shard_map.77.refs_0_), channel_id=1, source_target_pairs={{3,0},{2,1},{1,2},{0,3},{7,4},{6,5},{5,6},{4,7},{11,8},{10,9},{9,1... | collective-permute-start | bytes 393224 | tf_op jit(solution)/shard_map/ppermute | solution.py:29

commit v6 on v5

--- a/solution.py
+++ b/solution.py
@@ -378,7 +378,9 @@
     if len(order) < 2:
         return assembled([0] + order, ())
     attended = assembled([0, order[0]], ())
-    return assembled(order[:0:-1], (attended,))
+    for step in order[1:]:
+        attended = assembled([step], (attended,))
+    return attended
 
 
 def solution(mesh):

time: 30.4 us -> 30.4 us (level)
  waiting for transfers between devices: 10.4 us -> 9.67 us
  Pallas kernels: 6.91 us -> 7.53 us
    ppermute x6, waiting for transfers between devices: 8.65 us -> 7.97 us  [returned(): lax.ppermute(value, axis, [(peer_of(i, step, count), i) for i in range(co...]
    pallas_call x2 -> x3, Pallas kernels: 1.43 us -> 2.05 us  [assembled(): pl.pallas_call(functools.partial(assemble_kernel, n_head, steps), out_sha...]
  transfers between devices with their start and end apart: 10 -> 10, of which waited for: 5 -> 5; matrix products, arithmetic and copies ran while one was open for 0% -> 0% of each run, Pallas kernels for 15% -> 17%
where the time goes in v6:
time: 30.4 us; the launch traced here: 30.2 us
  starting transfers between devices  13 us (43%)
  waiting for transfers between devices  9.67 us (32%)
  Pallas kernels  7.53 us (25%)
    ppermute x6, starting transfers between devices, returned(): lax.ppermute(value, axis, [(peer_of(i, step, count), i) for i in range(co...  8.28 us
    ppermute x6, waiting for transfers between devices, returned(): lax.ppermute(value, axis, [(peer_of(i, step, count), i) for i in range(co...  7.97 us
    ppermute x3, starting transfers between devices, sent(): lax.ppermute(value, axis, [(i, peer_of(i, step, count)) for i in range(co...  4.16 us
    pallas_call x3, Pallas kernels, attended_for(): pl.pallas_call(functools.partial(attend_kernel, len(sources), n_ctx, kv_d...  3.81 us
    pallas_call x3, Pallas kernels, assembled(): pl.pallas_call(functools.partial(assemble_kernel, n_head, steps), out_sha...  2.05 us
    ppermute x3, waiting for transfers between devices, sent(): lax.ppermute(value, axis, [(i, peer_of(i, step, count)) for i in range(co...  1.7 us
    pallas_call x1, Pallas kernels, shards(): pl.pallas_call(functools.partial(dispatch_kernel, n_doc, n_ctx, cap), out...  1.43 us
  transfers between devices with their start and end apart: 10, of which 5 were waited for; matrix products, arithmetic and copies ran while one was open for 0% of the time, Pallas kernels for 17%

profile of v6, /device:TPU:0, one launch (start us, length us, event | category | flops | bytes accessed | tf_op | source)
XLA Modules:
  0.0 30.2 jit_solution(10554346569451625864)
XLA Ops:
  0.0 1.4 %shard_map.73 = (bf16[192,128]{1,0:T(8,128)(2,1)S(1)}, f32[2,1024]{1,0:T(2,128)S(1)}, bf16[2064,256]{1,0:T(8,128)(2,1)S(1)}, bf16[192,128]{1,0:T(8,128)(2,1)S(1)...) custom-call(s32[1,16]{1,0:T(1,128)} %bitcast.10, s32[1,4]{1,0:T(1,128)} %bitcast.11, ...), custom_call_target="tpu_custom_call" | custom-call | tf_op jit(solution)/shard_map/pallas_call | solution.py:307
  1.4 0.5 %collective-permute-start.1 = (bf16[2064,256]{1,0:T(8,128)(2,1)S(1)}, bf16[2064,256]{1,0:T(8,128)(2,1)S(1)}, u32[]{:S(2)}, u32[]{:S(2)}) collective-permute-start(bf16[2064,256]{1,0:T(8,128)(2,1)S(1)} %get-tuple-element.19.refs_1_.refs_2_), channel_id=1, source_target_pairs={{0,4},{4,0},{1,5},{5,1},{2,6},{6,2},{3,7},{7,3},{8,12},{12,8},{9,1... | collective-permute-start | bytes 3170312 | tf_op jit(solution)/shard_map/ppermute | solution.py:326
  2.0 3.5 %collective-permute-start = (bf16[192,128]{1,0:T(8,128)(2,1)S(1)}, bf16[192,128]{1,0:T(8,128)(2,1)S(1)}, u32[]{:S(2)}, u32[]{:S(2)}) collective-permute-start(bf16[192,128]{1,0:T(8,128)(2,1)S(1)} %get-tuple-element.18), channel_id=1, source_target_pairs={{0,24},{8,16},{16,8},{24,0},{1,25},{9,17},{17,9},{25,1},{2,26},{10... | collective-permute-start | bytes 147464 | tf_op jit(solution)/shard_map/ppermute | solution.py:24
  5.5 0.5 %collective-permute-start.2 = (bf16[192,128]{1,0:T(8,128)(2,1)S(1)}, bf16[192,128]{1,0:T(8,128)(2,1)S(1)}, u32[]{:S(2)}, u32[]{:S(2)}) collective-permute-start(bf16[192,128]{1,0:T(8,128)(2,1)S(1)} %get-tuple-element.22), channel_id=1, source_target_pairs={{0,8},{8,0},{16,24},{24,16},{1,9},{9,1},{17,25},{25,17},{2,10},{10... | collective-permute-start | bytes 147464 | tf_op jit(solution)/shard_map/ppermute | solution.py:24
  6.0 0.1 collective-permute-start.3
  6.1 1.7 %collective-permute-done.refs_0_ = bf16[192,128]{1,0:T(8,128)(2,1)S(1)} collective-permute-done((bf16[192,128]{1,0:T(8,128)(2,1)S(1)}, bf16[192,128]{1,0:T(8,128)(2,1)S(1)}, u32[]{:S(2)}, u32[]{:S(2)}) %collective-permute-start) | collective-permute-done | bytes 49184 | tf_op jit(solution)/shard_map/ppermute | solution.py:24
  7.8 1.1 %shard_map.74 = bf16[192,128]{1,0:T(8,128)(2,1)S(1)} custom-call(f32[2,1024]{1,0:T(2,128)S(1)} %get-tuple-element.20.valid_ref, bf16[192,128]{1,0:T(8,128)(2,1)S(1)} %collective-permute-done.refs_0_, bf16[2064,256]{1,0:T(8,128)(2,1)S(1)} %get-tuple-element.19.refs_1_.refs_2_, bf16[2064,256]{1,0:T(8,128)(2,1)S(1)} %collective-permute-done.1.refs_2_.refs_3_), custom_call_target="tpu_custom_call" | custom-call | flops 201326592 | bytes 2097152 | tf_op jit(solution)/shard_map/pallas_call | solution.py:333
  8.9 3.2 %collective-permute-start.6 = (bf16[192,128]{1,0:T(8,128)(2,1)S(1)}, bf16[192,128]{1,0:T(8,128)(2,1)S(1)}, u32[]{:S(2)}, u32[]{:S(2)}) collective-permute-start(bf16[192,128]{1,0:T(8,128)(2,1)S(1)} %shard_map.74), channel_id=1, source_target_pairs={{24,0},{16,8},{8,16},{0,24},{25,1},{17,9},{9,17},{1,25},{26,2},{18... | collective-permute-start | bytes 147464 | tf_op jit(solution)/shard_map/ppermute | solution.py:29
  12.1 0.0 collective-permute-done.2.refs_0_
  12.1 1.6 %shard_map.76 = (bf16[192,128]{1,0:T(8,128)(2,1)S(1)}, bf16[192,128]{1,0:T(8,128)(2,1)S(1)}) custom-call(f32[2,1024]{1,0:T(2,128)S(1)} %get-tuple-element.20.valid_ref, bf16[192,128]{1,0:T(8,128)(2,1)S(1)} %collective-permute-done.2.refs_0_, bf16[192,128]{1,0:T(8,128)(2,1)S(1)} %collective-permute-done.3.refs_1_, ...), custom_call_target="tpu_custom_call" | custom-call | flops 402653184 | bytes 2097152 | tf_op jit(solution)/shard_map/pallas_call | solution.py:333
  13.7 0.2 collective-permute-start.4
  13.9 0.4 %collective-permute-start.5 = (bf16[192,128]{1,0:T(8,128)(2,1)S(1)}, bf16[192,128]{1,0:T(8,128)(2,1)S(1)}, u32[]{:S(2)}, u32[]{:S(2)}) collective-permute-start(bf16[192,128]{1,0:T(8,128)(2,1)S(1)} %get-tuple-element.25), channel_id=1, source_target_pairs={{16,0},{24,8},{0,16},{8,24},{17,1},{25,9},{1,17},{9,25},{18,2},{26... | collective-permute-start | bytes 147464 | tf_op jit(solution)/shard_map/ppermute | solution.py:29
  14.4 1.1 %shard_map.75.refs_0_ = bf16[192,128]{1,0:T(8,128)(2,1)S(1)} custom-call(f32[2,1024]{1,0:T(2,128)S(1)} %get-tuple-element.20.valid_ref, bf16[192,128]{1,0:T(8,128)(2,1)S(1)} %get-tuple-element.21.refs_0_, bf16[2064,256]{1,0:T(8,128)(2,1)S(1)} %get-tuple-element.19.refs_1_.refs_2_, bf16[2064,256]{1,0:T(8,128)(2,1)S(1)} %collective-permute-done.1.refs_2_.refs_3_), custom_call_target="tpu_custom_call" | custom-call | flops 201326592 | bytes 2097152 | tf_op jit(solution)/shard_map/pallas_call | solution.py:333
  15.5 2.4 %collective-permute-done.4.refs_1_ = bf16[192,128]{1,0:T(8,128)(2,1)S(1)} collective-permute-done((bf16[192,128]{1,0:T(8,128)(2,1)S(1)}, bf16[192,128]{1,0:T(8,128)(2,1)S(1)}, u32[]{:S(2)}, u32[]{:S(2)}) %collective-permute-start.4) | collective-permute-done | bytes 49184 | tf_op jit(solution)/shard_map/ppermute | solution.py:29
  17.9 0.2 collective-permute-done.5.refs_2_
  18.0 0.2 shard_map.77.refs_0_
  18.3 2.6 %collective-permute-start.9 = (bf16[16,4096]{1,0:T(8,128)(2,1)S(1)}, bf16[16,4096]{1,0:T(8,128)(2,1)S(1)}, u32[]{:S(2)}, u32[]{:S(2)}) collective-permute-start(bf16[16,4096]{1,0:T(8,128)(2,1)S(1)} %shard_map.77.refs_0_), channel_id=1, source_target_pairs={{2,0},{3,1},{0,2},{1,3},{6,4},{7,5},{4,6},{5,7},{10,8},{11,9},{8,1... | collective-permute-start | bytes 393224 | tf_op jit(solution)/shard_map/ppermute | solution.py:29
  20.9 1.6 %collective-permute-start.8 = (bf16[16,4096]{1,0:T(8,128)(2,1)S(1)}, bf16[16,4096]{1,0:T(8,128)(2,1)S(1)}, u32[]{:S(2)}, u32[]{:S(2)}) collective-permute-start(bf16[16,4096]{1,0:T(8,128)(2,1)S(1)} %shard_map.77.refs_0_), channel_id=1, source_target_pairs={{1,0},{0,1},{3,2},{2,3},{5,4},{4,5},{7,6},{6,7},{9,8},{8,9},{11,10... | collective-permute-start | bytes 393224 | tf_op jit(solution)/shard_map/ppermute | solution.py:29
  22.5 0.2 collective-permute-start.7
  22.7 5.1 %collective-permute-done.9.refs_1_ = bf16[16,4096]{1,0:T(8,128)(2,1)S(1)} collective-permute-done((bf16[16,4096]{1,0:T(8,128)(2,1)S(1)}, bf16[16,4096]{1,0:T(8,128)(2,1)S(1)}, u32[]{:S(2)}, u32[]{:S(2)}) %collective-permute-start.9) | collective-permute-done | bytes 131104 | tf_op jit(solution)/shard_map/ppermute | solution.py:29
  27.9 0.7 %shard_map.78.refs_1_ = bf16[16,16384]{1,0:T(8,128)(2,1)} custom-call(bf16[16,4096]{1,0:T(8,128)(2,1)S(1)} %shard_map.77.refs_0_, bf16[16,4096]{1,0:T(8,128)(2,1)S(1)} %collective-permute-done.9.refs_1_), custom_call_target="tpu_custom_call" | custom-call | tf_op jit(solution)/shard_map/pallas_call | solution.py:364
  28.6 0.7 %shard_map.79.refs_1_ = bf16[16,16384]{1,0:T(8,128)(2,1)} custom-call(bf16[16,4096]{1,0:T(8,128)(2,1)S(1)} %collective-permute-done.8.refs_0_, bf16[16,16384]{1,0:T(8,128)(2,1)} %shard_map.78.refs_1_), custom_call_target="tpu_custom_call", output_to_operand_aliasing={{}: (1, {})} | custom-call | tf_op jit(solution)/shard_map/pallas_call | solution.py:364
  29.3 0.3 collective-permute-done.7.refs_0_
  29.6 0.7 %shard_map.80 = bf16[16,16384]{1,0:T(8,128)(2,1)} custom-call(bf16[16,4096]{1,0:T(8,128)(2,1)S(1)} %collective-permute-done.7.refs_0_, bf16[16,16384]{1,0:T(8,128)(2,1)} %shard_map.79.refs_1_), custom_call_target="tpu_custom_call", output_to_operand_aliasing={{}: (1, {})} | custom-call | tf_op jit(solution)/shard_map/pallas_call | solution.py:364
  (4 shorter events, 0.0 us)
Async XLA Ops:
  1.4 6.4 %collective-permute-start.1 = (bf16[2064,256]{1,0:T(8,128)(2,1)S(1)}, bf16[2064,256]{1,0:T(8,128)(2,1)S(1)}, u32[]{:S(2)}, u32[]{:S(2)}) collective-permute-start(bf16[2064,256]{1,0:T(8,128)(2,1)S(1)} %get-tuple-element.19.refs_1_.refs_2_), channel_id=1, source_target_pairs={{0,4},{4,0},{1,5},{5,1},{2,6},{6,2},{3,7},{7,3},{8,12},{12,8},{9,1... | collective-permute-start | bytes 3170312 | tf_op jit(solution)/shard_map/ppermute | solution.py:326
  2.0 5.9 %collective-permute-start = (bf16[192,128]{1,0:T(8,128)(2,1)S(1)}, bf16[192,128]{1,0:T(8,128)(2,1)S(1)}, u32[]{:S(2)}, u32[]{:S(2)}) collective-permute-start(bf16[192,128]{1,0:T(8,128)(2,1)S(1)} %get-tuple-element.18), channel_id=1, source_target_pairs={{0,24},{8,16},{16,8},{24,0},{1,25},{9,17},{17,9},{25,1},{2,26},{10... | collective-permute-start | bytes 147464 | tf_op jit(solution)/shard_map/ppermute | solution.py:24
  5.5 6.6 %collective-permute-start.2 = (bf16[192,128]{1,0:T(8,128)(2,1)S(1)}, bf16[192,128]{1,0:T(8,128)(2,1)S(1)}, u32[]{:S(2)}, u32[]{:S(2)}) collective-permute-start(bf16[192,128]{1,0:T(8,128)(2,1)S(1)} %get-tuple-element.22), channel_id=1, source_target_pairs={{0,8},{8,0},{16,24},{24,16},{1,9},{9,1},{17,25},{25,17},{2,10},{10... | collective-permute-start | bytes 147464 | tf_op jit(solution)/shard_map/ppermute | solution.py:24
  6.0 6.1 %collective-permute-start.3 = (bf16[192,128]{1,0:T(8,128)(2,1)S(1)}, bf16[192,128]{1,0:T(8,128)(2,1)S(1)}, u32[]{:S(2)}, u32[]{:S(2)}) collective-permute-start(bf16[192,128]{1,0:T(8,128)(2,1)S(1)} %get-tuple-element.23), channel_id=1, source_target_pairs={{0,16},{8,24},{16,0},{24,8},{1,17},{9,25},{17,1},{25,9},{2,18},{10... | collective-permute-start | bytes 147464 | tf_op jit(solution)/shard_map/ppermute | solution.py:24
  8.9 6.6 %collective-permute-start.6 = (bf16[192,128]{1,0:T(8,128)(2,1)S(1)}, bf16[192,128]{1,0:T(8,128)(2,1)S(1)}, u32[]{:S(2)}, u32[]{:S(2)}) collective-permute-start(bf16[192,128]{1,0:T(8,128)(2,1)S(1)} %shard_map.74), channel_id=1, source_target_pairs={{24,0},{16,8},{8,16},{0,24},{25,1},{17,9},{9,17},{1,25},{26,2},{18... | collective-permute-start | bytes 147464 | tf_op jit(solution)/shard_map/ppermute | solution.py:29
  13.7 4.2 %collective-permute-start.4 = (bf16[192,128]{1,0:T(8,128)(2,1)S(1)}, bf16[192,128]{1,0:T(8,128)(2,1)S(1)}, u32[]{:S(2)}, u32[]{:S(2)}) collective-permute-start(bf16[192,128]{1,0:T(8,128)(2,1)S(1)} %get-tuple-element.24), channel_id=1, source_target_pairs={{8,0},{0,8},{24,16},{16,24},{9,1},{1,9},{25,17},{17,25},{10,2},{2,... | collective-permute-start | bytes 147464 | tf_op jit(solution)/shard_map/ppermute | solution.py:29
  13.9 4.1 %collective-permute-start.5 = (bf16[192,128]{1,0:T(8,128)(2,1)S(1)}, bf16[192,128]{1,0:T(8,128)(2,1)S(1)}, u32[]{:S(2)}, u32[]{:S(2)}) collective-permute-start(bf16[192,128]{1,0:T(8,128)(2,1)S(1)} %get-tuple-element.25), channel_id=1, source_target_pairs={{16,0},{24,8},{0,16},{8,24},{17,1},{25,9},{1,17},{9,25},{18,2},{26... | collective-permute-start | bytes 147464 | tf_op jit(solution)/shard_map/ppermute | solution.py:29
  18.3 9.6 %collective-permute-start.9 = (bf16[16,4096]{1,0:T(8,128)(2,1)S(1)}, bf16[16,4096]{1,0:T(8,128)(2,1)S(1)}, u32[]{:S(2)}, u32[]{:S(2)}) collective-permute-start(bf16[16,4096]{1,0:T(8,128)(2,1)S(1)} %shard_map.77.refs_0_), channel_id=1, source_target_pairs={{2,0},{3,1},{0,2},{1,3},{6,4},{7,5},{4,6},{5,7},{10,8},{11,9},{8,1... | collective-permute-start | bytes 393224 | tf_op jit(solution)/shard_map/ppermute | solution.py:29
  20.9 7.7 %collective-permute-start.8 = (bf16[16,4096]{1,0:T(8,128)(2,1)S(1)}, bf16[16,4096]{1,0:T(8,128)(2,1)S(1)}, u32[]{:S(2)}, u32[]{:S(2)}) collective-permute-start(bf16[16,4096]{1,0:T(8,128)(2,1)S(1)} %shard_map.77.refs_0_), channel_id=1, source_target_pairs={{1,0},{0,1},{3,2},{2,3},{5,4},{4,5},{7,6},{6,7},{9,8},{8,9},{11,10... | collective-permute-start | bytes 393224 | tf_op jit(solution)/shard_map/ppermute | solution.py:29
  22.5 7.1 %collective-permute-start.7 = (bf16[16,4096]{1,0:T(8,128)(2,1)S(1)}, bf16[16,4096]{1,0:T(8,128)(2,1)S(1)}, u32[]{:S(2)}, u32[]{:S(2)}) collective-permute-start(bf16[16,4096]{1,0:T(8,128)(2,1)S(1)} %shard_map.77.refs_0_), channel_id=1, source_target_pairs={{3,0},{2,1},{1,2},{0,3},{7,4},{6,5},{5,6},{4,7},{11,8},{10,9},{9,1... | collective-permute-start | bytes 393224 | tf_op jit(solution)/shard_map/ppermute | solution.py:29

commit v7 on v6

--- a/solution.py
+++ b/solution.py
@@ -155,6 +155,10 @@
         copy.wait()
 
 
+def turn_kernel(placing_ref, after_ref, out_ref):
+    out_ref[...] = placing_ref[...].astype(jnp.float32).T.astype(jnp.bfloat16)
+
+
 def collect_kernel(n_doc, cap, placing_ref, *refs):
     back_refs, out_ref = refs[:n_doc], refs[n_doc]
     rows, width = out_ref.shape
@@ -166,9 +170,7 @@
         slots = jnp.concatenate(
             [back_refs[k][g * block : (g + 1) * block, :] for k in range(n_doc)], axis=0
         )
-        mine = lax.dot_general(
-            placing, slots, (((0,), (0,)), ((), ())), preferred_element_type=jnp.float32
-        ).astype(jnp.bfloat16)
+        mine = jnp.dot(placing, slots, preferred_element_type=jnp.float32).astype(jnp.bfloat16)
         for h in range(group):
             at = (g * group + h) * HEAD_WIDTH
             out_ref[:, at : at + HEAD_WIDTH] = mine[h * rows : (h + 1) * rows]
@@ -352,13 +354,20 @@
     finished[0] = attended_for((0,), valid)[0]
     back = [finished[0]] + [returned(finished[k], "doc", k) for k in range(1, n_doc)]
 
+    turned = pl.pallas_call(
+        turn_kernel,
+        out_shape=jax.ShapeDtypeStruct(placing.shape[::-1], placing.dtype),
+        in_specs=[vmem, anywhere],
+        out_specs=vmem,
+        compiler_params=params,
+    )(placing, finished[0])
     mine = pl.pallas_call(
         functools.partial(collect_kernel, n_doc, cap),
         out_shape=jax.ShapeDtypeStruct((rows_home, width), jnp.bfloat16),
         in_specs=[vmem] * (1 + n_doc),
         out_specs=vmem,
         compiler_params=params,
-    )(placing, *back)
+    )(turned, *back)
 
     def assembled(steps, before):
         return pl.pallas_call(

time: 30.4 us -> 30.4 us (level)
  transfers between devices with their start and end apart: 10 -> 10, of which waited for: 5 -> 5; matrix products, arithmetic and copies ran while one was open for 0% -> 0% of each run, Pallas kernels for 17% -> 18%
where the time goes in v7:
time: 30.4 us; the launch traced here: 30.2 us
  starting transfers between devices  13 us (43%)
  waiting for transfers between devices  9.57 us (31%)
  Pallas kernels  7.59 us (25%)
    ppermute x6, starting transfers between devices, returned(): lax.ppermute(value, axis, [(peer_of(i, step, count), i) for i in range(co...  8.28 us
    ppermute x6, waiting for transfers between devices, returned(): lax.ppermute(value, axis, [(peer_of(i, step, count), i) for i in range(co...  7.87 us
    ppermute x3, starting transfers between devices, sent(): lax.ppermute(value, axis, [(i, peer_of(i, step, count)) for i in range(co...  4.16 us
    pallas_call x3, Pallas kernels, attended_for(): pl.pallas_call(functools.partial(attend_kernel, len(sources), n_ctx, kv_d...  3.81 us
    pallas_call x3, Pallas kernels, assembled(): pl.pallas_call(functools.partial(assemble_kernel, n_head, steps), out_sha...  2.05 us
    ppermute x3, waiting for transfers between devices, sent(): lax.ppermute(value, axis, [(i, peer_of(i, step, count)) for i in range(co...  1.7 us
    pallas_call x1, Pallas kernels, shards(): pl.pallas_call(functools.partial(dispatch_kernel, n_doc, n_ctx, cap), out...  1.43 us
  transfers between devices with their start and end apart: 10, of which 5 were waited for; matrix products, arithmetic and copies ran while one was open for 0% of the time, Pallas kernels for 18%

profile of v7, /device:TPU:0, one launch (start us, length us, event | category | flops | bytes accessed | tf_op | source)
XLA Modules:
  0.0 30.2 jit_solution(16885419067078010328)
XLA Ops:
  0.0 1.4 %shard_map.73 = (bf16[192,128]{1,0:T(8,128)(2,1)S(1)}, f32[2,1024]{1,0:T(2,128)S(1)}, bf16[2064,256]{1,0:T(8,128)(2,1)S(1)}, bf16[192,128]{1,0:T(8,128)(2,1)S(1)...) custom-call(s32[1,16]{1,0:T(1,128)} %bitcast.10, s32[1,4]{1,0:T(1,128)} %bitcast.11, ...), custom_call_target="tpu_custom_call" | custom-call | tf_op jit(solution)/shard_map/pallas_call | solution.py:309
  1.4 0.5 %collective-permute-start.1 = (bf16[2064,256]{1,0:T(8,128)(2,1)S(1)}, bf16[2064,256]{1,0:T(8,128)(2,1)S(1)}, u32[]{:S(2)}, u32[]{:S(2)}) collective-permute-start(bf16[2064,256]{1,0:T(8,128)(2,1)S(1)} %get-tuple-element.19.refs_1_.refs_2_), channel_id=1, source_target_pairs={{0,4},{4,0},{1,5},{5,1},{2,6},{6,2},{3,7},{7,3},{8,12},{12,8},{9,1... | collective-permute-start | bytes 3170312 | tf_op jit(solution)/shard_map/ppermute | solution.py:328
  2.0 3.5 %collective-permute-start = (bf16[192,128]{1,0:T(8,128)(2,1)S(1)}, bf16[192,128]{1,0:T(8,128)(2,1)S(1)}, u32[]{:S(2)}, u32[]{:S(2)}) collective-permute-start(bf16[192,128]{1,0:T(8,128)(2,1)S(1)} %get-tuple-element.18), channel_id=1, source_target_pairs={{0,24},{8,16},{16,8},{24,0},{1,25},{9,17},{17,9},{25,1},{2,26},{10... | collective-permute-start | bytes 147464 | tf_op jit(solution)/shard_map/ppermute | solution.py:24
  5.5 0.5 %collective-permute-start.2 = (bf16[192,128]{1,0:T(8,128)(2,1)S(1)}, bf16[192,128]{1,0:T(8,128)(2,1)S(1)}, u32[]{:S(2)}, u32[]{:S(2)}) collective-permute-start(bf16[192,128]{1,0:T(8,128)(2,1)S(1)} %get-tuple-element.22), channel_id=1, source_target_pairs={{0,8},{8,0},{16,24},{24,16},{1,9},{9,1},{17,25},{25,17},{2,10},{10... | collective-permute-start | bytes 147464 | tf_op jit(solution)/shard_map/ppermute | solution.py:24
  6.0 0.1 collective-permute-start.3
  6.1 1.7 %collective-permute-done.refs_0_ = bf16[192,128]{1,0:T(8,128)(2,1)S(1)} collective-permute-done((bf16[192,128]{1,0:T(8,128)(2,1)S(1)}, bf16[192,128]{1,0:T(8,128)(2,1)S(1)}, u32[]{:S(2)}, u32[]{:S(2)}) %collective-permute-start) | collective-permute-done | bytes 49184 | tf_op jit(solution)/shard_map/ppermute | solution.py:24
  7.8 1.1 %shard_map.74 = bf16[192,128]{1,0:T(8,128)(2,1)S(1)} custom-call(f32[2,1024]{1,0:T(2,128)S(1)} %get-tuple-element.20.valid_ref, bf16[192,128]{1,0:T(8,128)(2,1)S(1)} %collective-permute-done.refs_0_, bf16[2064,256]{1,0:T(8,128)(2,1)S(1)} %get-tuple-element.19.refs_1_.refs_2_, bf16[2064,256]{1,0:T(8,128)(2,1)S(1)} %collective-permute-done.1.refs_2_.refs_3_), custom_call_target="tpu_custom_call" | custom-call | flops 201326592 | bytes 2097152 | tf_op jit(solution)/shard_map/pallas_call | solution.py:335
  8.9 3.2 %collective-permute-start.6 = (bf16[192,128]{1,0:T(8,128)(2,1)S(1)}, bf16[192,128]{1,0:T(8,128)(2,1)S(1)}, u32[]{:S(2)}, u32[]{:S(2)}) collective-permute-start(bf16[192,128]{1,0:T(8,128)(2,1)S(1)} %shard_map.74), channel_id=1, source_target_pairs={{24,0},{16,8},{8,16},{0,24},{25,1},{17,9},{9,17},{1,25},{26,2},{18... | collective-permute-start | bytes 147464 | tf_op jit(solution)/shard_map/ppermute | solution.py:29
  12.1 1.6 %shard_map.77 = (bf16[192,128]{1,0:T(8,128)(2,1)S(1)}, bf16[192,128]{1,0:T(8,128)(2,1)S(1)}) custom-call(f32[2,1024]{1,0:T(2,128)S(1)} %get-tuple-element.20.valid_ref, bf16[192,128]{1,0:T(8,128)(2,1)S(1)} %collective-permute-done.2.refs_0_, bf16[192,128]{1,0:T(8,128)(2,1)S(1)} %collective-permute-done.3.refs_1_, ...), custom_call_target="tpu_custom_call" | custom-call | flops 402653184 | bytes 2097152 | tf_op jit(solution)/shard_map/pallas_call | solution.py:335
  13.7 0.2 collective-permute-start.4
  13.9 0.4 %collective-permute-start.5 = (bf16[192,128]{1,0:T(8,128)(2,1)S(1)}, bf16[192,128]{1,0:T(8,128)(2,1)S(1)}, u32[]{:S(2)}, u32[]{:S(2)}) collective-permute-start(bf16[192,128]{1,0:T(8,128)(2,1)S(1)} %get-tuple-element.25), channel_id=1, source_target_pairs={{16,0},{24,8},{0,16},{8,24},{17,1},{25,9},{1,17},{9,25},{18,2},{26... | collective-permute-start | bytes 147464 | tf_op jit(solution)/shard_map/ppermute | solution.py:29
  14.4 1.1 %shard_map.75.after_ref.refs_0_ = bf16[192,128]{1,0:T(8,128)(2,1)S(1)} custom-call(f32[2,1024]{1,0:T(2,128)S(1)} %get-tuple-element.20.valid_ref, bf16[192,128]{1,0:T(8,128)(2,1)S(1)} %get-tuple-element.21.refs_0_, bf16[2064,256]{1,0:T(8,128)(2,1)S(1)} %get-tuple-element.19.refs_1_.refs_2_, bf16[2064,256]{1,0:T(8,128)(2,1)S(1)} %collective-permute-done.1.refs_2_.refs_3_), custom_call_target="tpu_custom_call" | custom-call | flops 201326592 | bytes 2097152 | tf_op jit(solution)/shard_map/pallas_call | solution.py:335
  15.5 0.1 shard_map.76.placing_ref
  15.6 2.3 %collective-permute-done.4.refs_1_ = bf16[192,128]{1,0:T(8,128)(2,1)S(1)} collective-permute-done((bf16[192,128]{1,0:T(8,128)(2,1)S(1)}, bf16[192,128]{1,0:T(8,128)(2,1)S(1)}, u32[]{:S(2)}, u32[]{:S(2)}) %collective-permute-start.4) | collective-permute-done | bytes 49184 | tf_op jit(solution)/shard_map/ppermute | solution.py:29
  17.9 0.2 collective-permute-done.5.refs_2_
  18.0 0.2 shard_map.78.refs_0_
  18.3 2.6 %collective-permute-start.9 = (bf16[16,4096]{1,0:T(8,128)(2,1)S(1)}, bf16[16,4096]{1,0:T(8,128)(2,1)S(1)}, u32[]{:S(2)}, u32[]{:S(2)}) collective-permute-start(bf16[16,4096]{1,0:T(8,128)(2,1)S(1)} %shard_map.78.refs_0_), channel_id=1, source_target_pairs={{2,0},{3,1},{0,2},{1,3},{6,4},{7,5},{4,6},{5,7},{10,8},{11,9},{8,1... | collective-permute-start | bytes 393224 | tf_op jit(solution)/shard_map/ppermute | solution.py:29
  20.9 1.6 %collective-permute-start.8 = (bf16[16,4096]{1,0:T(8,128)(2,1)S(1)}, bf16[16,4096]{1,0:T(8,128)(2,1)S(1)}, u32[]{:S(2)}, u32[]{:S(2)}) collective-permute-start(bf16[16,4096]{1,0:T(8,128)(2,1)S(1)} %shard_map.78.refs_0_), channel_id=1, source_target_pairs={{1,0},{0,1},{3,2},{2,3},{5,4},{4,5},{7,6},{6,7},{9,8},{8,9},{11,10... | collective-permute-start | bytes 393224 | tf_op jit(solution)/shard_map/ppermute | solution.py:29
  22.5 0.2 collective-permute-start.7
  22.7 5.1 %collective-permute-done.9.refs_1_ = bf16[16,4096]{1,0:T(8,128)(2,1)S(1)} collective-permute-done((bf16[16,4096]{1,0:T(8,128)(2,1)S(1)}, bf16[16,4096]{1,0:T(8,128)(2,1)S(1)}, u32[]{:S(2)}, u32[]{:S(2)}) %collective-permute-start.9) | collective-permute-done | bytes 131104 | tf_op jit(solution)/shard_map/ppermute | solution.py:29
  27.8 0.7 %shard_map.79.refs_1_ = bf16[16,16384]{1,0:T(8,128)(2,1)} custom-call(bf16[16,4096]{1,0:T(8,128)(2,1)S(1)} %shard_map.78.refs_0_, bf16[16,4096]{1,0:T(8,128)(2,1)S(1)} %collective-permute-done.9.refs_1_), custom_call_target="tpu_custom_call" | custom-call | tf_op jit(solution)/shard_map/pallas_call | solution.py:373
  28.6 0.7 %shard_map.80.refs_1_ = bf16[16,16384]{1,0:T(8,128)(2,1)} custom-call(bf16[16,4096]{1,0:T(8,128)(2,1)S(1)} %collective-permute-done.8.refs_0_, bf16[16,16384]{1,0:T(8,128)(2,1)} %shard_map.79.refs_1_), custom_call_target="tpu_custom_call", output_to_operand_aliasing={{}: (1, {})} | custom-call | tf_op jit(solution)/shard_map/pallas_call | solution.py:373
  29.2 0.3 collective-permute-done.7.refs_0_
  29.5 0.7 %shard_map.81 = bf16[16,16384]{1,0:T(8,128)(2,1)} custom-call(bf16[16,4096]{1,0:T(8,128)(2,1)S(1)} %collective-permute-done.7.refs_0_, bf16[16,16384]{1,0:T(8,128)(2,1)} %shard_map.80.refs_1_), custom_call_target="tpu_custom_call", output_to_operand_aliasing={{}: (1, {})} | custom-call | tf_op jit(solution)/shard_map/pallas_call | solution.py:373
  (5 shorter events, 0.0 us)
Async XLA Ops:
  1.4 6.4 %collective-permute-start.1 = (bf16[2064,256]{1,0:T(8,128)(2,1)S(1)}, bf16[2064,256]{1,0:T(8,128)(2,1)S(1)}, u32[]{:S(2)}, u32[]{:S(2)}) collective-permute-start(bf16[2064,256]{1,0:T(8,128)(2,1)S(1)} %get-tuple-element.19.refs_1_.refs_2_), channel_id=1, source_target_pairs={{0,4},{4,0},{1,5},{5,1},{2,6},{6,2},{3,7},{7,3},{8,12},{12,8},{9,1... | collective-permute-start | bytes 3170312 | tf_op jit(solution)/shard_map/ppermute | solution.py:328
  2.0 5.9 %collective-permute-start = (bf16[192,128]{1,0:T(8,128)(2,1)S(1)}, bf16[192,128]{1,0:T(8,128)(2,1)S(1)}, u32[]{:S(2)}, u32[]{:S(2)}) collective-permute-start(bf16[192,128]{1,0:T(8,128)(2,1)S(1)} %get-tuple-element.18), channel_id=1, source_target_pairs={{0,24},{8,16},{16,8},{24,0},{1,25},{9,17},{17,9},{25,1},{2,26},{10... | collective-permute-start | bytes 147464 | tf_op jit(solution)/shard_map/ppermute | solution.py:24
  5.5 6.6 %collective-permute-start.2 = (bf16[192,128]{1,0:T(8,128)(2,1)S(1)}, bf16[192,128]{1,0:T(8,128)(2,1)S(1)}, u32[]{:S(2)}, u32[]{:S(2)}) collective-permute-start(bf16[192,128]{1,0:T(8,128)(2,1)S(1)} %get-tuple-element.22), channel_id=1, source_target_pairs={{0,8},{8,0},{16,24},{24,16},{1,9},{9,1},{17,25},{25,17},{2,10},{10... | collective-permute-start | bytes 147464 | tf_op jit(solution)/shard_map/ppermute | solution.py:24
  6.0 6.1 %collective-permute-start.3 = (bf16[192,128]{1,0:T(8,128)(2,1)S(1)}, bf16[192,128]{1,0:T(8,128)(2,1)S(1)}, u32[]{:S(2)}, u32[]{:S(2)}) collective-permute-start(bf16[192,128]{1,0:T(8,128)(2,1)S(1)} %get-tuple-element.23), channel_id=1, source_target_pairs={{0,16},{8,24},{16,0},{24,8},{1,17},{9,25},{17,1},{25,9},{2,18},{10... | collective-permute-start | bytes 147464 | tf_op jit(solution)/shard_map/ppermute | solution.py:24
  8.9 6.7 %collective-permute-start.6 = (bf16[192,128]{1,0:T(8,128)(2,1)S(1)}, bf16[192,128]{1,0:T(8,128)(2,1)S(1)}, u32[]{:S(2)}, u32[]{:S(2)}) collective-permute-start(bf16[192,128]{1,0:T(8,128)(2,1)S(1)} %shard_map.74), channel_id=1, source_target_pairs={{24,0},{16,8},{8,16},{0,24},{25,1},{17,9},{9,17},{1,25},{26,2},{18... | collective-permute-start | bytes 147464 | tf_op jit(solution)/shard_map/ppermute | solution.py:29
  13.7 4.2 %collective-permute-start.4 = (bf16[192,128]{1,0:T(8,128)(2,1)S(1)}, bf16[192,128]{1,0:T(8,128)(2,1)S(1)}, u32[]{:S(2)}, u32[]{:S(2)}) collective-permute-start(bf16[192,128]{1,0:T(8,128)(2,1)S(1)} %get-tuple-element.24), channel_id=1, source_target_pairs={{8,0},{0,8},{24,16},{16,24},{9,1},{1,9},{25,17},{17,25},{10,2},{2,... | collective-permute-start | bytes 147464 | tf_op jit(solution)/shard_map/ppermute | solution.py:29
  13.9 4.1 %collective-permute-start.5 = (bf16[192,128]{1,0:T(8,128)(2,1)S(1)}, bf16[192,128]{1,0:T(8,128)(2,1)S(1)}, u32[]{:S(2)}, u32[]{:S(2)}) collective-permute-start(bf16[192,128]{1,0:T(8,128)(2,1)S(1)} %get-tuple-element.25), channel_id=1, source_target_pairs={{16,0},{24,8},{0,16},{8,24},{17,1},{25,9},{1,17},{9,25},{18,2},{26... | collective-permute-start | bytes 147464 | tf_op jit(solution)/shard_map/ppermute | solution.py:29
  18.3 9.6 %collective-permute-start.9 = (bf16[16,4096]{1,0:T(8,128)(2,1)S(1)}, bf16[16,4096]{1,0:T(8,128)(2,1)S(1)}, u32[]{:S(2)}, u32[]{:S(2)}) collective-permute-start(bf16[16,4096]{1,0:T(8,128)(2,1)S(1)} %shard_map.78.refs_0_), channel_id=1, source_target_pairs={{2,0},{3,1},{0,2},{1,3},{6,4},{7,5},{4,6},{5,7},{10,8},{11,9},{8,1... | collective-permute-start | bytes 393224 | tf_op jit(solution)/shard_map/ppermute | solution.py:29
  20.9 7.7 %collective-permute-start.8 = (bf16[16,4096]{1,0:T(8,128)(2,1)S(1)}, bf16[16,4096]{1,0:T(8,128)(2,1)S(1)}, u32[]{:S(2)}, u32[]{:S(2)}) collective-permute-start(bf16[16,4096]{1,0:T(8,128)(2,1)S(1)} %shard_map.78.refs_0_), channel_id=1, source_target_pairs={{1,0},{0,1},{3,2},{2,3},{5,4},{4,5},{7,6},{6,7},{9,8},{8,9},{11,10... | collective-permute-start | bytes 393224 | tf_op jit(solution)/shard_map/ppermute | solution.py:29
  22.5 7.1 %collective-permute-start.7 = (bf16[16,4096]{1,0:T(8,128)(2,1)S(1)}, bf16[16,4096]{1,0:T(8,128)(2,1)S(1)}, u32[]{:S(2)}, u32[]{:S(2)}) collective-permute-start(bf16[16,4096]{1,0:T(8,128)(2,1)S(1)} %shard_map.78.refs_0_), channel_id=1, source_target_pairs={{3,0},{2,1},{1,2},{0,3},{7,4},{6,5},{5,6},{4,7},{11,8},{10,9},{9,1... | collective-permute-start | bytes 393224 | tf_op jit(solution)/shard_map/ppermute | solution.py:29

commit v8 on v7

--- a/solution.py
+++ b/solution.py
@@ -346,11 +346,9 @@
         )(valid, *sources, *cache)
 
     finished = {}
-    for steps in (range(1, n_doc - 1), range(max(1, n_doc - 1), n_doc)):
-        if len(steps) > 0:
-            finished.update(zip(steps, attended_for(steps, valid)))
-    if n_doc > 1:
-        finished[n_doc - 1], valid = lax.optimization_barrier((finished[n_doc - 1], valid))
+    for step in sorted(range(1, n_doc), key=lambda step: (step % 2, step)):
+        finished[step] = attended_for((step,), valid)[0]
+        finished[step], valid = lax.optimization_barrier((finished[step], valid))
     finished[0] = attended_for((0,), valid)[0]
     back = [finished[0]] + [returned(finished[k], "doc", k) for k in range(1, n_doc)]
 

time: 30.4 us -> 30.4 us (level)
  Pallas kernels: 7.59 us -> 8.16 us
    ppermute x6, waiting for transfers between devices: 7.87 us -> 6.6 us  [returned(): lax.ppermute(value, axis, [(peer_of(i, step, count), i) for i in range(co...]
    ppermute x3, waiting for transfers between devices: 1.7 us -> 2.73 us  [sent(): lax.ppermute(value, axis, [(i, peer_of(i, step, count)) for i in range(co...]
    pallas_call x3 -> x4, Pallas kernels: 3.81 us -> 4.37 us  [attended_for(): pl.pallas_call(functools.partial(attend_kernel, len(sources), n_ctx, kv_d...]
  transfers between devices with their start and end apart: 10 -> 10, of which waited for: 5 -> 7; matrix products, arithmetic and copies ran while one was open for 0% -> 0% of each run, Pallas kernels for 18% -> 16%
where the time goes in v8:
time: 30.4 us; the launch traced here: 30.2 us
  starting transfers between devices  12.7 us (42%)
  waiting for transfers between devices  9.34 us (31%)
  Pallas kernels  8.16 us (27%)
    ppermute x6, starting transfers between devices, returned(): lax.ppermute(value, axis, [(peer_of(i, step, count), i) for i in range(co...  8.01 us
    ppermute x6, waiting for transfers between devices, returned(): lax.ppermute(value, axis, [(peer_of(i, step, count), i) for i in range(co...  6.6 us
    pallas_call x4, Pallas kernels, attended_for(): pl.pallas_call(functools.partial(attend_kernel, len(sources), n_ctx, kv_d...  4.37 us
    ppermute x3, starting transfers between devices, sent(): lax.ppermute(value, axis, [(i, peer_of(i, step, count)) for i in range(co...  4.13 us
    ppermute x3, waiting for transfers between devices, sent(): lax.ppermute(value, axis, [(i, peer_of(i, step, count)) for i in range(co...  2.73 us
    pallas_call x3, Pallas kernels, assembled(): pl.pallas_call(functools.partial(assemble_kernel, n_head, steps), out_sha...  2.05 us
    pallas_call x1, Pallas kernels, shards(): pl.pallas_call(functools.partial(dispatch_kernel, n_doc, n_ctx, cap), out...  1.43 us
  transfers between devices with their start and end apart: 10, of which 7 were waited for; matrix products, arithmetic and copies ran while one was open for 0% of the time, Pallas kernels for 16%

profile of v8, /device:TPU:0, one launch (start us, length us, event | category | flops | bytes accessed | tf_op | source)
XLA Modules:
  0.0 30.2 jit_solution(1705517745717590209)
XLA Ops:
  0.0 1.4 %shard_map.73 = (bf16[192,128]{1,0:T(8,128)(2,1)S(1)}, f32[2,1024]{1,0:T(2,128)S(1)}, bf16[2064,256]{1,0:T(8,128)(2,1)S(1)}, bf16[192,128]{1,0:T(8,128)(2,1)S(1)...) custom-call(s32[1,16]{1,0:T(1,128)} %bitcast.10, s32[1,4]{1,0:T(1,128)} %bitcast.11, ...), custom_call_target="tpu_custom_call" | custom-call | tf_op jit(solution)/shard_map/pallas_call | solution.py:309
  1.4 0.5 %collective-permute-start.1 = (bf16[2064,256]{1,0:T(8,128)(2,1)S(1)}, bf16[2064,256]{1,0:T(8,128)(2,1)S(1)}, u32[]{:S(2)}, u32[]{:S(2)}) collective-permute-start(bf16[2064,256]{1,0:T(8,128)(2,1)S(1)} %get-tuple-element.21.refs_1_), channel_id=1, source_target_pairs={{0,4},{4,0},{1,5},{5,1},{2,6},{6,2},{3,7},{7,3},{8,12},{12,8},{9,1... | collective-permute-start | bytes 3170312 | tf_op jit(solution)/shard_map/ppermute | solution.py:328
  2.0 2.6 %collective-permute-start = (bf16[192,128]{1,0:T(8,128)(2,1)S(1)}, bf16[192,128]{1,0:T(8,128)(2,1)S(1)}, u32[]{:S(2)}, u32[]{:S(2)}) collective-permute-start(bf16[192,128]{1,0:T(8,128)(2,1)S(1)} %get-tuple-element.20), channel_id=1, source_target_pairs={{0,16},{8,24},{16,0},{24,8},{1,17},{9,25},{17,1},{25,9},{2,18},{10... | collective-permute-start | bytes 147464 | tf_op jit(solution)/shard_map/ppermute | solution.py:24
  4.5 1.5 %collective-permute-start.2 = (bf16[192,128]{1,0:T(8,128)(2,1)S(1)}, bf16[192,128]{1,0:T(8,128)(2,1)S(1)}, u32[]{:S(2)}, u32[]{:S(2)}) collective-permute-start(bf16[192,128]{1,0:T(8,128)(2,1)S(1)} %get-tuple-element.23), channel_id=1, source_target_pairs={{0,8},{8,0},{16,24},{24,16},{1,9},{9,1},{17,25},{25,17},{2,10},{10... | collective-permute-start | bytes 147464 | tf_op jit(solution)/shard_map/ppermute | solution.py:24
  6.1 0.8 %collective-permute-done.refs_0_ = bf16[192,128]{1,0:T(8,128)(2,1)S(1)} collective-permute-done((bf16[192,128]{1,0:T(8,128)(2,1)S(1)}, bf16[192,128]{1,0:T(8,128)(2,1)S(1)}, u32[]{:S(2)}, u32[]{:S(2)}) %collective-permute-start) | collective-permute-done | bytes 49184 | tf_op jit(solution)/shard_map/ppermute | solution.py:24
  6.9 1.1 %shard_map.74 = bf16[192,128]{1,0:T(8,128)(2,1)S(1)} custom-call(f32[2,1024]{1,0:T(2,128)S(1)} %get-tuple-element.26.valid_ref, bf16[192,128]{1,0:T(8,128)(2,1)S(1)} %collective-permute-done.refs_0_, bf16[2064,256]{1,0:T(8,128)(2,1)S(1)} %get-tuple-element.21.refs_1_, bf16[2064,256]{1,0:T(8,128)(2,1)S(1)} %collective-permute-done.1.refs_2_), custom_call_target="tpu_custom_call" | custom-call | flops 201326592 | bytes 2097152 | tf_op jit(solution)/shard_map/pallas_call | solution.py:335
  8.0 0.9 %collective-permute-done.2.refs_0_ = bf16[192,128]{1,0:T(8,128)(2,1)S(1)} collective-permute-done((bf16[192,128]{1,0:T(8,128)(2,1)S(1)}, bf16[192,128]{1,0:T(8,128)(2,1)S(1)}, u32[]{:S(2)}, u32[]{:S(2)}) %collective-permute-start.2) | collective-permute-done | bytes 49184 | tf_op jit(solution)/shard_map/ppermute | solution.py:24
  8.9 1.1 %shard_map.75 = bf16[192,128]{1,0:T(8,128)(2,1)S(1)} custom-call(f32[2,1024]{1,0:T(2,128)S(1)} %get-tuple-element.26.valid_ref, bf16[192,128]{1,0:T(8,128)(2,1)S(1)} %collective-permute-done.2.refs_0_, bf16[2064,256]{1,0:T(8,128)(2,1)S(1)} %get-tuple-element.21.refs_1_, bf16[2064,256]{1,0:T(8,128)(2,1)S(1)} %collective-permute-done.1.refs_2_), custom_call_target="tpu_custom_call" | custom-call | flops 201326592 | bytes 2097152 | tf_op jit(solution)/shard_map/pallas_call | solution.py:335
  10.0 1.0 %collective-permute-done.3.refs_0_ = bf16[192,128]{1,0:T(8,128)(2,1)S(1)} collective-permute-done((bf16[192,128]{1,0:T(8,128)(2,1)S(1)}, bf16[192,128]{1,0:T(8,128)(2,1)S(1)}, u32[]{:S(2)}, u32[]{:S(2)}) %collective-permute-start.3) | collective-permute-done | bytes 49184 | tf_op jit(solution)/shard_map/ppermute | solution.py:24
  11.0 1.1 %shard_map.76 = bf16[192,128]{1,0:T(8,128)(2,1)S(1)} custom-call(f32[2,1024]{1,0:T(2,128)S(1)} %get-tuple-element.26.valid_ref, bf16[192,128]{1,0:T(8,128)(2,1)S(1)} %collective-permute-done.3.refs_0_, bf16[2064,256]{1,0:T(8,128)(2,1)S(1)} %get-tuple-element.21.refs_1_, bf16[2064,256]{1,0:T(8,128)(2,1)S(1)} %collective-permute-done.1.refs_2_), custom_call_target="tpu_custom_call" | custom-call | flops 201326592 | bytes 2097152 | tf_op jit(solution)/shard_map/pallas_call | solution.py:335
  12.1 0.8 %collective-permute-start.6 = (bf16[192,128]{1,0:T(8,128)(2,1)S(1)}, bf16[192,128]{1,0:T(8,128)(2,1)S(1)}, u32[]{:S(2)}, u32[]{:S(2)}) collective-permute-start(bf16[192,128]{1,0:T(8,128)(2,1)S(1)} %shard_map.76), channel_id=1, source_target_pairs={{24,0},{16,8},{8,16},{0,24},{25,1},{17,9},{9,17},{1,25},{26,2},{18... | collective-permute-start | bytes 147464 | tf_op jit(solution)/shard_map/ppermute | solution.py:29
  13.0 1.2 %collective-permute-start.4 = (bf16[192,128]{1,0:T(8,128)(2,1)S(1)}, bf16[192,128]{1,0:T(8,128)(2,1)S(1)}, u32[]{:S(2)}, u32[]{:S(2)}) collective-permute-start(bf16[192,128]{1,0:T(8,128)(2,1)S(1)} %shard_map.75), channel_id=1, source_target_pairs={{8,0},{0,8},{24,16},{16,24},{9,1},{1,9},{25,17},{17,25},{10,2},{2,... | collective-permute-start | bytes 147464 | tf_op jit(solution)/shard_map/ppermute | solution.py:29
  14.2 1.5 %collective-permute-start.5 = (bf16[192,128]{1,0:T(8,128)(2,1)S(1)}, bf16[192,128]{1,0:T(8,128)(2,1)S(1)}, u32[]{:S(2)}, u32[]{:S(2)}) collective-permute-start(bf16[192,128]{1,0:T(8,128)(2,1)S(1)} %shard_map.74), channel_id=1, source_target_pairs={{16,0},{24,8},{0,16},{8,24},{17,1},{25,9},{1,17},{9,25},{18,2},{26... | collective-permute-start | bytes 147464 | tf_op jit(solution)/shard_map/ppermute | solution.py:29
  15.7 1.1 %shard_map.77.after_ref.refs_0_ = bf16[192,128]{1,0:T(8,128)(2,1)S(1)} custom-call(f32[2,1024]{1,0:T(2,128)S(1)} %get-tuple-element.26.valid_ref, bf16[192,128]{1,0:T(8,128)(2,1)S(1)} %get-tuple-element.27.refs_0_, bf16[2064,256]{1,0:T(8,128)(2,1)S(1)} %get-tuple-element.21.refs_1_, bf16[2064,256]{1,0:T(8,128)(2,1)S(1)} %collective-permute-done.1.refs_2_), custom_call_target="tpu_custom_call" | custom-call | flops 201326592 | bytes 2097152 | tf_op jit(solution)/shard_map/pallas_call | solution.py:335
  16.9 0.3 collective-permute-done.6.refs_3_
  17.2 1.1 %collective-permute-done.5.refs_2_ = bf16[192,128]{1,0:T(8,128)(2,1)S(1)} collective-permute-done((bf16[192,128]{1,0:T(8,128)(2,1)S(1)}, bf16[192,128]{1,0:T(8,128)(2,1)S(1)}, u32[]{:S(2)}, u32[]{:S(2)}) %collective-permute-start.5) | collective-permute-done | bytes 49184 | tf_op jit(solution)/shard_map/ppermute | solution.py:29
  18.5 2.7 %collective-permute-start.9 = (bf16[16,4096]{1,0:T(8,128)(2,1)S(1)}, bf16[16,4096]{1,0:T(8,128)(2,1)S(1)}, u32[]{:S(2)}, u32[]{:S(2)}) collective-permute-start(bf16[16,4096]{1,0:T(8,128)(2,1)S(1)} %shard_map.79.refs_0_), channel_id=1, source_target_pairs={{2,0},{3,1},{0,2},{1,3},{6,4},{7,5},{4,6},{5,7},{10,8},{11,9},{8,1... | collective-permute-start | bytes 393224 | tf_op jit(solution)/shard_map/ppermute | solution.py:29
  21.1 1.6 %collective-permute-start.8 = (bf16[16,4096]{1,0:T(8,128)(2,1)S(1)}, bf16[16,4096]{1,0:T(8,128)(2,1)S(1)}, u32[]{:S(2)}, u32[]{:S(2)}) collective-permute-start(bf16[16,4096]{1,0:T(8,128)(2,1)S(1)} %shard_map.79.refs_0_), channel_id=1, source_target_pairs={{1,0},{0,1},{3,2},{2,3},{5,4},{4,5},{7,6},{6,7},{9,8},{8,9},{11,10... | collective-permute-start | bytes 393224 | tf_op jit(solution)/shard_map/ppermute | solution.py:29
  22.7 0.2 collective-permute-start.7
  22.9 4.8 %collective-permute-done.9.refs_1_ = bf16[16,4096]{1,0:T(8,128)(2,1)S(1)} collective-permute-done((bf16[16,4096]{1,0:T(8,128)(2,1)S(1)}, bf16[16,4096]{1,0:T(8,128)(2,1)S(1)}, u32[]{:S(2)}, u32[]{:S(2)}) %collective-permute-start.9) | collective-permute-done | bytes 131104 | tf_op jit(solution)/shard_map/ppermute | solution.py:29
  27.8 0.7 %shard_map.80.refs_1_ = bf16[16,16384]{1,0:T(8,128)(2,1)} custom-call(bf16[16,4096]{1,0:T(8,128)(2,1)S(1)} %shard_map.79.refs_0_, bf16[16,4096]{1,0:T(8,128)(2,1)S(1)} %collective-permute-done.9.refs_1_), custom_call_target="tpu_custom_call" | custom-call | tf_op jit(solution)/shard_map/pallas_call | solution.py:371
  28.5 0.7 %shard_map.81.refs_1_ = bf16[16,16384]{1,0:T(8,128)(2,1)} custom-call(bf16[16,4096]{1,0:T(8,128)(2,1)S(1)} %collective-permute-done.8.refs_0_, bf16[16,16384]{1,0:T(8,128)(2,1)} %shard_map.80.refs_1_), custom_call_target="tpu_custom_call", output_to_operand_aliasing={{}: (1, {})} | custom-call | tf_op jit(solution)/shard_map/pallas_call | solution.py:371
  29.2 0.4 %collective-permute-done.7.refs_0_ = bf16[16,4096]{1,0:T(8,128)(2,1)S(1)} collective-permute-done((bf16[16,4096]{1,0:T(8,128)(2,1)S(1)}, bf16[16,4096]{1,0:T(8,128)(2,1)S(1)}, u32[]{:S(2)}, u32[]{:S(2)}) %collective-permute-start.7) | collective-permute-done | bytes 131104 | tf_op jit(solution)/shard_map/ppermute | solution.py:29
  29.6 0.7 %shard_map.82 = bf16[16,16384]{1,0:T(8,128)(2,1)} custom-call(bf16[16,4096]{1,0:T(8,128)(2,1)S(1)} %collective-permute-done.7.refs_0_, bf16[16,16384]{1,0:T(8,128)(2,1)} %shard_map.81.refs_1_), custom_call_target="tpu_custom_call", output_to_operand_aliasing={{}: (1, {})} | custom-call | tf_op jit(solution)/shard_map/pallas_call | solution.py:371
  (6 shorter events, 0.4 us)
Async XLA Ops:
  1.4 5.4 %collective-permute-start.1 = (bf16[2064,256]{1,0:T(8,128)(2,1)S(1)}, bf16[2064,256]{1,0:T(8,128)(2,1)S(1)}, u32[]{:S(2)}, u32[]{:S(2)}) collective-permute-start(bf16[2064,256]{1,0:T(8,128)(2,1)S(1)} %get-tuple-element.21.refs_1_), channel_id=1, source_target_pairs={{0,4},{4,0},{1,5},{5,1},{2,6},{6,2},{3,7},{7,3},{8,12},{12,8},{9,1... | collective-permute-start | bytes 3170312 | tf_op jit(solution)/shard_map/ppermute | solution.py:328
  2.0 4.9 %collective-permute-start = (bf16[192,128]{1,0:T(8,128)(2,1)S(1)}, bf16[192,128]{1,0:T(8,128)(2,1)S(1)}, u32[]{:S(2)}, u32[]{:S(2)}) collective-permute-start(bf16[192,128]{1,0:T(8,128)(2,1)S(1)} %get-tuple-element.20), channel_id=1, source_target_pairs={{0,16},{8,24},{16,0},{24,8},{1,17},{9,25},{17,1},{25,9},{2,18},{10... | collective-permute-start | bytes 147464 | tf_op jit(solution)/shard_map/ppermute | solution.py:24
  4.5 4.4 %collective-permute-start.2 = (bf16[192,128]{1,0:T(8,128)(2,1)S(1)}, bf16[192,128]{1,0:T(8,128)(2,1)S(1)}, u32[]{:S(2)}, u32[]{:S(2)}) collective-permute-start(bf16[192,128]{1,0:T(8,128)(2,1)S(1)} %get-tuple-element.23), channel_id=1, source_target_pairs={{0,8},{8,0},{16,24},{24,16},{1,9},{9,1},{17,25},{25,17},{2,10},{10... | collective-permute-start | bytes 147464 | tf_op jit(solution)/shard_map/ppermute | solution.py:24
  6.0 5.0 %collective-permute-start.3 = (bf16[192,128]{1,0:T(8,128)(2,1)S(1)}, bf16[192,128]{1,0:T(8,128)(2,1)S(1)}, u32[]{:S(2)}, u32[]{:S(2)}) collective-permute-start(bf16[192,128]{1,0:T(8,128)(2,1)S(1)} %get-tuple-element.25), channel_id=1, source_target_pairs={{0,24},{8,16},{16,8},{24,0},{1,25},{9,17},{17,9},{25,1},{2,26},{10... | collective-permute-start | bytes 147464 | tf_op jit(solution)/shard_map/ppermute | solution.py:24
  12.1 5.1 %collective-permute-start.6 = (bf16[192,128]{1,0:T(8,128)(2,1)S(1)}, bf16[192,128]{1,0:T(8,128)(2,1)S(1)}, u32[]{:S(2)}, u32[]{:S(2)}) collective-permute-start(bf16[192,128]{1,0:T(8,128)(2,1)S(1)} %shard_map.76), channel_id=1, source_target_pairs={{24,0},{16,8},{8,16},{0,24},{25,1},{17,9},{9,17},{1,25},{26,2},{18... | collective-permute-start | bytes 147464 | tf_op jit(solution)/shard_map/ppermute | solution.py:29
  13.0 4.2 %collective-permute-start.4 = (bf16[192,128]{1,0:T(8,128)(2,1)S(1)}, bf16[192,128]{1,0:T(8,128)(2,1)S(1)}, u32[]{:S(2)}, u32[]{:S(2)}) collective-permute-start(bf16[192,128]{1,0:T(8,128)(2,1)S(1)} %shard_map.75), channel_id=1, source_target_pairs={{8,0},{0,8},{24,16},{16,24},{9,1},{1,9},{25,17},{17,25},{10,2},{2,... | collective-permute-start | bytes 147464 | tf_op jit(solution)/shard_map/ppermute | solution.py:29
  14.2 4.1 %collective-permute-start.5 = (bf16[192,128]{1,0:T(8,128)(2,1)S(1)}, bf16[192,128]{1,0:T(8,128)(2,1)S(1)}, u32[]{:S(2)}, u32[]{:S(2)}) collective-permute-start(bf16[192,128]{1,0:T(8,128)(2,1)S(1)} %shard_map.74), channel_id=1, source_target_pairs={{16,0},{24,8},{0,16},{8,24},{17,1},{25,9},{1,17},{9,25},{18,2},{26... | collective-permute-start | bytes 147464 | tf_op jit(solution)/shard_map/ppermute | solution.py:29
  18.5 9.3 %collective-permute-start.9 = (bf16[16,4096]{1,0:T(8,128)(2,1)S(1)}, bf16[16,4096]{1,0:T(8,128)(2,1)S(1)}, u32[]{:S(2)}, u32[]{:S(2)}) collective-permute-start(bf16[16,4096]{1,0:T(8,128)(2,1)S(1)} %shard_map.79.refs_0_), channel_id=1, source_target_pairs={{2,0},{3,1},{0,2},{1,3},{6,4},{7,5},{4,6},{5,7},{10,8},{11,9},{8,1... | collective-permute-start | bytes 393224 | tf_op jit(solution)/shard_map/ppermute | solution.py:29
  21.1 7.4 %collective-permute-start.8 = (bf16[16,4096]{1,0:T(8,128)(2,1)S(1)}, bf16[16,4096]{1,0:T(8,128)(2,1)S(1)}, u32[]{:S(2)}, u32[]{:S(2)}) collective-permute-start(bf16[16,4096]{1,0:T(8,128)(2,1)S(1)} %shard_map.79.refs_0_), channel_id=1, source_target_pairs={{1,0},{0,1},{3,2},{2,3},{5,4},{4,5},{7,6},{6,7},{9,8},{8,9},{11,10... | collective-permute-start | bytes 393224 | tf_op jit(solution)/shard_map/ppermute | solution.py:29
  22.7 6.9 %collective-permute-start.7 = (bf16[16,4096]{1,0:T(8,128)(2,1)S(1)}, bf16[16,4096]{1,0:T(8,128)(2,1)S(1)}, u32[]{:S(2)}, u32[]{:S(2)}) collective-permute-start(bf16[16,4096]{1,0:T(8,128)(2,1)S(1)} %shard_map.79.refs_0_), channel_id=1, source_target_pairs={{3,0},{2,1},{1,2},{0,3},{7,4},{6,5},{5,6},{4,7},{11,8},{10,9},{9,1... | collective-permute-start | bytes 393224 | tf_op jit(solution)/shard_map/ppermute | solution.py:29

commit v9 on v8

--- a/solution.py
+++ b/solution.py
@@ -90,13 +90,13 @@
     )
     shard_len, span = key_hbm.shape
     pairs = (
+        (query_hbm, query_ref),
         (doc_hbm, doc_ref),
-        (query_hbm, query_ref),
-        (length_hbm, length_ref),
+        (key_hbm, cache_ref.at[pl.ds(0, shard_len)]),
+        (value_hbm, cache_ref.at[pl.ds(shard_len, shard_len)]),
         (key_scale_hbm, key_scale_ref),
         (value_scale_hbm, value_scale_ref),
-        (key_hbm, cache_ref.at[pl.ds(0, shard_len)]),
-        (value_hbm, cache_ref.at[pl.ds(shard_len, shard_len)]),
+        (length_hbm, length_ref),
     )
     copies = [
         pltpu.make_async_copy(source, target, sems.at[at])
@@ -110,10 +110,10 @@
     block = group * cap
     signs = sign_matrix()
     scale = 1.0 / math.sqrt(HEAD_WIDTH)
-    copies[0].wait()
+    copies[1].wait()
     placing = placing_matrix(doc_ref[...], n_doc, cap)
     placing_ref[...] = placing
-    copies[1].wait()
+    copies[0].wait()
     rotated = []
     for g in range(heads // group):
         stacked = jnp.concatenate(
@@ -131,7 +131,7 @@
         )
         for k in range(n_doc):
             out_refs[k][g * block : (g + 1) * block, :] = placed[k * block : (k + 1) * block]
-    for copy in copies[2:5]:
+    for copy in copies[4:]:
         copy.wait()
     scale_rows = []
     for scale_ref in (key_scale_ref, value_scale_ref):
@@ -151,7 +151,7 @@
     anchor = (lax.axis_index("ctx") - step + n_ctx) % n_ctx
     position = lax.broadcasted_iota(jnp.int32, valid_ref.shape, 1) + anchor * shard_len
     valid_ref[...] = jnp.where(position < length, 1.0, 0.0)
-    for copy in copies[5:]:
+    for copy in copies[2:4]:
         copy.wait()
 
 

time: 30.4 us -> 30.4 us (level)
  no operation moved by 1% of the time
where the time goes in v9:
time: 30.4 us; the launch traced here: 30.2 us
  starting transfers between devices  12.7 us (42%)
  waiting for transfers between devices  9.34 us (31%)
  Pallas kernels  8.14 us (27%)
    ppermute x6, starting transfers between devices, returned(): lax.ppermute(value, axis, [(peer_of(i, step, count), i) for i in range(co...  8.01 us
    ppermute x6, waiting for transfers between devices, returned(): lax.ppermute(value, axis, [(peer_of(i, step, count), i) for i in range(co...  6.6 us
    pallas_call x4, Pallas kernels, attended_for(): pl.pallas_call(functools.partial(attend_kernel, len(sources), n_ctx, kv_d...  4.37 us
    ppermute x3, starting transfers between devices, sent(): lax.ppermute(value, axis, [(i, peer_of(i, step, count)) for i in range(co...  4.13 us
    ppermute x3, waiting for transfers between devices, sent(): lax.ppermute(value, axis, [(i, peer_of(i, step, count)) for i in range(co...  2.73 us
    pallas_call x3, Pallas kernels, assembled(): pl.pallas_call(functools.partial(assemble_kernel, n_head, steps), out_sha...  2.05 us
    pallas_call x1, Pallas kernels, shards(): pl.pallas_call(functools.partial(dispatch_kernel, n_doc, n_ctx, cap), out...  1.41 us
  transfers between devices with their start and end apart: 10, of which 7 were waited for; matrix products, arithmetic and copies ran while one was open for 0% of the time, Pallas kernels for 16%

profile of v9, /device:TPU:0, one launch (start us, length us, event | category | flops | bytes accessed | tf_op | source)
XLA Modules:
  0.0 30.2 jit_solution(3465927671444429222)
XLA Ops:
  0.0 1.4 %shard_map.73 = (bf16[192,128]{1,0:T(8,128)(2,1)S(1)}, f32[2,1024]{1,0:T(2,128)S(1)}, bf16[2064,256]{1,0:T(8,128)(2,1)S(1)}, bf16[192,128]{1,0:T(8,128)(2,1)S(1)...) custom-call(s32[1,16]{1,0:T(1,128)} %bitcast.10, s32[1,4]{1,0:T(1,128)} %bitcast.11, ...), custom_call_target="tpu_custom_call" | custom-call | tf_op jit(solution)/shard_map/pallas_call | solution.py:309
  1.4 0.5 %collective-permute-start.1 = (bf16[2064,256]{1,0:T(8,128)(2,1)S(1)}, bf16[2064,256]{1,0:T(8,128)(2,1)S(1)}, u32[]{:S(2)}, u32[]{:S(2)}) collective-permute-start(bf16[2064,256]{1,0:T(8,128)(2,1)S(1)} %get-tuple-element.21.refs_1_), channel_id=1, source_target_pairs={{0,4},{4,0},{1,5},{5,1},{2,6},{6,2},{3,7},{7,3},{8,12},{12,8},{9,1... | collective-permute-start | bytes 3170312 | tf_op jit(solution)/shard_map/ppermute | solution.py:328
  1.9 2.6 %collective-permute-start = (bf16[192,128]{1,0:T(8,128)(2,1)S(1)}, bf16[192,128]{1,0:T(8,128)(2,1)S(1)}, u32[]{:S(2)}, u32[]{:S(2)}) collective-permute-start(bf16[192,128]{1,0:T(8,128)(2,1)S(1)} %get-tuple-element.20), channel_id=1, source_target_pairs={{0,16},{8,24},{16,0},{24,8},{1,17},{9,25},{17,1},{25,9},{2,18},{10... | collective-permute-start | bytes 147464 | tf_op jit(solution)/shard_map/ppermute | solution.py:24
  4.5 1.5 %collective-permute-start.2 = (bf16[192,128]{1,0:T(8,128)(2,1)S(1)}, bf16[192,128]{1,0:T(8,128)(2,1)S(1)}, u32[]{:S(2)}, u32[]{:S(2)}) collective-permute-start(bf16[192,128]{1,0:T(8,128)(2,1)S(1)} %get-tuple-element.23), channel_id=1, source_target_pairs={{0,8},{8,0},{16,24},{24,16},{1,9},{9,1},{17,25},{25,17},{2,10},{10... | collective-permute-start | bytes 147464 | tf_op jit(solution)/shard_map/ppermute | solution.py:24
  6.1 0.8 %collective-permute-done.refs_0_ = bf16[192,128]{1,0:T(8,128)(2,1)S(1)} collective-permute-done((bf16[192,128]{1,0:T(8,128)(2,1)S(1)}, bf16[192,128]{1,0:T(8,128)(2,1)S(1)}, u32[]{:S(2)}, u32[]{:S(2)}) %collective-permute-start) | collective-permute-done | bytes 49184 | tf_op jit(solution)/shard_map/ppermute | solution.py:24
  6.9 1.1 %shard_map.74 = bf16[192,128]{1,0:T(8,128)(2,1)S(1)} custom-call(f32[2,1024]{1,0:T(2,128)S(1)} %get-tuple-element.26.valid_ref, bf16[192,128]{1,0:T(8,128)(2,1)S(1)} %collective-permute-done.refs_0_, bf16[2064,256]{1,0:T(8,128)(2,1)S(1)} %get-tuple-element.21.refs_1_, bf16[2064,256]{1,0:T(8,128)(2,1)S(1)} %collective-permute-done.1.refs_2_), custom_call_target="tpu_custom_call" | custom-call | flops 201326592 | bytes 2097152 | tf_op jit(solution)/shard_map/pallas_call | solution.py:335
  8.0 0.9 %collective-permute-done.2.refs_0_ = bf16[192,128]{1,0:T(8,128)(2,1)S(1)} collective-permute-done((bf16[192,128]{1,0:T(8,128)(2,1)S(1)}, bf16[192,128]{1,0:T(8,128)(2,1)S(1)}, u32[]{:S(2)}, u32[]{:S(2)}) %collective-permute-start.2) | collective-permute-done | bytes 49184 | tf_op jit(solution)/shard_map/ppermute | solution.py:24
  8.9 1.1 %shard_map.75 = bf16[192,128]{1,0:T(8,128)(2,1)S(1)} custom-call(f32[2,1024]{1,0:T(2,128)S(1)} %get-tuple-element.26.valid_ref, bf16[192,128]{1,0:T(8,128)(2,1)S(1)} %collective-permute-done.2.refs_0_, bf16[2064,256]{1,0:T(8,128)(2,1)S(1)} %get-tuple-element.21.refs_1_, bf16[2064,256]{1,0:T(8,128)(2,1)S(1)} %collective-permute-done.1.refs_2_), custom_call_target="tpu_custom_call" | custom-call | flops 201326592 | bytes 2097152 | tf_op jit(solution)/shard_map/pallas_call | solution.py:335
  10.0 1.0 %collective-permute-done.3.refs_0_ = bf16[192,128]{1,0:T(8,128)(2,1)S(1)} collective-permute-done((bf16[192,128]{1,0:T(8,128)(2,1)S(1)}, bf16[192,128]{1,0:T(8,128)(2,1)S(1)}, u32[]{:S(2)}, u32[]{:S(2)}) %collective-permute-start.3) | collective-permute-done | bytes 49184 | tf_op jit(solution)/shard_map/ppermute | solution.py:24
  11.0 1.1 %shard_map.76 = bf16[192,128]{1,0:T(8,128)(2,1)S(1)} custom-call(f32[2,1024]{1,0:T(2,128)S(1)} %get-tuple-element.26.valid_ref, bf16[192,128]{1,0:T(8,128)(2,1)S(1)} %collective-permute-done.3.refs_0_, bf16[2064,256]{1,0:T(8,128)(2,1)S(1)} %get-tuple-element.21.refs_1_, bf16[2064,256]{1,0:T(8,128)(2,1)S(1)} %collective-permute-done.1.refs_2_), custom_call_target="tpu_custom_call" | custom-call | flops 201326592 | bytes 2097152 | tf_op jit(solution)/shard_map/pallas_call | solution.py:335
  12.1 0.8 %collective-permute-start.6 = (bf16[192,128]{1,0:T(8,128)(2,1)S(1)}, bf16[192,128]{1,0:T(8,128)(2,1)S(1)}, u32[]{:S(2)}, u32[]{:S(2)}) collective-permute-start(bf16[192,128]{1,0:T(8,128)(2,1)S(1)} %shard_map.76), channel_id=1, source_target_pairs={{24,0},{16,8},{8,16},{0,24},{25,1},{17,9},{9,17},{1,25},{26,2},{18... | collective-permute-start | bytes 147464 | tf_op jit(solution)/shard_map/ppermute | solution.py:29
  13.0 1.2 %collective-permute-start.4 = (bf16[192,128]{1,0:T(8,128)(2,1)S(1)}, bf16[192,128]{1,0:T(8,128)(2,1)S(1)}, u32[]{:S(2)}, u32[]{:S(2)}) collective-permute-start(bf16[192,128]{1,0:T(8,128)(2,1)S(1)} %shard_map.75), channel_id=1, source_target_pairs={{8,0},{0,8},{24,16},{16,24},{9,1},{1,9},{25,17},{17,25},{10,2},{2,... | collective-permute-start | bytes 147464 | tf_op jit(solution)/shard_map/ppermute | solution.py:29
  14.1 1.5 %collective-permute-start.5 = (bf16[192,128]{1,0:T(8,128)(2,1)S(1)}, bf16[192,128]{1,0:T(8,128)(2,1)S(1)}, u32[]{:S(2)}, u32[]{:S(2)}) collective-permute-start(bf16[192,128]{1,0:T(8,128)(2,1)S(1)} %shard_map.74), channel_id=1, source_target_pairs={{16,0},{24,8},{0,16},{8,24},{17,1},{25,9},{1,17},{9,25},{18,2},{26... | collective-permute-start | bytes 147464 | tf_op jit(solution)/shard_map/ppermute | solution.py:29
  15.7 1.1 %shard_map.77.after_ref.refs_0_ = bf16[192,128]{1,0:T(8,128)(2,1)S(1)} custom-call(f32[2,1024]{1,0:T(2,128)S(1)} %get-tuple-element.26.valid_ref, bf16[192,128]{1,0:T(8,128)(2,1)S(1)} %get-tuple-element.27.refs_0_, bf16[2064,256]{1,0:T(8,128)(2,1)S(1)} %get-tuple-element.21.refs_1_, bf16[2064,256]{1,0:T(8,128)(2,1)S(1)} %collective-permute-done.1.refs_2_), custom_call_target="tpu_custom_call" | custom-call | flops 201326592 | bytes 2097152 | tf_op jit(solution)/shard_map/pallas_call | solution.py:335
  16.9 0.3 collective-permute-done.6.refs_3_
  17.2 1.1 %collective-permute-done.5.refs_2_ = bf16[192,128]{1,0:T(8,128)(2,1)S(1)} collective-permute-done((bf16[192,128]{1,0:T(8,128)(2,1)S(1)}, bf16[192,128]{1,0:T(8,128)(2,1)S(1)}, u32[]{:S(2)}, u32[]{:S(2)}) %collective-permute-start.5) | collective-permute-done | bytes 49184 | tf_op jit(solution)/shard_map/ppermute | solution.py:29
  18.5 2.7 %collective-permute-start.9 = (bf16[16,4096]{1,0:T(8,128)(2,1)S(1)}, bf16[16,4096]{1,0:T(8,128)(2,1)S(1)}, u32[]{:S(2)}, u32[]{:S(2)}) collective-permute-start(bf16[16,4096]{1,0:T(8,128)(2,1)S(1)} %shard_map.79.refs_0_), channel_id=1, source_target_pairs={{2,0},{3,1},{0,2},{1,3},{6,4},{7,5},{4,6},{5,7},{10,8},{11,9},{8,1... | collective-permute-start | bytes 393224 | tf_op jit(solution)/shard_map/ppermute | solution.py:29
  21.1 1.6 %collective-permute-start.8 = (bf16[16,4096]{1,0:T(8,128)(2,1)S(1)}, bf16[16,4096]{1,0:T(8,128)(2,1)S(1)}, u32[]{:S(2)}, u32[]{:S(2)}) collective-permute-start(bf16[16,4096]{1,0:T(8,128)(2,1)S(1)} %shard_map.79.refs_0_), channel_id=1, source_target_pairs={{1,0},{0,1},{3,2},{2,3},{5,4},{4,5},{7,6},{6,7},{9,8},{8,9},{11,10... | collective-permute-start | bytes 393224 | tf_op jit(solution)/shard_map/ppermute | solution.py:29
  22.7 0.2 collective-permute-start.7
  22.9 4.8 %collective-permute-done.9.refs_1_ = bf16[16,4096]{1,0:T(8,128)(2,1)S(1)} collective-permute-done((bf16[16,4096]{1,0:T(8,128)(2,1)S(1)}, bf16[16,4096]{1,0:T(8,128)(2,1)S(1)}, u32[]{:S(2)}, u32[]{:S(2)}) %collective-permute-start.9) | collective-permute-done | bytes 131104 | tf_op jit(solution)/shard_map/ppermute | solution.py:29
  27.7 0.7 %shard_map.80.refs_1_ = bf16[16,16384]{1,0:T(8,128)(2,1)} custom-call(bf16[16,4096]{1,0:T(8,128)(2,1)S(1)} %shard_map.79.refs_0_, bf16[16,4096]{1,0:T(8,128)(2,1)S(1)} %collective-permute-done.9.refs_1_), custom_call_target="tpu_custom_call" | custom-call | tf_op jit(solution)/shard_map/pallas_call | solution.py:371
  28.5 0.7 %shard_map.81.refs_1_ = bf16[16,16384]{1,0:T(8,128)(2,1)} custom-call(bf16[16,4096]{1,0:T(8,128)(2,1)S(1)} %collective-permute-done.8.refs_0_, bf16[16,16384]{1,0:T(8,128)(2,1)} %shard_map.80.refs_1_), custom_call_target="tpu_custom_call", output_to_operand_aliasing={{}: (1, {})} | custom-call | tf_op jit(solution)/shard_map/pallas_call | solution.py:371
  29.2 0.4 %collective-permute-done.7.refs_0_ = bf16[16,4096]{1,0:T(8,128)(2,1)S(1)} collective-permute-done((bf16[16,4096]{1,0:T(8,128)(2,1)S(1)}, bf16[16,4096]{1,0:T(8,128)(2,1)S(1)}, u32[]{:S(2)}, u32[]{:S(2)}) %collective-permute-start.7) | collective-permute-done | bytes 131104 | tf_op jit(solution)/shard_map/ppermute | solution.py:29
  29.6 0.7 %shard_map.82 = bf16[16,16384]{1,0:T(8,128)(2,1)} custom-call(bf16[16,4096]{1,0:T(8,128)(2,1)S(1)} %collective-permute-done.7.refs_0_, bf16[16,16384]{1,0:T(8,128)(2,1)} %shard_map.81.refs_1_), custom_call_target="tpu_custom_call", output_to_operand_aliasing={{}: (1, {})} | custom-call | tf_op jit(solution)/shard_map/pallas_call | solution.py:371
  (6 shorter events, 0.4 us)
Async XLA Ops:
  1.4 5.4 %collective-permute-start.1 = (bf16[2064,256]{1,0:T(8,128)(2,1)S(1)}, bf16[2064,256]{1,0:T(8,128)(2,1)S(1)}, u32[]{:S(2)}, u32[]{:S(2)}) collective-permute-start(bf16[2064,256]{1,0:T(8,128)(2,1)S(1)} %get-tuple-element.21.refs_1_), channel_id=1, source_target_pairs={{0,4},{4,0},{1,5},{5,1},{2,6},{6,2},{3,7},{7,3},{8,12},{12,8},{9,1... | collective-permute-start | bytes 3170312 | tf_op jit(solution)/shard_map/ppermute | solution.py:328
  1.9 4.9 %collective-permute-start = (bf16[192,128]{1,0:T(8,128)(2,1)S(1)}, bf16[192,128]{1,0:T(8,128)(2,1)S(1)}, u32[]{:S(2)}, u32[]{:S(2)}) collective-permute-start(bf16[192,128]{1,0:T(8,128)(2,1)S(1)} %get-tuple-element.20), channel_id=1, source_target_pairs={{0,16},{8,24},{16,0},{24,8},{1,17},{9,25},{17,1},{25,9},{2,18},{10... | collective-permute-start | bytes 147464 | tf_op jit(solution)/shard_map/ppermute | solution.py:24
  4.5 4.4 %collective-permute-start.2 = (bf16[192,128]{1,0:T(8,128)(2,1)S(1)}, bf16[192,128]{1,0:T(8,128)(2,1)S(1)}, u32[]{:S(2)}, u32[]{:S(2)}) collective-permute-start(bf16[192,128]{1,0:T(8,128)(2,1)S(1)} %get-tuple-element.23), channel_id=1, source_target_pairs={{0,8},{8,0},{16,24},{24,16},{1,9},{9,1},{17,25},{25,17},{2,10},{10... | collective-permute-start | bytes 147464 | tf_op jit(solution)/shard_map/ppermute | solution.py:24
  6.0 5.0 %collective-permute-start.3 = (bf16[192,128]{1,0:T(8,128)(2,1)S(1)}, bf16[192,128]{1,0:T(8,128)(2,1)S(1)}, u32[]{:S(2)}, u32[]{:S(2)}) collective-permute-start(bf16[192,128]{1,0:T(8,128)(2,1)S(1)} %get-tuple-element.25), channel_id=1, source_target_pairs={{0,24},{8,16},{16,8},{24,0},{1,25},{9,17},{17,9},{25,1},{2,26},{10... | collective-permute-start | bytes 147464 | tf_op jit(solution)/shard_map/ppermute | solution.py:24
  12.1 5.1 %collective-permute-start.6 = (bf16[192,128]{1,0:T(8,128)(2,1)S(1)}, bf16[192,128]{1,0:T(8,128)(2,1)S(1)}, u32[]{:S(2)}, u32[]{:S(2)}) collective-permute-start(bf16[192,128]{1,0:T(8,128)(2,1)S(1)} %shard_map.76), channel_id=1, source_target_pairs={{24,0},{16,8},{8,16},{0,24},{25,1},{17,9},{9,17},{1,25},{26,2},{18... | collective-permute-start | bytes 147464 | tf_op jit(solution)/shard_map/ppermute | solution.py:29
  13.0 4.2 %collective-permute-start.4 = (bf16[192,128]{1,0:T(8,128)(2,1)S(1)}, bf16[192,128]{1,0:T(8,128)(2,1)S(1)}, u32[]{:S(2)}, u32[]{:S(2)}) collective-permute-start(bf16[192,128]{1,0:T(8,128)(2,1)S(1)} %shard_map.75), channel_id=1, source_target_pairs={{8,0},{0,8},{24,16},{16,24},{9,1},{1,9},{25,17},{17,25},{10,2},{2,... | collective-permute-start | bytes 147464 | tf_op jit(solution)/shard_map/ppermute | solution.py:29
  14.1 4.1 %collective-permute-start.5 = (bf16[192,128]{1,0:T(8,128)(2,1)S(1)}, bf16[192,128]{1,0:T(8,128)(2,1)S(1)}, u32[]{:S(2)}, u32[]{:S(2)}) collective-permute-start(bf16[192,128]{1,0:T(8,128)(2,1)S(1)} %shard_map.74), channel_id=1, source_target_pairs={{16,0},{24,8},{0,16},{8,24},{17,1},{25,9},{1,17},{9,25},{18,2},{26... | collective-permute-start | bytes 147464 | tf_op jit(solution)/shard_map/ppermute | solution.py:29
  18.5 9.3 %collective-permute-start.9 = (bf16[16,4096]{1,0:T(8,128)(2,1)S(1)}, bf16[16,4096]{1,0:T(8,128)(2,1)S(1)}, u32[]{:S(2)}, u32[]{:S(2)}) collective-permute-start(bf16[16,4096]{1,0:T(8,128)(2,1)S(1)} %shard_map.79.refs_0_), channel_id=1, source_target_pairs={{2,0},{3,1},{0,2},{1,3},{6,4},{7,5},{4,6},{5,7},{10,8},{11,9},{8,1... | collective-permute-start | bytes 393224 | tf_op jit(solution)/shard_map/ppermute | solution.py:29
  21.1 7.4 %collective-permute-start.8 = (bf16[16,4096]{1,0:T(8,128)(2,1)S(1)}, bf16[16,4096]{1,0:T(8,128)(2,1)S(1)}, u32[]{:S(2)}, u32[]{:S(2)}) collective-permute-start(bf16[16,4096]{1,0:T(8,128)(2,1)S(1)} %shard_map.79.refs_0_), channel_id=1, source_target_pairs={{1,0},{0,1},{3,2},{2,3},{5,4},{4,5},{7,6},{6,7},{9,8},{8,9},{11,10... | collective-permute-start | bytes 393224 | tf_op jit(solution)/shard_map/ppermute | solution.py:29
  22.7 6.9 %collective-permute-start.7 = (bf16[16,4096]{1,0:T(8,128)(2,1)S(1)}, bf16[16,4096]{1,0:T(8,128)(2,1)S(1)}, u32[]{:S(2)}, u32[]{:S(2)}) collective-permute-start(bf16[16,4096]{1,0:T(8,128)(2,1)S(1)} %shard_map.79.refs_0_), channel_id=1, source_target_pairs={{3,0},{2,1},{1,2},{0,3},{7,4},{6,5},{5,6},{4,7},{11,8},{10,9},{9,1... | collective-permute-start | bytes 393224 | tf_op jit(solution)/shard_map/ppermute | solution.py:29
